TPU v7x, 32 devices: a whole 2x2x4 slice. The times are simulated.
32 devices in a mesh: grp: 2 (over x), tok: 16 (over z, y, core).
Axes of the slice: x: 2, y: 2, z: 4, core: 2. Of those that a mesh axis runs over, the one named last changes fastest.
Arguments:
- keys: bfloat16 [4096, 1024], P(('grp', 'tok')), parts along dimension 0, may hold values from -6 to 6
- values: bfloat16 [4096, 1024], P(('grp', 'tok')), parts along dimension 0, may hold values from -6 to 6
- queries: bfloat16 [4096, 1024], P(('grp', 'tok')), parts along dimension 0, may hold values from -6 to 6
- rates: float32 [2, 4096], P(None, ('grp', 'tok')), parts along dimension 1, may hold values from 0.3 to 3
- fast_weights: bfloat16 [2, 3, 512, 512], replicated, may hold values from -0.25 to 0.25
Outputs:
- readout: bfloat16 [4096, 1024], P(('grp', 'tok')), parts along dimension 0
- new_weights: bfloat16 [4, 3, 512, 512], P('grp'), parts along dimension 0
There are 2 independent parts, one for each index of `grp`. A program takes and returns all parts, laid end to end along the dimension named above; an argument that names none is the same for every part. Nothing has to cross between parts.
All inputs are finite; a program needn't handle non-finite values.
Results may differ from a plain program's by a relative error of at most 0.017.
Values may be sent and summed in bfloat16 or wider, within the bound.
No kernel may reach another device: no remote copies, remote signals or barrier semaphores. Data moves between devices by JAX's collectives and lax.ppermute only.
A program may use at most 64 MiB of HBM per device.

v0:
```python
import jax
import jax.numpy as jnp
from jax import lax
from jax.sharding import PartitionSpec as P

DH = 512
HEADS = 2
NS_STEPS = 2


def swiglu_grads(key_rows, value_rows, rate_col, gate_w, up_w, down_w):
    gate = jnp.dot(key_rows, gate_w, preferred_element_type=jnp.float32)
    upper = jnp.dot(key_rows, up_w, preferred_element_type=jnp.float32)
    sigma = jax.nn.sigmoid(gate)
    silu_gate = gate * sigma
    hidden = (silu_gate * upper).astype(jnp.bfloat16)
    outer = (-rate_col[:, None] * value_rows.astype(jnp.float32)).astype(jnp.bfloat16)
    back = jnp.dot(outer, down_w.T, preferred_element_type=jnp.float32)
    d_gate = (back * upper * sigma * (1.0 + gate * (1.0 - sigma))).astype(jnp.bfloat16)
    d_upper = (back * silu_gate).astype(jnp.bfloat16)
    grad_gate = jnp.dot(key_rows.T, d_gate, preferred_element_type=jnp.float32)
    grad_upper = jnp.dot(key_rows.T, d_upper, preferred_element_type=jnp.float32)
    grad_down = jnp.dot(hidden.T, outer, preferred_element_type=jnp.float32)
    return jnp.stack([grad_gate, grad_upper, grad_down])


def newton_schulz(matrix):
    wide = matrix.astype(jnp.float32)
    iterate = (wide / (jnp.sqrt(jnp.sum(wide * wide)) + 1e-07)).astype(jnp.bfloat16)
    for step in range(NS_STEPS):
        gram = jnp.dot(iterate, iterate.T, preferred_element_type=jnp.float32).astype(jnp.bfloat16)
        square = jnp.dot(gram, gram, preferred_element_type=jnp.float32)
        mixed = (-4.775 * gram.astype(jnp.float32) + 2.0315 * square).astype(jnp.bfloat16)
        iterate = (
            3.4445 * iterate.astype(jnp.float32)
            + jnp.dot(mixed, iterate, preferred_element_type=jnp.float32)
        ).astype(jnp.bfloat16)
    return iterate


def renormed(weight, update):
    old = weight.astype(jnp.float32)
    fresh = old - update.astype(jnp.float32)
    scale = jnp.sqrt(
        (jnp.mean(old * old, axis=1, keepdims=True) + 1e-06)
        / (jnp.mean(fresh * fresh, axis=1, keepdims=True) + 1e-06)
    )
    return (fresh * scale).astype(jnp.bfloat16)


def apply_fast(query_rows, gate_w, up_w, down_w):
    gate = jnp.dot(query_rows, gate_w, preferred_element_type=jnp.float32)
    upper = jnp.dot(query_rows, up_w, preferred_element_type=jnp.float32)
    hidden = (jax.nn.silu(gate) * upper).astype(jnp.bfloat16)
    return jnp.dot(hidden, down_w, preferred_element_type=jnp.float32).astype(jnp.bfloat16)


def summed_grads(partial_value):
    total = lax.psum(partial_value, "tok")
    return total.astype(jnp.bfloat16)


def body(keys, values, queries, rates, fast_weights):
    width = fast_weights.shape[2]
    count = 3 * HEADS
    rounded_all = []
    for head in range(HEADS):
        cols = slice(head * DH, (head + 1) * DH)
        partial_value = swiglu_grads(
            keys[:, cols],
            values[:, cols],
            rates[head],
            fast_weights[head, 0],
            fast_weights[head, 1],
            fast_weights[head, 2],
        )
        rounded_all.append(summed_grads(partial_value))
    stacked = jnp.concatenate(rounded_all, axis=0)
    old_all = fast_weights.reshape(count, width, width)
    fresh_all = [
        renormed(old_all[matrix], newton_schulz(stacked[matrix])) for matrix in range(count)
    ]
    outputs = []
    for head in range(HEADS):
        cols = slice(head * DH, (head + 1) * DH)
        outputs.append(
            apply_fast(
                queries[:, cols],
                fresh_all[3 * head],
                fresh_all[3 * head + 1],
                fresh_all[3 * head + 2],
            )
        )
    new_weights = jnp.stack(fresh_all).reshape(HEADS, 3, width, width)
    return (jnp.concatenate(outputs, axis=1), new_weights)


def solution(mesh):
    return jax.shard_map(
        body,
        mesh=mesh,
        in_specs=(
            P(("grp", "tok"), None),
            P(("grp", "tok"), None),
            P(("grp", "tok"), None),
            P(None, ("grp", "tok")),
            P(),
        ),
        out_specs=(P(("grp", "tok"), None), P("grp", None, None, None)),
        check_vma=False,
    )
```

profile of v0, /device:TPU:0, one launch (start us, length us, event | category | flops | bytes accessed | tf_op | source)
XLA Modules:
  0.0 251.5 jit_solution(15024841520664925883)
XLA Ops:
  0.7 0.9 negate_bitcast_fusion.1
  1.5 1.6 fusion.100
  3.1 1.3 fusion.94
  4.5 1.4 fusion.104
  5.9 1.4 fusion.98
  7.8 0.4 convolution_bitcast_fusion
  8.2 0.4 convolution_bitcast_fusion.2
  8.9 2.0 pad_maximum_fusion.1
  10.9 0.4 convolution_bitcast_fusion.3
  11.3 0.4 convolution_bitcast_fusion.5
  12.0 2.0 pad_maximum_fusion
  14.0 140.4 %all-reduce.2 = (bf16[3,512,512]{1,2,0:T(8,128)(2,1)}, bf16[3,512,512]{1,2,0:T(8,128)(2,1)}) all-reduce(f32[3,512,512]{1,2,0:T(8,128)} %pad_maximum_fusion.1, f32[3,512,512]{1,2,0:T(8,128)} %pad_maximum_fusion), channel_id=1, replica_groups=mesh['grp'=2,'tok'=16] {'tok'}, use_global_device_ids=true, to_apply=%region_10.0 | all-reduce | flops 1572864 | bytes 9437184 | tf_op jit(solution)/shard_map/psum | solution.py:59
  154.4 3.1 %fusion.50 = (f32[]{:T(128)}, f32[]{:T(128)}, f32[]{:T(128)}, f32[]{:T(128)}, f32[]{:T(128)}, /*index=5*/f32[]{:T(128)}) fusion(bf16[3,512,512]{1,2,0:T(8,128)(2,1)} %get-tuple-element.17, bf16[3,512,512]{1,2,0:T(8,128)(2,1)} %get-tuple-element.16), kind=kLoop, calls=%fused_computation.124 | loop fusion | flops 4718586 | bytes 3145752 | tf_op jit(solution)/shard_map/reduce_sum | solution.py:29
  161.6 2.6 %convolution_convert_fusion.7 = bf16[512,512]{1,0:T(8,128)(2,1)} fusion(f32[]{:T(128)S(6)} %add.226, bf16[3,512,512]{1,2,0:T(8,128)(2,1)} %get-tuple-element.17), kind=kOutput, calls=%fused_computation.87 | convolution fusion | flops 269484032 | bytes 1048580 | tf_op jit(solution)/shard_map/dot_general | solution.py:31
  164.2 3.5 %fusion.30 = bf16[512,512]{0,1:T(8,128)(2,1)} fusion(bf16[512,512]{1,0:T(8,128)(2,1)} %convolution_convert_fusion.7, f32[]{:T(128)S(6)} %add.226, bf16[3,512,512]{1,2,0:T(8,128)(2,1)} %get-tuple-element.17), kind=kOutput, calls=%fused_computation.98 | convolution fusion | flops 540803072 | bytes 3146752 | tf_op jit(solution)/shard_map/dot_general | solution.py:36
  167.7 2.5 convolution_convert_fusion.6
  170.2 2.5 convolution_convert_fusion.9
  172.7 3.5 %fusion.27 = bf16[512,512]{0,1:T(8,128)(2,1)} fusion(bf16[512,512]{1,0:T(8,128)(2,1)} %convolution_convert_fusion.9, f32[]{:T(128)S(6)} %add.219, bf16[3,512,512]{1,2,0:T(8,128)(2,1)} %get-tuple-element.17), kind=kOutput, calls=%fused_computation.95 | convolution fusion | flops 540803072 | bytes 3146752 | tf_op jit(solution)/shard_map/dot_general | solution.py:36
  176.2 2.5 convolution_convert_fusion.8
  178.7 2.5 convolution_convert_fusion.11
  181.2 3.5 %fusion.24 = bf16[512,512]{0,1:T(8,128)(2,1)} fusion(bf16[512,512]{1,0:T(8,128)(2,1)} %convolution_convert_fusion.11, f32[]{:T(128)S(6)} %add.211, bf16[3,512,512]{1,2,0:T(8,128)(2,1)} %get-tuple-element.17), kind=kOutput, calls=%fused_computation.92 | convolution fusion | flops 540803072 | bytes 3146752 | tf_op jit(solution)/shard_map/dot_general | solution.py:36
  184.6 2.5 convolution_convert_fusion.10
  187.1 2.5 convolution_convert_fusion.5
  189.6 3.5 %fusion.33 = bf16[512,512]{0,1:T(8,128)(2,1)} fusion(bf16[512,512]{1,0:T(8,128)(2,1)} %convolution_convert_fusion.5, f32[]{:T(128)S(6)} %add.235, bf16[3,512,512]{1,2,0:T(8,128)(2,1)} %get-tuple-element.16), kind=kOutput, calls=%fused_computation.101 | convolution fusion | flops 540803072 | bytes 3146752 | tf_op jit(solution)/shard_map/dot_general | solution.py:36
  193.1 2.5 convolution_convert_fusion.4
  195.6 2.5 convolution_convert_fusion.3
  198.1 3.6 %fusion.36 = bf16[512,512]{0,1:T(8,128)(2,1)} fusion(bf16[512,512]{1,0:T(8,128)(2,1)} %convolution_convert_fusion.3, f32[]{:T(128)S(6)} %add.243, bf16[3,512,512]{1,2,0:T(8,128)(2,1)} %get-tuple-element.16), kind=kOutput, calls=%fused_computation.104 | convolution fusion | flops 540803072 | bytes 3146752 | tf_op jit(solution)/shard_map/dot_general | solution.py:36
  201.6 2.6 %convolution_convert_fusion.2 = bf16[512,512]{1,0:T(8,128)(2,1)} fusion(bf16[512,512]{0,1:T(8,128)(2,1)} %fusion.36), kind=kOutput, calls=%fused_computation.82 | convolution fusion | flops 268697600 | bytes 1048576 | tf_op jit(solution)/shard_map/dot_general | solution.py:31
  204.2 2.5 convolution_convert_fusion.1
  206.7 3.4 %fusion.39 = bf16[512,512]{0,1:T(8,128)(2,1)} fusion(bf16[512,512]{1,0:T(8,128)(2,1)} %convolution_convert_fusion.1, f32[]{:T(128)S(6)} %add.250, bf16[3,512,512]{1,2,0:T(8,128)(2,1)} %get-tuple-element.16), kind=kOutput, calls=%fused_computation.107 | convolution fusion | flops 540803072 | bytes 3146752 | tf_op jit(solution)/shard_map/dot_general | solution.py:36
  210.1 2.5 convolution_convert_fusion
  212.5 2.8 %copy.7 = bf16[2,3,512,512]{2,3,1,0:T(8,128)(2,1)} copy(bf16[2,3,512,512]{3,2,1,0:T(8,128)(2,1)S(1)} %copy-done) | data formatting | bytes 6291456 | tf_op args[4]
  215.3 3.8 %multiply_reduce_fusion = (f32[512]{0:T(512)S(1)}, f32[512,512]{0,1:T(8,128)}) fusion(bf16[512,512]{0,1:T(8,128)(2,1)} %fusion.39, bf16[512,512]{1,0:T(8,128)(2,1)} %convolution_convert_fusion, bf16[6,512,512]{1,2,0:T(8,128)(2,1)} %bitcast.202), kind=kOutput, calls=%fused_computation.139 | convolution fusion | flops 540540416 | bytes 4196352 | tf_op jit(solution)/shard_map/dot_general | solution.py:36
  219.2 3.6 %multiply_reduce_fusion.1 = (f32[512]{0:T(512)S(1)}, f32[512,512]{0,1:T(8,128)}) fusion(bf16[512,512]{0,1:T(8,128)(2,1)} %fusion.36, bf16[512,512]{1,0:T(8,128)(2,1)} %convolution_convert_fusion.2, bf16[6,512,512]{1,2,0:T(8,128)(2,1)S(1)} %bitcast.203), kind=kOutput, calls=%fused_computation.145 | convolution fusion | flops 540540416 | bytes 4196352 | tf_op jit(solution)/shard_map/dot_general | solution.py:36
  222.7 3.6 %multiply_reduce_fusion.2 = (f32[512]{0:T(512)S(1)}, f32[512,512]{0,1:T(8,128)}) fusion(bf16[512,512]{0,1:T(8,128)(2,1)} %fusion.33, bf16[512,512]{1,0:T(8,128)(2,1)} %convolution_convert_fusion.4, bf16[6,512,512]{1,2,0:T(8,128)(2,1)S(1)} %bitcast.204), kind=kOutput, calls=%fused_computation.151 | convolution fusion | flops 540540416 | bytes 4196352 | tf_op jit(solution)/shard_map/dot_general | solution.py:36
  226.4 3.6 %multiply_reduce_fusion.3 = (f32[512]{0:T(512)S(1)}, f32[512,512]{0,1:T(8,128)}) fusion(bf16[512,512]{0,1:T(8,128)(2,1)} %fusion.30, bf16[512,512]{1,0:T(8,128)(2,1)} %convolution_convert_fusion.6, bf16[6,512,512]{1,2,0:T(8,128)(2,1)S(1)} %bitcast.205), kind=kOutput, calls=%fused_computation.157 | convolution fusion | flops 540540416 | bytes 4196352 | tf_op jit(solution)/shard_map/dot_general | solution.py:36
  230.0 3.7 %multiply_reduce_fusion.4 = (f32[512]{0:T(512)S(1)}, f32[512,512]{0,1:T(8,128)}) fusion(bf16[512,512]{0,1:T(8,128)(2,1)} %fusion.27, bf16[512,512]{1,0:T(8,128)(2,1)} %convolution_convert_fusion.8, bf16[6,512,512]{1,2,0:T(8,128)(2,1)S(1)} %bitcast.206), kind=kOutput, calls=%fused_computation.163 | convolution fusion | flops 540540416 | bytes 4196352 | tf_op jit(solution)/shard_map/dot_general | solution.py:36
  233.6 3.8 %multiply_reduce_fusion.5 = (f32[512]{0:T(512)S(1)}, f32[512,512]{0,1:T(8,128)}) fusion(bf16[512,512]{0,1:T(8,128)(2,1)} %fusion.24, bf16[512,512]{1,0:T(8,128)(2,1)} %convolution_convert_fusion.10, bf16[6,512,512]{1,2,0:T(8,128)(2,1)S(1)} %bitcast.207), kind=kOutput, calls=%fused_computation.169 | convolution fusion | flops 540540416 | bytes 4196352 | tf_op jit(solution)/shard_map/dot_general | solution.py:36
  237.4 0.6 fusion.60
  238.1 0.6 fusion.171
  238.7 0.6 fusion.172
  239.7 2.1 convolution_convert_fusion.12
  241.9 1.2 convolution_bitcast_fusion.9
  243.1 1.4 convolution_convert_fusion.13
  244.6 0.7 pad_maximum_fusion.2
  245.3 1.4 bitcast_dynamic-update-slice_fusion.5
  246.8 1.4 bitcast_dynamic-update-slice_fusion.4
  248.8 2.8 %copy.12 = bf16[2,3,512,512]{3,2,1,0:T(8,128)(2,1)} copy(bf16[2,3,512,512]{2,3,1,0:T(8,128)(2,1)S(1)} %bitcast.209) | data formatting | bytes 6291456
  (41 shorter events, 2.0 us)
Async XLA Ops:
  0.6 6.7 %copy-start.10 = (bf16[128,1024]{1,0:T(8,128)(2,1)S(1)}, bf16[128,1024]{1,0:T(8,128)(2,1)}, u32[]{:S(2)}) copy-start(bf16[128,1024]{1,0:T(8,128)(2,1)} %param.5) | copy-start | bytes 786436
  0.6 6.7 %copy-start = (bf16[2,3,512,512]{3,2,1,0:T(8,128)(2,1)S(1)}, bf16[2,3,512,512]{3,2,1,0:T(8,128)(2,1)}, u32[]{:S(2)}) copy-start(bf16[2,3,512,512]{3,2,1,0:T(8,128)(2,1)} %param.9) | copy-start | bytes 9437188
  0.7 7.1 %copy-start.11 = (bf16[128,1024]{1,0:T(8,128)(2,1)S(1)}, bf16[128,1024]{1,0:T(8,128)(2,1)}, u32[]{:S(2)}) copy-start(bf16[128,1024]{1,0:T(8,128)(2,1)} %param.6) | copy-start | bytes 786436
  215.3 3.8 %copy-start.1 = (bf16[2,3,512,512]{2,3,1,0:T(8,128)(2,1)S(1)}, bf16[2,3,512,512]{2,3,1,0:T(8,128)(2,1)}, u32[]{:S(2)}) copy-start(bf16[2,3,512,512]{2,3,1,0:T(8,128)(2,1)} %copy.7) | copy-start | bytes 9437188
  237.4 2.0 copy-start.7
  237.4 2.0 copy-start.12
  238.1 3.8 %copy-start.9 = (f32[512,512]{0,1:T(8,128)S(1)}, f32[512,512]{0,1:T(8,128)}, u32[]{:S(2)}) copy-start(f32[512,512]{0,1:T(8,128)} %get-tuple-element.27) | copy-start | bytes 3145732
  238.1 5.0 %copy-start.4 = (f32[512,512]{0,1:T(8,128)S(1)}, f32[512,512]{0,1:T(8,128)}, u32[]{:S(2)}) copy-start(f32[512,512]{0,1:T(8,128)} %get-tuple-element.31) | copy-start | bytes 3145732
  238.1 5.0 %copy-start.6 = (f32[512,512]{0,1:T(8,128)S(1)}, f32[512,512]{0,1:T(8,128)}, u32[]{:S(2)}) copy-start(f32[512,512]{0,1:T(8,128)} %get-tuple-element.29) | copy-start | bytes 3145732
  244.6 3.7 %copy-start.5 = (f32[512,512]{0,1:T(8,128)S(1)}, f32[512,512]{0,1:T(8,128)}, u32[]{:S(2)}) copy-start(f32[512,512]{0,1:T(8,128)} %get-tuple-element.31) | copy-start | bytes 3145732
  244.6 3.7 %copy-start.13 = (f32[512]{0:T(512)S(1)}, f32[512]{0:T(512)}, u32[]{:S(2)}) copy-start(f32[512]{0:T(512)} %fusion.172) | copy-start | bytes 6148
  244.6 3.8 %copy-start.8 = (f32[512,512]{0,1:T(8,128)S(1)}, f32[512,512]{0,1:T(8,128)}, u32[]{:S(2)}) copy-start(f32[512,512]{0,1:T(8,128)} %get-tuple-element.21) | copy-start | bytes 3145732
  245.3 3.2 %copy-start.3 = (f32[512,512]{0,1:T(8,128)S(1)}, f32[512,512]{0,1:T(8,128)}, u32[]{:S(2)}) copy-start(f32[512,512]{0,1:T(8,128)} %get-tuple-element.23) | copy-start | bytes 3145732
  246.8 1.9 copy-start.2
where the time goes:
time: 255 us; the launch traced here: 252 us
  blocking collectives  140 us (55%)
  matrix products  86.6 us (34%)
  other arithmetic  13.9 us (5%)
  local copies, waits for them, and re-layouts  5.62 us (2%)
  between operations  5.04 us (2%)
    psum x1, blocking collectives, summed_grads(): total = lax.psum(partial_value, 'tok')  140 us
    dot_general x12, matrix products, newton_schulz(): jnp.dot(mixed, iterate, preferred_element_type=jnp.float32)  43 us
    dot_general x12, matrix products, newton_schulz(): jnp.dot(iterate, iterate.T, preferred_element_type=jnp.float32)  30 us
    unnamed x30, local copies, waits for them, and re-layouts  5.62 us

commit v1 on v0

v1 whole, which is shorter than its diff:
```python
import functools

import jax
import jax.numpy as jnp
from jax import lax
from jax.experimental import pallas as pl
from jax.experimental.pallas import tpu as pltpu
from jax.sharding import PartitionSpec as P

NS_STEPS = 2
F32 = jnp.float32
BF16 = jnp.bfloat16
VMEM_SPEC = pl.BlockSpec(memory_space=pltpu.VMEM)
ANY_SPEC = pl.BlockSpec(memory_space=pl.ANY)
PARAMS = pltpu.CompilerParams(vmem_limit_bytes=40 * 1024 * 1024)


def place():
    me = lax.axis_index("tok")
    core = me % 2
    bit1 = (me // 2) % 2
    bit2 = (me // 4) % 2
    half = jnp.where(core == 0, bit1, bit2)
    quarter = jnp.where(core == 0, bit2, bit1)
    return core, half, quarter


def dot(a, b, ca=1, cb=0):
    return lax.dot_general(a, b, (((ca,), (cb,)), ((), ())), preferred_element_type=F32)


def pack_kernel(keys, values, rates, own, other):
    tokens, width = own.shape[1:]
    core, _, _ = place()
    for head, out in ((core, own), (1 - core, other)):
        cols = pl.ds(pl.multiple_of(head * width, width), width)
        out[0] = keys[:, cols]
        rate = jnp.where(head == 0, rates[0:1, :], rates[1:2, :])
        rate = jnp.broadcast_to(rate, (tokens, tokens)).T[:, 0:1]
        out[1] = (-rate * values[:, cols].astype(F32)).astype(BF16)


def grads_kernel(t0, t1, t2, t3, weights, send_a, send_b, keep_a, keep_b, keys, outer, gate_w, up_w, down_w, sems):
    tokens, width = t0.shape[1:]
    part = width // 2
    piece = part // 2
    core, half, quarter = place()
    cols = pl.ds(pl.multiple_of(half * part, part), part)
    copies = [
        pltpu.make_async_copy(weights.at[core, 0, :, cols], gate_w, sems.at[0]),
        pltpu.make_async_copy(weights.at[core, 1, :, cols], up_w, sems.at[1]),
        pltpu.make_async_copy(weights.at[core, 2, cols, :], down_w, sems.at[2]),
    ]
    for copy in copies:
        copy.start()
    for at, src in enumerate((t0, t1, t2, t3)):
        keys[at * tokens : (at + 1) * tokens, :] = src[0]
        outer[at * tokens : (at + 1) * tokens, :] = src[1]
    for copy in copies:
        copy.wait()
    k = keys[...]
    o = outer[...]
    for mine in (0, 1):
        at = (1 - quarter) if mine == 0 else quarter
        cut = pl.ds(pl.multiple_of(at * piece, piece), piece)
        gate = dot(k, gate_w[:, cut])
        upper = dot(k, up_w[:, cut])
        back = dot(o, down_w[cut, :], 1, 1)
        sigma = jax.nn.sigmoid(gate)
        silu_gate = gate * sigma
        hidden = (silu_gate * upper).astype(BF16)
        d_gate = (back * upper * sigma * (1.0 + gate * (1.0 - sigma))).astype(BF16)
        d_upper = (back * silu_gate).astype(BF16)
        out_a, out_b = (send_a, send_b) if mine == 0 else (keep_a, keep_b)
        out_a[0] = dot(k, d_gate, 0, 0).astype(out_a.dtype)
        out_a[1] = dot(k, d_upper, 0, 0).astype(out_a.dtype)
        out_b[...] = dot(hidden, o, 0, 0).astype(out_b.dtype)


def newton_schulz(matrix):
    wide = matrix.astype(F32)
    norm = jnp.sqrt(jnp.sum(wide * wide)) + 1e-07
    iterate = (wide / norm).astype(BF16)
    for _ in range(NS_STEPS):
        gram = dot(iterate, iterate, 1, 1).astype(BF16)
        mixed = (-4.775 * gram.astype(F32) + 2.0315 * dot(gram, gram)).astype(BF16)
        iterate = (3.4445 * iterate.astype(F32) + dot(mixed, iterate)).astype(BF16)
    return iterate


def renormed(old, update):
    old = old.astype(F32)
    fresh = old - update.astype(F32)
    scale = jnp.sqrt(
        (jnp.mean(old * old, axis=1, keepdims=True) + 1e-06)
        / (jnp.mean(fresh * fresh, axis=1, keepdims=True) + 1e-06)
    )
    return (fresh * scale).astype(BF16)


def ns_kernel(first, rows_cut, p_own, p_second, p_first, p_both, weights, new, total, old, sem):
    count = new.shape[0]
    core, half, quarter = place()
    copy = pltpu.make_async_copy(weights.at[core, pl.ds(first, count)], old, sem)
    copy.start()
    for piece, h, q in (
        (p_own, half, quarter),
        (p_second, half, 1 - quarter),
        (p_first, 1 - half, quarter),
        (p_both, 1 - half, 1 - quarter),
    ):
        size = piece.shape[0] if rows_cut else piece.shape[2]
        cut = pl.ds(pl.multiple_of((2 * h + q) * size, size), size)
        if rows_cut:
            total[0, cut, :] = piece[...]
        else:
            for at in range(count):
                total[at, :, cut] = piece[at]
    updates = [newton_schulz(total[at]) for at in range(count)]
    copy.wait()
    for at in range(count):
        new[at] = renormed(old[at], updates[at])


def updated(first, rows_cut, pieces, weights):
    width = weights.shape[3]
    count = 1 if rows_cut else pieces[0].shape[0]
    return pl.pallas_call(
        functools.partial(ns_kernel, first, rows_cut),
        out_shape=jax.ShapeDtypeStruct((count, width, width), BF16),
        in_specs=[VMEM_SPEC] * 4 + [ANY_SPEC],
        out_specs=VMEM_SPEC,
        scratch_shapes=[
            pltpu.VMEM((count, width, width), BF16),
            pltpu.VMEM((count, width, width), BF16),
            pltpu.SemaphoreType.DMA,
        ],
        compiler_params=PARAMS,
    )(*pieces, weights)


def gate_up_kernel(queries, own, other, hidden, new_weights, sems):
    width = own.shape[2]
    core, _, _ = place()
    copies = []
    for at, (head, part) in enumerate(((core, own), (1 - core, other))):
        copy = pltpu.make_async_copy(part, new_weights.at[head, pl.ds(0, 2)], sems.at[at])
        copy.start()
        copies.append(copy)
    for head, part in ((core, own), (1 - core, other)):
        cols = pl.ds(pl.multiple_of(head * width, width), width)
        gate = dot(queries[:, cols], part[0])
        upper = dot(queries[:, cols], part[1])
        hidden[:, cols] = (gate * jax.nn.sigmoid(gate) * upper).astype(BF16)
    for copy in copies:
        copy.wait()


def down_kernel(hidden, own, other, held, readout, new_weights, sems):
    width = own.shape[2]
    core, _, _ = place()
    copies = []
    for at, (head, part) in enumerate(((core, own), (1 - core, other))):
        copy = pltpu.make_async_copy(part, new_weights.at[head, pl.ds(2, 1)], sems.at[at])
        copy.start()
        copies.append(copy)
    for head, part in ((core, own), (1 - core, other)):
        cols = pl.ds(pl.multiple_of(head * width, width), width)
        readout[:, cols] = dot(hidden[:, cols], part[0]).astype(BF16)
    for copy in copies:
        copy.wait()


def body(size, keys, values, queries, rates, fast_weights):
    tokens = keys.shape[0]
    heads, _, width, _ = fast_weights.shape
    quarter = width // 4
    sibling = [(i, i ^ 1) for i in range(size)]
    first = [(i, i ^ (2 if i % 2 == 0 else 4)) for i in range(size)]
    second = [(i, i ^ (4 if i % 2 == 0 else 2)) for i in range(size)]
    across = [(i, i ^ 1 ^ (4 if i % 2 == 0 else 2)) for i in range(size)]
    rest = [[(i, i ^ (1 << bit)) for i in range(size)] for bit in range(3, size.bit_length() - 1)]

    def move(value, pairs):
        return lax.ppermute(value, "tok", pairs)

    pair = jax.ShapeDtypeStruct((2, tokens, width), BF16)
    own, other = pl.pallas_call(
        pack_kernel,
        out_shape=(pair, pair),
        in_specs=[VMEM_SPEC] * 3,
        out_specs=(VMEM_SPEC, VMEM_SPEC),
        compiler_params=PARAMS,
    )(keys, values, rates)
    blocks = (own, move(other, sibling), move(own, first), move(other, across))
    shape_a, shape_b = (2, width, quarter), (quarter, width)
    send_a, send_b, keep_a, keep_b = pl.pallas_call(
        grads_kernel,
        out_shape=(
            jax.ShapeDtypeStruct(shape_a, BF16),
            jax.ShapeDtypeStruct(shape_b, BF16),
            jax.ShapeDtypeStruct(shape_a, F32),
            jax.ShapeDtypeStruct(shape_b, F32),
        ),
        in_specs=[VMEM_SPEC] * 4 + [ANY_SPEC],
        out_specs=(VMEM_SPEC,) * 4,
        scratch_shapes=[
            pltpu.VMEM((4 * tokens, width), BF16),
            pltpu.VMEM((4 * tokens, width), BF16),
            pltpu.VMEM((width, width // 2), BF16),
            pltpu.VMEM((width, width // 2), BF16),
            pltpu.VMEM((width // 2, width), BF16),
            pltpu.SemaphoreType.DMA((3,)),
        ],
        compiler_params=PARAMS,
    )(*blocks, fast_weights)

    def reduced(send, keep):
        part = (keep + move(send, second).astype(F32)).astype(BF16)
        for pairs in rest:
            part = (part.astype(F32) + move(part, pairs).astype(F32)).astype(BF16)
        return part

    def gathered(part):
        over_second = move(part, second)
        over_first = move(part, first)
        return part, over_second, over_first, move(over_second, first)

    sum_a = reduced(send_a, keep_a)
    sum_b = reduced(send_b, keep_b)
    new_a = updated(0, False, gathered(sum_a), fast_weights)
    swap_a = move(new_a, sibling)
    hidden, new_weights = pl.pallas_call(
        gate_up_kernel,
        out_shape=(
            jax.ShapeDtypeStruct(queries.shape, BF16),
            jax.ShapeDtypeStruct(fast_weights.shape, BF16),
        ),
        in_specs=[VMEM_SPEC] * 3,
        out_specs=(VMEM_SPEC, ANY_SPEC),
        scratch_shapes=[pltpu.SemaphoreType.DMA((2,))],
        compiler_params=PARAMS,
    )(queries, new_a, swap_a)
    new_b = updated(2, True, gathered(sum_b), fast_weights)
    swap_b = move(new_b, sibling)
    return pl.pallas_call(
        down_kernel,
        out_shape=(
            jax.ShapeDtypeStruct(queries.shape, BF16),
            jax.ShapeDtypeStruct(fast_weights.shape, BF16),
        ),
        in_specs=[VMEM_SPEC] * 3 + [ANY_SPEC],
        out_specs=(VMEM_SPEC, ANY_SPEC),
        scratch_shapes=[pltpu.SemaphoreType.DMA((2,))],
        input_output_aliases={3: 1},
        compiler_params=PARAMS,
    )(hidden, new_b, swap_b, new_weights)


def solution(mesh):
    return jax.shard_map(
        functools.partial(body, mesh.shape["tok"]),
        mesh=mesh,
        in_specs=(
            P(("grp", "tok"), None),
            P(("grp", "tok"), None),
            P(("grp", "tok"), None),
            P(None, ("grp", "tok")),
            P(),
        ),
        out_specs=(P(("grp", "tok"), None), P("grp", None, None, None)),
        check_vma=False,
    )
```

time: 255 us -> 76.7 us (0.30); the launches traced: 252 us -> 76.5 us
  blocking collectives: 140 us -> 0 us
  matrix products: 86.6 us -> 0 us
  waiting for transfers between devices: 0 us -> 39 us
  starting transfers between devices: 0 us -> 17.6 us
  Pallas kernels: 0 us -> 14.4 us
  other arithmetic: 13.9 us -> 0.19 us
  between operations: 5.04 us -> 0.78 us
    psum x1 -> x0, blocking collectives: 140 us -> none  [summed_grads(): total = lax.psum(partial_value, 'tok')]
    dot_general x40 -> x0, matrix products: 86.6 us -> none  [the longest x12 43 us: newton_schulz(): jnp.dot(mixed, iterate, preferred_element_type=jnp.float32)]
    ppermute x0 -> x15, waiting for transfers between devices: none -> 39 us  [move(): return lax.ppermute(value, 'tok', pairs)]
    ppermute x0 -> x15, starting transfers between devices: none -> 17.6 us  [move(): return lax.ppermute(value, 'tok', pairs)]
    pallas_call x0 -> x6, Pallas kernels: none -> 14.4 us  [the longest x2 8.39 us: updated(): pl.pallas_call(functools.partial(ns_kernel, first, rows_cut), out_shape=j...]
    another operation x3 -> x0, other arithmetic: 4.07 us -> none  [the longest x2 3.95 us: swiglu_grads(): return jnp.stack([grad_gate, grad_upper, grad_down])]
    reduce_sum x2 -> x0, other arithmetic: 3.77 us -> none  [the longest x1 3.13 us: newton_schulz(): jnp.sum(wide * wide)]
    unnamed x5 -> x0, other arithmetic: 3.23 us -> none
  transfers between devices with their start and end apart: 0 -> 15, of which waited for: 0 -> 10; matrix products, arithmetic and copies ran while one was open for 0% -> 0% of each run, Pallas kernels for 0% -> 13%
where the time goes in v1:
time: 76.7 us; the launch traced here: 76.5 us
  waiting for transfers between devices  39 us (51%)
  starting transfers between devices  17.6 us (23%)
  Pallas kernels  14.4 us (19%)
  local copies, waits for them, and re-layouts  4.47 us (6%)
  between operations  0.78 us (1%)
    ppermute x15, waiting for transfers between devices, move(): return lax.ppermute(value, 'tok', pairs)  39 us
    ppermute x15, starting transfers between devices, move(): return lax.ppermute(value, 'tok', pairs)  17.6 us
    pallas_call x2, Pallas kernels, updated(): pl.pallas_call(functools.partial(ns_kernel, first, rows_cut), out_shape=j...  8.39 us
    unnamed x12, local copies, waits for them, and re-layouts  4.47 us
    pallas_call x1, Pallas kernels, body(): pl.pallas_call(grads_kernel, out_shape=(jax.ShapeDtypeStruct(shape_a, BF1...  2.38 us
    pallas_call x1, Pallas kernels, body(): pl.pallas_call(down_kernel, out_shape=(jax.ShapeDtypeStruct(queries.shape...  1.82 us
    pallas_call x1, Pallas kernels, body(): pl.pallas_call(gate_up_kernel, out_shape=(jax.ShapeDtypeStruct(queries.sh...  1.65 us
  transfers between devices with their start and end apart: 15, of which 10 were waited for; matrix products, arithmetic and copies ran while one was open for 0% of the time, Pallas kernels for 13%

profile of v1, /device:TPU:0, one launch (start us, length us, event | category | flops | bytes accessed | tf_op | source)
XLA Modules:
  0.0 76.5 jit_solution(8266565676513366191)
XLA Ops:
  0.6 0.0 copy-start.3
  0.6 0.9 %copy-done.3 = bf16[128,1024]{1,0:T(8,128)(2,1)S(1)} copy-done((bf16[128,1024]{1,0:T(8,128)(2,1)S(1)}, bf16[128,1024]{1,0:T(8,128)(2,1)}, u32[]{:S(2)}) %copy-start.3) | copy-done | bytes 262168
  1.6 0.0 copy-start.4
  1.6 0.9 %copy-done.4 = bf16[128,1024]{1,0:T(8,128)(2,1)S(1)} copy-done((bf16[128,1024]{1,0:T(8,128)(2,1)S(1)}, bf16[128,1024]{1,0:T(8,128)(2,1)}, u32[]{:S(2)}) %copy-start.4) | copy-done | bytes 262168
  2.5 0.0 copy-start.5
  2.5 0.7 copy-done.5
  3.2 0.2 shard_map.68
  3.4 3.0 %collective-permute-start.1 = (bf16[2,128,512]{2,1,0:T(8,128)(2,1)S(1)}, bf16[2,128,512]{2,1,0:T(8,128)(2,1)S(1)}, u32[]{:S(2)}, u32[]{:S(2)}) collective-permute-start(bf16[2,128,512]{2,1,0:T(8,128)(2,1)S(1)} %get-tuple-element.10.t0), channel_id=1, source_target_pairs={{0,2},{1,5},{2,0},{3,7},{4,6},{5,1},{6,4},{7,3},{8,10},{9,13},{10,... | collective-permute-start | bytes 786440 | tf_op jit(solution)/shard_map/ppermute | solution.py:185
  6.4 0.0 collective-permute-start.2
  6.4 0.2 collective-permute-start
  6.6 6.0 %collective-permute-done.1.t2 = bf16[2,128,512]{2,1,0:T(8,128)(2,1)S(1)} collective-permute-done((bf16[2,128,512]{2,1,0:T(8,128)(2,1)S(1)}, bf16[2,128,512]{2,1,0:T(8,128)(2,1)S(1)}, u32[]{:S(2)}, u32[]{:S(2)}) %collective-permute-start.1) | collective-permute-done | bytes 262176 | tf_op jit(solution)/shard_map/ppermute | solution.py:185
  12.6 1.0 %collective-permute-done.2.t3 = bf16[2,128,512]{2,1,0:T(8,128)(2,1)S(1)} collective-permute-done((bf16[2,128,512]{2,1,0:T(8,128)(2,1)S(1)}, bf16[2,128,512]{2,1,0:T(8,128)(2,1)S(1)}, u32[]{:S(2)}, u32[]{:S(2)}) %collective-permute-start.2) | collective-permute-done | bytes 262176 | tf_op jit(solution)/shard_map/ppermute | solution.py:185
  13.6 0.0 collective-permute-done.t1
  13.6 1.9 %copy-done = bf16[2,3,512,512]{3,2,1,0:T(8,128)(2,1)S(1)} copy-done((bf16[2,3,512,512]{3,2,1,0:T(8,128)(2,1)S(1)}, bf16[2,3,512,512]{3,2,1,0:T(8,128)(2,1)}, u32[]{:S(2)}) %copy-start) | copy-done | bytes 3145752
  15.5 2.4 %shard_map.69 = (bf16[2,512,128]{2,1,0:T(8,128)(2,1)S(1)}, bf16[128,512]{1,0:T(8,128)(2,1)S(1)}, f32[2,512,128]{2,1,0:T(8,128)S(1)}, f32[128,512]{1,0:T(8,128)S(1)}) custom-call(bf16[2,128,512]{2,1,0:T(8,128)(2,1)S(1)} %get-tuple-element.10.t0, bf16[2,128,512]{2,1,0:T(8,128)(2,1)S(1)} %collective-permute-done.t1, ...), custom_call_target="tpu_custom_call" | custom-call | tf_op jit(solution)/shard_map/pallas_call | solution.py:197
  17.9 2.1 %collective-permute-start.3 = (bf16[2,512,128]{2,1,0:T(8,128)(2,1)S(1)}, bf16[2,512,128]{2,1,0:T(8,128)(2,1)S(1)}, u32[]{:S(2)}, u32[]{:S(2)}) collective-permute-start(bf16[2,512,128]{2,1,0:T(8,128)(2,1)S(1)} %get-tuple-element.13), channel_id=1, source_target_pairs={{0,4},{1,3},{2,6},{3,1},{4,0},{5,7},{6,2},{7,5},{8,12},{9,11},{10,... | collective-permute-start | bytes 786440 | tf_op jit(solution)/shard_map/ppermute | solution.py:185
  20.0 4.4 %collective-permute-done.3 = bf16[2,512,128]{2,1,0:T(8,128)(2,1)S(1)} collective-permute-done((bf16[2,512,128]{2,1,0:T(8,128)(2,1)S(1)}, bf16[2,512,128]{2,1,0:T(8,128)(2,1)S(1)}, u32[]{:S(2)}, u32[]{:S(2)}) %collective-permute-start.3) | collective-permute-done | bytes 262176 | tf_op jit(solution)/shard_map/ppermute | solution.py:185
  24.4 0.1 add_convert_fusion.1
  24.4 3.1 %collective-permute-start.4 = (bf16[2,512,128]{2,1,0:T(8,128)(2,1)S(1)}, bf16[2,512,128]{2,1,0:T(8,128)(2,1)S(1)}, u32[]{:S(2)}, u32[]{:S(2)}) collective-permute-start(bf16[2,512,128]{2,1,0:T(8,128)(2,1)S(1)} %add_convert_fusion.1), channel_id=1, source_target_pairs={{0,8},{1,9},{2,10},{3,11},{4,12},{5,13},{6,14},{7,15},{8,0},{9,1},... | collective-permute-start | bytes 786440 | tf_op jit(solution)/shard_map/ppermute | solution.py:185
  27.5 10.3 %collective-permute-done.4 = bf16[2,512,128]{2,1,0:T(8,128)(2,1)S(1)} collective-permute-done((bf16[2,512,128]{2,1,0:T(8,128)(2,1)S(1)}, bf16[2,512,128]{2,1,0:T(8,128)(2,1)S(1)}, u32[]{:S(2)}, u32[]{:S(2)}) %collective-permute-start.4) | collective-permute-done | bytes 262176 | tf_op jit(solution)/shard_map/ppermute | solution.py:185
  37.8 0.1 add_convert_fusion.p_own
  37.9 0.8 %collective-permute-start.5 = (bf16[2,512,128]{2,1,0:T(8,128)(2,1)S(1)}, bf16[2,512,128]{2,1,0:T(8,128)(2,1)S(1)}, u32[]{:S(2)}, u32[]{:S(2)}) collective-permute-start(bf16[2,512,128]{2,1,0:T(8,128)(2,1)S(1)} %add_convert_fusion.p_own), channel_id=1, source_target_pairs={{0,4},{1,3},{2,6},{3,1},{4,0},{5,7},{6,2},{7,5},{8,12},{9,11},{10,... | collective-permute-start | bytes 786440 | tf_op jit(solution)/shard_map/ppermute | solution.py:185
  38.6 1.3 %collective-permute-start.9 = (bf16[128,512]{1,0:T(8,128)(2,1)S(1)}, bf16[128,512]{1,0:T(8,128)(2,1)S(1)}, u32[]{:S(2)}, u32[]{:S(2)}) collective-permute-start(bf16[128,512]{1,0:T(8,128)(2,1)S(1)} %get-tuple-element.16), channel_id=1, source_target_pairs={{0,4},{1,3},{2,6},{3,1},{4,0},{5,7},{6,2},{7,5},{8,12},{9,11},{10,... | collective-permute-start | bytes 393224 | tf_op jit(solution)/shard_map/ppermute | solution.py:185
  40.0 1.5 %collective-permute-start.6 = (bf16[2,512,128]{2,1,0:T(8,128)(2,1)S(1)}, bf16[2,512,128]{2,1,0:T(8,128)(2,1)S(1)}, u32[]{:S(2)}, u32[]{:S(2)}) collective-permute-start(bf16[2,512,128]{2,1,0:T(8,128)(2,1)S(1)} %add_convert_fusion.p_own), channel_id=1, source_target_pairs={{0,2},{1,5},{2,0},{3,7},{4,6},{5,1},{6,4},{7,3},{8,10},{9,13},{10,... | collective-permute-start | bytes 786440 | tf_op jit(solution)/shard_map/ppermute | solution.py:185
  41.5 5.6 %collective-permute-done.5.p_second = bf16[2,512,128]{2,1,0:T(8,128)(2,1)S(1)} collective-permute-done((bf16[2,512,128]{2,1,0:T(8,128)(2,1)S(1)}, bf16[2,512,128]{2,1,0:T(8,128)(2,1)S(1)}, u32[]{:S(2)}, u32[]{:S(2)}) %collective-permute-start.5) | collective-permute-done | bytes 262176 | tf_op jit(solution)/shard_map/ppermute | solution.py:185
  47.0 1.5 %collective-permute-start.7 = (bf16[2,512,128]{2,1,0:T(8,128)(2,1)S(1)}, bf16[2,512,128]{2,1,0:T(8,128)(2,1)S(1)}, u32[]{:S(2)}, u32[]{:S(2)}) collective-permute-start(bf16[2,512,128]{2,1,0:T(8,128)(2,1)S(1)} %collective-permute-done.5.p_second), channel_id=1, source_target_pairs={{0,2},{1,5},{2,0},{3,7},{4,6},{5,1},{6,4},{7,3},{8,10},{9,13},{10,... | collective-permute-start | bytes 786440 | tf_op jit(solution)/shard_map/ppermute | solution.py:185
  48.6 2.7 %collective-permute-done.9 = bf16[128,512]{1,0:T(8,128)(2,1)S(1)} collective-permute-done((bf16[128,512]{1,0:T(8,128)(2,1)S(1)}, bf16[128,512]{1,0:T(8,128)(2,1)S(1)}, u32[]{:S(2)}, u32[]{:S(2)}) %collective-permute-start.9) | collective-permute-done | bytes 131104 | tf_op jit(solution)/shard_map/ppermute | solution.py:185
  51.3 0.1 collective-permute-start.10
  51.4 0.0 collective-permute-done.6.p_first
  51.4 2.0 %collective-permute-done.7.p_both = bf16[2,512,128]{2,1,0:T(8,128)(2,1)S(1)} collective-permute-done((bf16[2,512,128]{2,1,0:T(8,128)(2,1)S(1)}, bf16[2,512,128]{2,1,0:T(8,128)(2,1)S(1)}, u32[]{:S(2)}, u32[]{:S(2)}) %collective-permute-start.7) | collective-permute-done | bytes 262176 | tf_op jit(solution)/shard_map/ppermute | solution.py:185
  53.4 0.0 copy-done.1
  53.4 5.4 %shard_map.70.own = bf16[2,512,512]{2,1,0:T(8,128)(2,1)S(1)} custom-call(bf16[2,512,128]{2,1,0:T(8,128)(2,1)S(1)} %add_convert_fusion.p_own, bf16[2,512,128]{2,1,0:T(8,128)(2,1)S(1)} %collective-permute-done.5.p_second, bf16[2,512,128]{2,1,0:T(8,128)(2,1)S(1)} %collective-permute-done.6.p_first, bf16[2,512,128]{2,1,0:T(8,128)(2,1)S(1)} %collective-permute-done.7.p_both, ...), custom_call_target="tpu_custom_call" | custom-call | tf_op jit(solution)/shard_map/pallas_call | solution.py:128
  58.8 0.0 copy-start.2
  58.8 0.1 collective-permute-start.8
  58.9 0.0 collective-permute-done.10
  59.0 0.4 collective-permute-start.11
  59.4 1.5 %collective-permute-start.12 = (bf16[128,512]{1,0:T(8,128)(2,1)S(1)}, bf16[128,512]{1,0:T(8,128)(2,1)S(1)}, u32[]{:S(2)}, u32[]{:S(2)}) collective-permute-start(bf16[128,512]{1,0:T(8,128)(2,1)S(1)} %add_convert_fusion.2.p_own), channel_id=1, source_target_pairs={{0,2},{1,5},{2,0},{3,7},{4,6},{5,1},{6,4},{7,3},{8,10},{9,13},{10,... | collective-permute-start | bytes 393224 | tf_op jit(solution)/shard_map/ppermute | solution.py:185
  60.8 3.8 %collective-permute-done.11.p_second = bf16[128,512]{1,0:T(8,128)(2,1)S(1)} collective-permute-done((bf16[128,512]{1,0:T(8,128)(2,1)S(1)}, bf16[128,512]{1,0:T(8,128)(2,1)S(1)}, u32[]{:S(2)}, u32[]{:S(2)}) %collective-permute-start.11) | collective-permute-done | bytes 131104 | tf_op jit(solution)/shard_map/ppermute | solution.py:185
  64.7 2.0 %collective-permute-start.13 = (bf16[128,512]{1,0:T(8,128)(2,1)S(1)}, bf16[128,512]{1,0:T(8,128)(2,1)S(1)}, u32[]{:S(2)}, u32[]{:S(2)}) collective-permute-start(bf16[128,512]{1,0:T(8,128)(2,1)S(1)} %collective-permute-done.11.p_second), channel_id=1, source_target_pairs={{0,2},{1,5},{2,0},{3,7},{4,6},{5,1},{6,4},{7,3},{8,10},{9,13},{10,... | collective-permute-start | bytes 393224 | tf_op jit(solution)/shard_map/ppermute | solution.py:185
  66.7 0.0 collective-permute-done.12.p_first
  66.7 3.0 %collective-permute-done.13.p_both = bf16[128,512]{1,0:T(8,128)(2,1)S(1)} collective-permute-done((bf16[128,512]{1,0:T(8,128)(2,1)S(1)}, bf16[128,512]{1,0:T(8,128)(2,1)S(1)}, u32[]{:S(2)}, u32[]{:S(2)}) %collective-permute-start.13) | collective-permute-done | bytes 131104 | tf_op jit(solution)/shard_map/ppermute | solution.py:185
  69.6 3.0 %shard_map.72.own = bf16[1,512,512]{2,1,0:T(8,128)(2,1)S(1)} custom-call(bf16[128,512]{1,0:T(8,128)(2,1)S(1)} %add_convert_fusion.2.p_own, bf16[128,512]{1,0:T(8,128)(2,1)S(1)} %collective-permute-done.11.p_second, bf16[128,512]{1,0:T(8,128)(2,1)S(1)} %collective-permute-done.12.p_first, bf16[128,512]{1,0:T(8,128)(2,1)S(1)} %collective-permute-done.13.p_both, ...), custom_call_target="tpu_custom_call" | custom-call | tf_op jit(solution)/shard_map/pallas_call | solution.py:128
  72.7 0.1 collective-permute-start.14
  72.7 0.0 collective-permute-done.8.other
  72.7 0.0 copy-done.2
  72.8 1.7 %shard_map.71 = (bf16[128,1024]{1,0:T(8,128)(2,1)S(1)}, bf16[2,3,512,512]{3,2,1,0:T(8,128)(2,1)}) custom-call(bf16[128,1024]{1,0:T(8,128)(2,1)S(1)} %copy-done.2, bf16[2,512,512]{2,1,0:T(8,128)(2,1)S(1)} %shard_map.70.own, bf16[2,512,512]{2,1,0:T(8,128)(2,1)S(1)} %collective-permute-done.8.other), custom_call_target="tpu_custom_call" | custom-call | tf_op jit(solution)/shard_map/pallas_call | solution.py:233
  74.4 0.2 collective-permute-done.14.other
  74.6 1.8 %shard_map.73 = (bf16[128,1024]{1,0:T(8,128)(2,1)}, bf16[2,3,512,512]{3,2,1,0:T(8,128)(2,1)}) custom-call(bf16[128,1024]{1,0:T(8,128)(2,1)S(1)} %get-tuple-element.14.hidden, bf16[1,512,512]{2,1,0:T(8,128)(2,1)S(1)} %shard_map.72.own, bf16[1,512,512]{2,1,0:T(8,128)(2,1)S(1)} %collective-permute-done.14.other, ...), custom_call_target="tpu_custom_call", output_to_operand_aliasing={{1}: (3, {})} | custom-call | tf_op jit(solution)/shard_map/pallas_call | solution.py:246
  (4 shorter events, 0.1 us)
Async XLA Ops:
  0.6 1.0 %copy-start.3 = (bf16[128,1024]{1,0:T(8,128)(2,1)S(1)}, bf16[128,1024]{1,0:T(8,128)(2,1)}, u32[]{:S(2)}) copy-start(bf16[128,1024]{1,0:T(8,128)(2,1)} %keys.1) | copy-start | bytes 786436
  1.6 0.9 %copy-start.4 = (bf16[128,1024]{1,0:T(8,128)(2,1)S(1)}, bf16[128,1024]{1,0:T(8,128)(2,1)}, u32[]{:S(2)}) copy-start(bf16[128,1024]{1,0:T(8,128)(2,1)} %values.1) | copy-start | bytes 786436
  2.5 0.7 copy-start.5
  3.4 9.2 %collective-permute-start.1 = (bf16[2,128,512]{2,1,0:T(8,128)(2,1)S(1)}, bf16[2,128,512]{2,1,0:T(8,128)(2,1)S(1)}, u32[]{:S(2)}, u32[]{:S(2)}) collective-permute-start(bf16[2,128,512]{2,1,0:T(8,128)(2,1)S(1)} %get-tuple-element.10.t0), channel_id=1, source_target_pairs={{0,2},{1,5},{2,0},{3,7},{4,6},{5,1},{6,4},{7,3},{8,10},{9,13},{10,... | collective-permute-start | bytes 786440 | tf_op jit(solution)/shard_map/ppermute | solution.py:185
  6.4 7.2 %collective-permute-start.2 = (bf16[2,128,512]{2,1,0:T(8,128)(2,1)S(1)}, bf16[2,128,512]{2,1,0:T(8,128)(2,1)S(1)}, u32[]{:S(2)}, u32[]{:S(2)}) collective-permute-start(bf16[2,128,512]{2,1,0:T(8,128)(2,1)S(1)} %get-tuple-element.11), channel_id=1, source_target_pairs={{0,5},{1,2},{2,7},{3,0},{4,1},{5,6},{6,3},{7,4},{8,13},{9,10},{10,... | collective-permute-start | bytes 786440 | tf_op jit(solution)/shard_map/ppermute | solution.py:185
  6.4 7.2 %collective-permute-start = (bf16[2,128,512]{2,1,0:T(8,128)(2,1)S(1)}, bf16[2,128,512]{2,1,0:T(8,128)(2,1)S(1)}, u32[]{:S(2)}, u32[]{:S(2)}) collective-permute-start(bf16[2,128,512]{2,1,0:T(8,128)(2,1)S(1)} %get-tuple-element.11), channel_id=1, source_target_pairs={{0,1},{1,0},{2,3},{3,2},{4,5},{5,4},{6,7},{7,6},{8,9},{9,8},{10,11... | collective-permute-start | bytes 786440 | tf_op jit(solution)/shard_map/ppermute | solution.py:185
  13.6 1.9 %copy-start = (bf16[2,3,512,512]{3,2,1,0:T(8,128)(2,1)S(1)}, bf16[2,3,512,512]{3,2,1,0:T(8,128)(2,1)}, u32[]{:S(2)}) copy-start(bf16[2,3,512,512]{3,2,1,0:T(8,128)(2,1)} %weights.5) | copy-start | bytes 9437188
  15.5 37.9 %copy-start.1 = (bf16[2,3,512,512]{3,2,1,0:T(8,128)(2,1)S(1)}, bf16[2,3,512,512]{3,2,1,0:T(8,128)(2,1)}, u32[]{:S(2)}) copy-start(bf16[2,3,512,512]{3,2,1,0:T(8,128)(2,1)} %weights.5) | copy-start | bytes 9437188
  17.9 6.5 %collective-permute-start.3 = (bf16[2,512,128]{2,1,0:T(8,128)(2,1)S(1)}, bf16[2,512,128]{2,1,0:T(8,128)(2,1)S(1)}, u32[]{:S(2)}, u32[]{:S(2)}) collective-permute-start(bf16[2,512,128]{2,1,0:T(8,128)(2,1)S(1)} %get-tuple-element.13), channel_id=1, source_target_pairs={{0,4},{1,3},{2,6},{3,1},{4,0},{5,7},{6,2},{7,5},{8,12},{9,11},{10,... | collective-permute-start | bytes 786440 | tf_op jit(solution)/shard_map/ppermute | solution.py:185
  24.4 13.4 %collective-permute-start.4 = (bf16[2,512,128]{2,1,0:T(8,128)(2,1)S(1)}, bf16[2,512,128]{2,1,0:T(8,128)(2,1)S(1)}, u32[]{:S(2)}, u32[]{:S(2)}) collective-permute-start(bf16[2,512,128]{2,1,0:T(8,128)(2,1)S(1)} %add_convert_fusion.1), channel_id=1, source_target_pairs={{0,8},{1,9},{2,10},{3,11},{4,12},{5,13},{6,14},{7,15},{8,0},{9,1},... | collective-permute-start | bytes 786440 | tf_op jit(solution)/shard_map/ppermute | solution.py:185
  37.9 9.2 %collective-permute-start.5 = (bf16[2,512,128]{2,1,0:T(8,128)(2,1)S(1)}, bf16[2,512,128]{2,1,0:T(8,128)(2,1)S(1)}, u32[]{:S(2)}, u32[]{:S(2)}) collective-permute-start(bf16[2,512,128]{2,1,0:T(8,128)(2,1)S(1)} %add_convert_fusion.p_own), channel_id=1, source_target_pairs={{0,4},{1,3},{2,6},{3,1},{4,0},{5,7},{6,2},{7,5},{8,12},{9,11},{10,... | collective-permute-start | bytes 786440 | tf_op jit(solution)/shard_map/ppermute | solution.py:185
  38.6 12.6 %collective-permute-start.9 = (bf16[128,512]{1,0:T(8,128)(2,1)S(1)}, bf16[128,512]{1,0:T(8,128)(2,1)S(1)}, u32[]{:S(2)}, u32[]{:S(2)}) collective-permute-start(bf16[128,512]{1,0:T(8,128)(2,1)S(1)} %get-tuple-element.16), channel_id=1, source_target_pairs={{0,4},{1,3},{2,6},{3,1},{4,0},{5,7},{6,2},{7,5},{8,12},{9,11},{10,... | collective-permute-start | bytes 393224 | tf_op jit(solution)/shard_map/ppermute | solution.py:185
  40.0 11.4 %collective-permute-start.6 = (bf16[2,512,128]{2,1,0:T(8,128)(2,1)S(1)}, bf16[2,512,128]{2,1,0:T(8,128)(2,1)S(1)}, u32[]{:S(2)}, u32[]{:S(2)}) collective-permute-start(bf16[2,512,128]{2,1,0:T(8,128)(2,1)S(1)} %add_convert_fusion.p_own), channel_id=1, source_target_pairs={{0,2},{1,5},{2,0},{3,7},{4,6},{5,1},{6,4},{7,3},{8,10},{9,13},{10,... | collective-permute-start | bytes 786440 | tf_op jit(solution)/shard_map/ppermute | solution.py:185
  47.0 6.4 %collective-permute-start.7 = (bf16[2,512,128]{2,1,0:T(8,128)(2,1)S(1)}, bf16[2,512,128]{2,1,0:T(8,128)(2,1)S(1)}, u32[]{:S(2)}, u32[]{:S(2)}) collective-permute-start(bf16[2,512,128]{2,1,0:T(8,128)(2,1)S(1)} %collective-permute-done.5.p_second), channel_id=1, source_target_pairs={{0,2},{1,5},{2,0},{3,7},{4,6},{5,1},{6,4},{7,3},{8,10},{9,13},{10,... | collective-permute-start | bytes 786440 | tf_op jit(solution)/shard_map/ppermute | solution.py:185
  51.3 7.6 %collective-permute-start.10 = (bf16[128,512]{1,0:T(8,128)(2,1)S(1)}, bf16[128,512]{1,0:T(8,128)(2,1)S(1)}, u32[]{:S(2)}, u32[]{:S(2)}) collective-permute-start(bf16[128,512]{1,0:T(8,128)(2,1)S(1)} %add_convert_fusion.3), channel_id=1, source_target_pairs={{0,8},{1,9},{2,10},{3,11},{4,12},{5,13},{6,14},{7,15},{8,0},{9,1},... | collective-permute-start | bytes 393224 | tf_op jit(solution)/shard_map/ppermute | solution.py:185
  58.8 13.9 %copy-start.2 = (bf16[128,1024]{1,0:T(8,128)(2,1)S(1)}, bf16[128,1024]{1,0:T(8,128)(2,1)}, u32[]{:S(2)}) copy-start(bf16[128,1024]{1,0:T(8,128)(2,1)} %queries.1) | copy-start | bytes 786436
  58.8 13.9 %collective-permute-start.8 = (bf16[2,512,512]{2,1,0:T(8,128)(2,1)S(1)}, bf16[2,512,512]{2,1,0:T(8,128)(2,1)S(1)}, u32[]{:S(2)}, u32[]{:S(2)}) collective-permute-start(bf16[2,512,512]{2,1,0:T(8,128)(2,1)S(1)} %shard_map.70.own), channel_id=1, source_target_pairs={{0,1},{1,0},{2,3},{3,2},{4,5},{5,4},{6,7},{7,6},{8,9},{9,8},{10,11... | collective-permute-start | bytes 3145736 | tf_op jit(solution)/shard_map/ppermute | solution.py:185
  59.0 5.7 %collective-permute-start.11 = (bf16[128,512]{1,0:T(8,128)(2,1)S(1)}, bf16[128,512]{1,0:T(8,128)(2,1)S(1)}, u32[]{:S(2)}, u32[]{:S(2)}) collective-permute-start(bf16[128,512]{1,0:T(8,128)(2,1)S(1)} %add_convert_fusion.2.p_own), channel_id=1, source_target_pairs={{0,4},{1,3},{2,6},{3,1},{4,0},{5,7},{6,2},{7,5},{8,12},{9,11},{10,... | collective-permute-start | bytes 393224 | tf_op jit(solution)/shard_map/ppermute | solution.py:185
  59.4 7.3 %collective-permute-start.12 = (bf16[128,512]{1,0:T(8,128)(2,1)S(1)}, bf16[128,512]{1,0:T(8,128)(2,1)S(1)}, u32[]{:S(2)}, u32[]{:S(2)}) collective-permute-start(bf16[128,512]{1,0:T(8,128)(2,1)S(1)} %add_convert_fusion.2.p_own), channel_id=1, source_target_pairs={{0,2},{1,5},{2,0},{3,7},{4,6},{5,1},{6,4},{7,3},{8,10},{9,13},{10,... | collective-permute-start | bytes 393224 | tf_op jit(solution)/shard_map/ppermute | solution.py:185
  64.7 5.0 %collective-permute-start.13 = (bf16[128,512]{1,0:T(8,128)(2,1)S(1)}, bf16[128,512]{1,0:T(8,128)(2,1)S(1)}, u32[]{:S(2)}, u32[]{:S(2)}) collective-permute-start(bf16[128,512]{1,0:T(8,128)(2,1)S(1)} %collective-permute-done.11.p_second), channel_id=1, source_target_pairs={{0,2},{1,5},{2,0},{3,7},{4,6},{5,1},{6,4},{7,3},{8,10},{9,13},{10,... | collective-permute-start | bytes 393224 | tf_op jit(solution)/shard_map/ppermute | solution.py:185
  72.7 2.0 %collective-permute-start.14 = (bf16[1,512,512]{2,1,0:T(8,128)(2,1)S(1)}, bf16[1,512,512]{2,1,0:T(8,128)(2,1)S(1)}, u32[]{:S(2)}, u32[]{:S(2)}) collective-permute-start(bf16[1,512,512]{2,1,0:T(8,128)(2,1)S(1)} %shard_map.72.own), channel_id=1, source_target_pairs={{0,1},{1,0},{2,3},{3,2},{4,5},{5,4},{6,7},{7,6},{8,9},{9,8},{10,11... | collective-permute-start | bytes 1572872 | tf_op jit(solution)/shard_map/ppermute | solution.py:185

commit v2 on v1

v2 whole, which is shorter than its diff:
```python
import functools

import jax
import jax.numpy as jnp
from jax import lax
from jax.experimental import pallas as pl
from jax.experimental.pallas import tpu as pltpu
from jax.sharding import PartitionSpec as P

NS_STEPS = 2
F32 = jnp.float32
BF16 = jnp.bfloat16
VMEM_SPEC = pl.BlockSpec(memory_space=pltpu.VMEM)
ANY_SPEC = pl.BlockSpec(memory_space=pl.ANY)
PARAMS = pltpu.CompilerParams(vmem_limit_bytes=40 * 1024 * 1024)
WHOLE_VMEM = pltpu.CompilerParams(vmem_limit_bytes=62 * 1024 * 1024)


def place():
    me = lax.axis_index("tok")
    core = me % 2
    bit1 = (me // 2) % 2
    bit2 = (me // 4) % 2
    half = jnp.where(core == 0, bit1, bit2)
    quarter = jnp.where(core == 0, bit2, bit1)
    return core, half, quarter


def dot(a, b, ca=1, cb=0):
    return lax.dot_general(a, b, (((ca,), (cb,)), ((), ())), preferred_element_type=F32)


def span(at, size):
    return pl.ds(pl.multiple_of(at * size, size), size)


def pack_kernel(keys, values, rates, own, other, held, rate, sems):
    tokens, width = own.shape[1:]
    core, _, _ = place()
    copies = [
        pltpu.make_async_copy(values, held, sems.at[0]),
        pltpu.make_async_copy(rates, rate, sems.at[1]),
    ]
    for at, (head, out) in enumerate(((core, own), (1 - core, other))):
        copies.append(pltpu.make_async_copy(keys.at[:, span(head, width)], out.at[0], sems.at[2 + at]))
    for copy in copies:
        copy.start()
    for copy in copies:
        copy.wait()
    for head, out in ((core, own), (1 - core, other)):
        row = jnp.where(head == 0, rate[0:1, :], rate[1:2, :])
        column = jnp.broadcast_to(row, (tokens, tokens)).T[:, 0:1]
        out[1] = (-column * held[:, span(head, width)].astype(F32)).astype(BF16)


def token_grads(k, o, weights, cut):
    gate = dot(k, weights[0, :, cut])
    upper = dot(k, weights[1, :, cut])
    back = dot(o, weights[2, cut, :], 1, 1)
    sigma = jax.nn.sigmoid(gate)
    silu_gate = gate * sigma
    hidden = (silu_gate * upper).astype(BF16)
    d_gate = (back * upper * sigma * (1.0 + gate * (1.0 - sigma))).astype(BF16)
    d_upper = (back * silu_gate).astype(BF16)
    return dot(k, d_gate, 0, 0), dot(k, d_upper, 0, 0), dot(hidden, o, 0, 0)


def cuts(width):
    _, half, quarter = place()
    return span(2 * half + 1 - quarter, width // 4), span(2 * half + quarter, width // 4)


def near_kernel(t0, t1, weights, send, keep, mine, keys, outer, sem):
    tokens, width = t0.shape[1:]
    piece = width // 4
    core, _, _ = place()
    copy = pltpu.make_async_copy(weights.at[core], mine, sem)
    copy.start()
    for at, src in enumerate((t0, t1)):
        keys[at * tokens : (at + 1) * tokens, :] = src[0]
        outer[at * tokens : (at + 1) * tokens, :] = src[1]
    copy.wait()
    for out, cut in zip((send, keep), cuts(width)):
        gate, upper, down = token_grads(keys[...], outer[...], mine, cut)
        out[0] = gate
        out[1] = upper
        for at in range(width // piece):
            out[2, at * piece : (at + 1) * piece, :] = down[:, at * piece : (at + 1) * piece]


def far_kernel(t2, t3, mine, near_send, near_keep, *refs):
    outs, (keys, outer) = refs[:6], refs[6:]
    tokens, width = t2.shape[1:]
    piece = width // 4
    for at, src in enumerate((t2, t3)):
        keys[at * tokens : (at + 1) * tokens, :] = src[0]
        outer[at * tokens : (at + 1) * tokens, :] = src[1]
    for out, near, cut in zip((outs[:3], outs[3:]), (near_send, near_keep), cuts(width)):
        gate, upper, down = token_grads(keys[...], outer[...], mine, cut)
        out[0][...] = (near[0] + gate).astype(out[0].dtype)
        out[1][...] = (near[1] + upper).astype(out[1].dtype)
        for at in range(width // piece):
            rows = slice(at * piece, (at + 1) * piece)
            out[2][rows, :] = (near[2, rows, :] + down[:, rows]).astype(out[2].dtype)


def newton_schulz(matrix):
    wide = matrix.astype(F32)
    norm = jnp.sqrt(jnp.sum(wide * wide)) + 1e-07
    iterate = (wide / norm).astype(BF16)
    for _ in range(NS_STEPS):
        gram = dot(iterate, iterate, 1, 1).astype(BF16)
        mixed = (-4.775 * gram.astype(F32) + 2.0315 * dot(gram, gram)).astype(BF16)
        iterate = (3.4445 * iterate.astype(F32) + dot(mixed, iterate)).astype(BF16)
    return iterate


def renormed(old, update):
    old = old.astype(F32)
    fresh = old - update.astype(F32)
    scale = jnp.sqrt(
        (jnp.mean(old * old, axis=1, keepdims=True) + 1e-06)
        / (jnp.mean(fresh * fresh, axis=1, keepdims=True) + 1e-06)
    )
    return (fresh * scale).astype(BF16)


def ns_kernel(which, earlier, mine, *refs):
    count = len(which)
    pieces, (total, sems) = refs[: 4 * count], refs[-2:]
    if earlier:
        before, new, new_weights = refs[4 * count : -2]
    else:
        new = refs[4 * count]
    _, width, _ = new.shape
    size = width // 4
    core, half, quarter = place()
    places = ((half, quarter), (half, 1 - quarter), (1 - half, quarter), (1 - half, 1 - quarter))
    for at, matrix in enumerate(which):
        for (h, q), piece in zip(places, pieces[4 * at : 4 * at + 4]):
            cut = span(2 * h + q, size)
            if matrix < 2:
                total[at, :, cut] = piece[...]
            else:
                for block in range(width // size):
                    rows = slice(block * size, (block + 1) * size)
                    total[at, cut, rows] = piece[rows, :]
    copies = []
    if earlier:
        for at, matrix in enumerate(earlier):
            copy = pltpu.make_async_copy(before.at[at], new_weights.at[core, matrix], sems.at[at])
            copy.start()
            copies.append(copy)
    updates = [newton_schulz(total[at]) for at in range(count)]
    for at, matrix in enumerate(which):
        new[at] = renormed(mine[matrix], updates[at])
    for copy in copies:
        copy.wait()


def updated(which, pieces, mine, earlier=(), before=None):
    heads, width = 2, mine.shape[2]
    count = len(which)
    flat = [piece for four in pieces for piece in four]
    out = [jax.ShapeDtypeStruct((count, width, width), BF16)]
    if earlier:
        flat.append(before)
        out.append(jax.ShapeDtypeStruct((heads, *mine.shape), BF16))
    return pl.pallas_call(
        functools.partial(ns_kernel, which, earlier),
        out_shape=out,
        in_specs=[VMEM_SPEC] * (len(flat) + 1),
        out_specs=[VMEM_SPEC, ANY_SPEC][: len(out)],
        scratch_shapes=[
            pltpu.VMEM((count, width, width), BF16),
            pltpu.SemaphoreType.DMA((max(1, len(earlier)),)),
        ],
        compiler_params=PARAMS,
    )(mine, *flat)


def gate_up_kernel(queries, own, other, own_down, held, hidden, new_weights, sems):
    width = own.shape[2]
    core, _, _ = place()
    copies = [
        pltpu.make_async_copy(other, new_weights.at[1 - core, pl.ds(0, 2)], sems.at[0]),
        pltpu.make_async_copy(own_down, new_weights.at[core, pl.ds(2, 1)], sems.at[1]),
    ]
    for copy in copies:
        copy.start()
    for head, part in ((core, own), (1 - core, other)):
        cols = span(head, width)
        gate = dot(queries[:, cols], part[0])
        upper = dot(queries[:, cols], part[1])
        hidden[:, cols] = (gate * jax.nn.sigmoid(gate) * upper).astype(BF16)
    for copy in copies:
        copy.wait()


def down_kernel(hidden, own, other, held, readout, new_weights, sems):
    width = own.shape[2]
    core, _, _ = place()
    copy = pltpu.make_async_copy(other, new_weights.at[1 - core, pl.ds(2, 1)], sems.at[0])
    copy.start()
    for head, part in ((core, own), (1 - core, other)):
        cols = span(head, width)
        readout[:, cols] = dot(hidden[:, cols], part[0]).astype(BF16)
    copy.wait()


def body(size, keys, values, queries, rates, fast_weights):
    tokens = keys.shape[0]
    heads, _, width, _ = fast_weights.shape
    quarter = width // 4
    sibling = [(i, i ^ 1) for i in range(size)]
    first = [(i, i ^ (2 if i % 2 == 0 else 4)) for i in range(size)]
    second = [(i, i ^ (4 if i % 2 == 0 else 2)) for i in range(size)]
    across = [(i, i ^ 1 ^ (4 if i % 2 == 0 else 2)) for i in range(size)]
    rest = [[(i, i ^ (1 << bit)) for i in range(size)] for bit in range(3, size.bit_length() - 1)]

    def move(value, pairs):
        return lax.ppermute(value, "tok", pairs)

    def tie(*values):
        return lax.optimization_barrier(values)

    pair = jax.ShapeDtypeStruct((2, tokens, width), BF16)
    own, other = pl.pallas_call(
        pack_kernel,
        out_shape=(pair, pair),
        in_specs=[ANY_SPEC] * 3,
        out_specs=(VMEM_SPEC, VMEM_SPEC),
        scratch_shapes=[
            pltpu.VMEM(values.shape, BF16),
            pltpu.VMEM(rates.shape, F32),
            pltpu.SemaphoreType.DMA((4,)),
        ],
        compiler_params=WHOLE_VMEM,
    )(keys, values, rates)
    part16 = jax.ShapeDtypeStruct((width, quarter), BF16)
    part32 = jax.ShapeDtypeStruct((width, quarter), F32)
    three32 = jax.ShapeDtypeStruct((3, width, quarter), F32)
    rows_scratch = [pltpu.VMEM((2 * tokens, width), BF16)] * 2
    near_send, near_keep, mine = pl.pallas_call(
        near_kernel,
        out_shape=(three32, three32, jax.ShapeDtypeStruct((3, width, width), BF16)),
        in_specs=[VMEM_SPEC] * 2 + [ANY_SPEC],
        out_specs=(VMEM_SPEC,) * 3,
        scratch_shapes=rows_scratch + [pltpu.SemaphoreType.DMA],
        compiler_params=PARAMS,
    )(own, move(other, sibling), fast_weights)
    outs = pl.pallas_call(
        far_kernel,
        out_shape=(part16,) * 3 + (part32,) * 3,
        in_specs=[VMEM_SPEC] * 5,
        out_specs=(VMEM_SPEC,) * 6,
        scratch_shapes=rows_scratch,
        compiler_params=PARAMS,
    )(move(own, first), move(other, across), mine, near_send, near_keep)
    send, keep = outs[:3], outs[3:]

    def reduced(at):
        return (keep[at] + move(send[at], second).astype(F32)).astype(BF16)

    def crossed(part):
        for pairs in rest:
            part = (part.astype(F32) + move(part, pairs).astype(F32)).astype(BF16)
        return part

    def pieces(part):
        over = move(part, second)
        return part, over, move(part, first), move(over, first)

    four = [pieces(crossed(reduced(at))) for at in range(3)]
    flat = tie(*four[0], *four[1], *four[2])
    (new_a,) = updated((0, 1), (flat[0:4], flat[4:8]), mine)
    new_d, new_weights = updated((2,), (flat[8:12],), mine, (0, 1), new_a)
    hidden, new_weights = pl.pallas_call(
        gate_up_kernel,
        out_shape=(
            jax.ShapeDtypeStruct(queries.shape, BF16),
            jax.ShapeDtypeStruct(fast_weights.shape, BF16),
        ),
        in_specs=[VMEM_SPEC] * 4 + [ANY_SPEC],
        out_specs=(VMEM_SPEC, ANY_SPEC),
        scratch_shapes=[pltpu.SemaphoreType.DMA((2,))],
        input_output_aliases={4: 1},
        compiler_params=PARAMS,
    )(queries, new_a, move(new_a, sibling), new_d, new_weights)


    return pl.pallas_call(
        down_kernel,
        out_shape=(
            jax.ShapeDtypeStruct(queries.shape, BF16),
            jax.ShapeDtypeStruct(fast_weights.shape, BF16),
        ),
        in_specs=[VMEM_SPEC] * 3 + [ANY_SPEC],
        out_specs=(VMEM_SPEC, ANY_SPEC),
        scratch_shapes=[pltpu.SemaphoreType.DMA((1,))],
        input_output_aliases={3: 1},
        compiler_params=PARAMS,
    )(hidden, new_d, move(new_d, sibling), new_weights)


def solution(mesh):
    return jax.shard_map(
        functools.partial(body, mesh.shape["tok"]),
        mesh=mesh,
        in_specs=(
            P(("grp", "tok"), None),
            P(("grp", "tok"), None),
            P(("grp", "tok"), None),
            P(None, ("grp", "tok")),
            P(),
        ),
        out_specs=(P(("grp", "tok"), None), P("grp", None, None, None)),
        check_vma=False,
    )
```

time: 76.7 us -> 64.5 us (0.84)
  waiting for transfers between devices: 39 us -> 18.6 us
  starting transfers between devices: 17.6 us -> 25.9 us
  local copies, waits for them, and re-layouts: 4.47 us -> 2.85 us
  Pallas kernels: 14.4 us -> 16 us
    ppermute x15 -> x20, waiting for transfers between devices: 39 us -> 18.6 us  [move(): return lax.ppermute(value, 'tok', pairs)]
    ppermute x15 -> x20, starting transfers between devices: 17.6 us -> 25.9 us  [move(): return lax.ppermute(value, 'tok', pairs)]
    pallas_call x4 -> x5, Pallas kernels: 10.9 us -> 12.9 us  [the longest x2 7.87 us: updated(): pl.pallas_call(functools.partial(ns_kernel, which, earlier), out_shape=ou...]
    unnamed x12 -> x6, local copies, waits for them, and re-layouts: 4.47 us -> 2.85 us
  transfers between devices with their start and end apart: 15 -> 20, of which waited for: 10 -> 11; matrix products, arithmetic and copies ran while one was open for 0% -> 0% of each run, Pallas kernels for 13% -> 9%
where the time goes in v2:
time: 64.5 us; the launch traced here: 64.2 us
  starting transfers between devices  25.9 us (40%)
  waiting for transfers between devices  18.6 us (29%)
  Pallas kernels  16 us (25%)
  local copies, waits for them, and re-layouts  2.85 us (4%)
  between operations  0.74 us (1%)
    ppermute x20, starting transfers between devices, move(): return lax.ppermute(value, 'tok', pairs)  25.9 us
    ppermute x20, waiting for transfers between devices, move(): return lax.ppermute(value, 'tok', pairs)  18.6 us
    pallas_call x2, Pallas kernels, updated(): pl.pallas_call(functools.partial(ns_kernel, which, earlier), out_shape=ou...  7.87 us
    unnamed x6, local copies, waits for them, and re-layouts  2.85 us
    pallas_call x1, Pallas kernels, body(): pl.pallas_call(pack_kernel, out_shape=(pair, pair), in_specs=[ANY_SPEC] *...  2.06 us
    pallas_call x1, Pallas kernels, body(): pl.pallas_call(down_kernel, out_shape=(jax.ShapeDtypeStruct(queries.shape...  1.64 us
    pallas_call x1, Pallas kernels, body(): pl.pallas_call(near_kernel, out_shape=(three32, three32, jax.ShapeDtypeSt...  1.55 us
    pallas_call x1, Pallas kernels, body(): pl.pallas_call(gate_up_kernel, out_shape=(jax.ShapeDtypeStruct(queries.sh...  1.47 us
  transfers between devices with their start and end apart: 20, of which 11 were waited for; matrix products, arithmetic and copies ran while one was open for 0% of the time, Pallas kernels for 9%

profile of v2, /device:TPU:0, one launch (start us, length us, event | category | flops | bytes accessed | tf_op | source)
XLA Modules:
  0.0 64.2 jit_solution(11396531391154423171)
XLA Ops:
  0.6 2.1 %shard_map.68 = (bf16[2,128,512]{2,1,0:T(8,128)(2,1)}, bf16[2,128,512]{2,1,0:T(8,128)(2,1)}) custom-call(bf16[128,1024]{1,0:T(8,128)(2,1)} %keys.1, bf16[128,1024]{1,0:T(8,128)(2,1)} %values.1, f32[2,128]{1,0:T(2,128)} %rates.1), custom_call_target="tpu_custom_call" | custom-call | tf_op jit(solution)/shard_map/pallas_call | solution.py:228
  2.7 0.5 collective-permute-start
  3.2 2.6 %collective-permute-start.1 = (bf16[2,128,512]{2,1,0:T(8,128)(2,1)}, bf16[2,128,512]{2,1,0:T(8,128)(2,1)S(1)}, u32[]{:S(2)}, u32[]{:S(2)}) collective-permute-start(bf16[2,128,512]{2,1,0:T(8,128)(2,1)} %get-tuple-element.29.t0), channel_id=1, source_target_pairs={{0,2},{1,5},{2,0},{3,7},{4,6},{5,1},{6,4},{7,3},{8,10},{9,13},{10,... | collective-permute-start | bytes 786440 | tf_op jit(solution)/shard_map/ppermute | solution.py:222
  5.8 0.1 collective-permute-start.2
  5.9 0.0 collective-permute-done.t1
  5.9 1.9 %copy-done = bf16[2,3,512,512]{3,2,1,0:T(8,128)(2,1)S(1)} copy-done((bf16[2,3,512,512]{3,2,1,0:T(8,128)(2,1)S(1)}, bf16[2,3,512,512]{3,2,1,0:T(8,128)(2,1)}, u32[]{:S(2)}) %copy-start) | copy-done | bytes 3145752
  7.8 0.9 %copy-done.1 = bf16[2,128,512]{2,1,0:T(8,128)(2,1)S(1)} copy-done((bf16[2,128,512]{2,1,0:T(8,128)(2,1)S(1)}, bf16[2,128,512]{2,1,0:T(8,128)(2,1)}, u32[]{:S(2)}) %copy-start.1) | copy-done | bytes 262168
  8.8 1.5 %shard_map.69 = (f32[3,512,128]{2,1,0:T(8,128)S(1)}, f32[3,512,128]{2,1,0:T(8,128)S(1)}, bf16[3,512,512]{2,1,0:T(8,128)(2,1)S(1)}) custom-call(bf16[2,128,512]{2,1,0:T(8,128)(2,1)S(1)} %copy-done.1, bf16[2,128,512]{2,1,0:T(8,128)(2,1)S(1)} %collective-permute-done.t1, bf16[2,3,512,512]{3,2,1,0:T(8,128)(2,1)S(1)} %copy-done), custom_call_target="tpu_custom_call" | custom-call | tf_op jit(solution)/shard_map/pallas_call | solution.py:244
  10.3 2.0 %collective-permute-done.1.t2 = bf16[2,128,512]{2,1,0:T(8,128)(2,1)S(1)} collective-permute-done((bf16[2,128,512]{2,1,0:T(8,128)(2,1)}, bf16[2,128,512]{2,1,0:T(8,128)(2,1)S(1)}, u32[]{:S(2)}, u32[]{:S(2)}) %collective-permute-start.1) | collective-permute-done | bytes 262176 | tf_op jit(solution)/shard_map/ppermute | solution.py:222
  12.3 0.8 %collective-permute-done.2.t3 = bf16[2,128,512]{2,1,0:T(8,128)(2,1)S(1)} collective-permute-done((bf16[2,128,512]{2,1,0:T(8,128)(2,1)}, bf16[2,128,512]{2,1,0:T(8,128)(2,1)S(1)}, u32[]{:S(2)}, u32[]{:S(2)}) %collective-permute-start.2) | collective-permute-done | bytes 262176 | tf_op jit(solution)/shard_map/ppermute | solution.py:222
  13.2 1.4 %shard_map.70 = (bf16[512,128]{1,0:T(8,128)(2,1)S(1)}, bf16[512,128]{1,0:T(8,128)(2,1)S(1)}, bf16[512,128]{1,0:T(8,128)(2,1)S(1)}, f32[512,128]{1,0:T(8,128)S(1)...) custom-call(bf16[2,128,512]{2,1,0:T(8,128)(2,1)S(1)} %collective-permute-done.1.t2, ...), custom_call_target="tpu_custom_call" | custom-call | tf_op jit(solution)/shard_map/pallas_call | solution.py:252
  14.6 2.1 %collective-permute-start.3 = (bf16[512,128]{1,0:T(8,128)(2,1)S(1)}, bf16[512,128]{1,0:T(8,128)(2,1)S(1)}, u32[]{:S(2)}, u32[]{:S(2)}) collective-permute-start(bf16[512,128]{1,0:T(8,128)(2,1)S(1)} %get-tuple-element.35), channel_id=1, source_target_pairs={{0,4},{1,3},{2,6},{3,1},{4,0},{5,7},{6,2},{7,5},{8,12},{9,11},{10,... | collective-permute-start | bytes 393224 | tf_op jit(solution)/shard_map/ppermute | solution.py:222
  16.7 0.1 collective-permute-start.8
  16.8 1.9 %collective-permute-start.13 = (bf16[512,128]{1,0:T(8,128)(2,1)S(1)}, bf16[512,128]{1,0:T(8,128)(2,1)S(1)}, u32[]{:S(2)}, u32[]{:S(2)}) collective-permute-start(bf16[512,128]{1,0:T(8,128)(2,1)S(1)} %get-tuple-element.39), channel_id=1, source_target_pairs={{0,4},{1,3},{2,6},{3,1},{4,0},{5,7},{6,2},{7,5},{8,12},{9,11},{10,... | collective-permute-start | bytes 393224 | tf_op jit(solution)/shard_map/ppermute | solution.py:222
  18.8 0.9 %collective-permute-done.3 = bf16[512,128]{1,0:T(8,128)(2,1)S(1)} collective-permute-done((bf16[512,128]{1,0:T(8,128)(2,1)S(1)}, bf16[512,128]{1,0:T(8,128)(2,1)S(1)}, u32[]{:S(2)}, u32[]{:S(2)}) %collective-permute-start.3) | collective-permute-done | bytes 131104 | tf_op jit(solution)/shard_map/ppermute | solution.py:222
  19.7 3.1 %collective-permute-start.4 = (bf16[512,128]{1,0:T(8,128)(2,1)S(1)}, bf16[512,128]{1,0:T(8,128)(2,1)S(1)}, u32[]{:S(2)}, u32[]{:S(2)}) collective-permute-start(bf16[512,128]{1,0:T(8,128)(2,1)S(1)} %add_convert_fusion.5), channel_id=1, source_target_pairs={{0,8},{1,9},{2,10},{3,11},{4,12},{5,13},{6,14},{7,15},{8,0},{9,1},... | collective-permute-start | bytes 393224 | tf_op jit(solution)/shard_map/ppermute | solution.py:222
  22.8 0.0 collective-permute-done.8
  22.9 1.8 %collective-permute-start.9 = (bf16[512,128]{1,0:T(8,128)(2,1)S(1)}, bf16[512,128]{1,0:T(8,128)(2,1)S(1)}, u32[]{:S(2)}, u32[]{:S(2)}) collective-permute-start(bf16[512,128]{1,0:T(8,128)(2,1)S(1)} %add_convert_fusion.3), channel_id=1, source_target_pairs={{0,8},{1,9},{2,10},{3,11},{4,12},{5,13},{6,14},{7,15},{8,0},{9,1},... | collective-permute-start | bytes 393224 | tf_op jit(solution)/shard_map/ppermute | solution.py:222
  24.6 0.0 collective-permute-done.13
  24.7 2.7 %collective-permute-start.14 = (bf16[512,128]{1,0:T(8,128)(2,1)S(1)}, bf16[512,128]{1,0:T(8,128)(2,1)S(1)}, u32[]{:S(2)}, u32[]{:S(2)}) collective-permute-start(bf16[512,128]{1,0:T(8,128)(2,1)S(1)} %add_convert_fusion.1), channel_id=1, source_target_pairs={{0,8},{1,9},{2,10},{3,11},{4,12},{5,13},{6,14},{7,15},{8,0},{9,1},... | collective-permute-start | bytes 393224 | tf_op jit(solution)/shard_map/ppermute | solution.py:222
  27.5 7.5 %collective-permute-done.4 = bf16[512,128]{1,0:T(8,128)(2,1)S(1)} collective-permute-done((bf16[512,128]{1,0:T(8,128)(2,1)S(1)}, bf16[512,128]{1,0:T(8,128)(2,1)S(1)}, u32[]{:S(2)}, u32[]{:S(2)}) %collective-permute-start.4) | collective-permute-done | bytes 131104 | tf_op jit(solution)/shard_map/ppermute | solution.py:222
  34.9 1.5 %collective-permute-start.6 = (bf16[512,128]{1,0:T(8,128)(2,1)S(1)}, bf16[512,128]{1,0:T(8,128)(2,1)S(1)}, u32[]{:S(2)}, u32[]{:S(2)}) collective-permute-start(bf16[512,128]{1,0:T(8,128)(2,1)S(1)} %add_convert_fusion.4.refs_0_), channel_id=1, source_target_pairs={{0,2},{1,5},{2,0},{3,7},{4,6},{5,1},{6,4},{7,3},{8,10},{9,13},{10,... | collective-permute-start | bytes 393224 | tf_op jit(solution)/shard_map/ppermute | solution.py:222
  36.5 0.0 collective-permute-start.5
  36.5 1.3 %collective-permute-done.9 = bf16[512,128]{1,0:T(8,128)(2,1)S(1)} collective-permute-done((bf16[512,128]{1,0:T(8,128)(2,1)S(1)}, bf16[512,128]{1,0:T(8,128)(2,1)S(1)}, u32[]{:S(2)}, u32[]{:S(2)}) %collective-permute-start.9) | collective-permute-done | bytes 131104 | tf_op jit(solution)/shard_map/ppermute | solution.py:222
  37.9 0.8 %collective-permute-start.10 = (bf16[512,128]{1,0:T(8,128)(2,1)S(1)}, bf16[512,128]{1,0:T(8,128)(2,1)S(1)}, u32[]{:S(2)}, u32[]{:S(2)}) collective-permute-start(bf16[512,128]{1,0:T(8,128)(2,1)S(1)} %add_convert_fusion.2.refs_4_), channel_id=1, source_target_pairs={{0,4},{1,3},{2,6},{3,1},{4,0},{5,7},{6,2},{7,5},{8,12},{9,11},{10,... | collective-permute-start | bytes 393224 | tf_op jit(solution)/shard_map/ppermute | solution.py:222
  38.6 0.9 %collective-permute-done.14 = bf16[512,128]{1,0:T(8,128)(2,1)S(1)} collective-permute-done((bf16[512,128]{1,0:T(8,128)(2,1)S(1)}, bf16[512,128]{1,0:T(8,128)(2,1)S(1)}, u32[]{:S(2)}, u32[]{:S(2)}) %collective-permute-start.14) | collective-permute-done | bytes 131104 | tf_op jit(solution)/shard_map/ppermute | solution.py:222
  39.5 0.0 copy-start.2
  39.5 0.7 %collective-permute-start.15 = (bf16[512,128]{1,0:T(8,128)(2,1)S(1)}, bf16[512,128]{1,0:T(8,128)(2,1)S(1)}, u32[]{:S(2)}, u32[]{:S(2)}) collective-permute-start(bf16[512,128]{1,0:T(8,128)(2,1)S(1)} %add_convert_fusion.refs_0_), channel_id=1, source_target_pairs={{0,4},{1,3},{2,6},{3,1},{4,0},{5,7},{6,2},{7,5},{8,12},{9,11},{10,... | collective-permute-start | bytes 393224 | tf_op jit(solution)/shard_map/ppermute | solution.py:222
  40.2 1.5 %collective-permute-start.11 = (bf16[512,128]{1,0:T(8,128)(2,1)S(1)}, bf16[512,128]{1,0:T(8,128)(2,1)S(1)}, u32[]{:S(2)}, u32[]{:S(2)}) collective-permute-start(bf16[512,128]{1,0:T(8,128)(2,1)S(1)} %add_convert_fusion.2.refs_4_), channel_id=1, source_target_pairs={{0,2},{1,5},{2,0},{3,7},{4,6},{5,1},{6,4},{7,3},{8,10},{9,13},{10,... | collective-permute-start | bytes 393224 | tf_op jit(solution)/shard_map/ppermute | solution.py:222
  41.8 0.0 collective-permute-done.6.refs_2_
  41.8 0.8 %collective-permute-start.16 = (bf16[512,128]{1,0:T(8,128)(2,1)S(1)}, bf16[512,128]{1,0:T(8,128)(2,1)S(1)}, u32[]{:S(2)}, u32[]{:S(2)}) collective-permute-start(bf16[512,128]{1,0:T(8,128)(2,1)S(1)} %add_convert_fusion.refs_0_), channel_id=1, source_target_pairs={{0,2},{1,5},{2,0},{3,7},{4,6},{5,1},{6,4},{7,3},{8,10},{9,13},{10,... | collective-permute-start | bytes 393224 | tf_op jit(solution)/shard_map/ppermute | solution.py:222
  42.6 0.0 collective-permute-done.5.refs_1_
  42.6 1.2 %collective-permute-start.7 = (bf16[512,128]{1,0:T(8,128)(2,1)S(1)}, bf16[512,128]{1,0:T(8,128)(2,1)S(1)}, u32[]{:S(2)}, u32[]{:S(2)}) collective-permute-start(bf16[512,128]{1,0:T(8,128)(2,1)S(1)} %collective-permute-done.5.refs_1_), channel_id=1, source_target_pairs={{0,2},{1,5},{2,0},{3,7},{4,6},{5,1},{6,4},{7,3},{8,10},{9,13},{10,... | collective-permute-start | bytes 393224 | tf_op jit(solution)/shard_map/ppermute | solution.py:222
  43.8 1.0 %collective-permute-done.10.refs_5_ = bf16[512,128]{1,0:T(8,128)(2,1)S(1)} collective-permute-done((bf16[512,128]{1,0:T(8,128)(2,1)S(1)}, bf16[512,128]{1,0:T(8,128)(2,1)S(1)}, u32[]{:S(2)}, u32[]{:S(2)}) %collective-permute-start.10) | collective-permute-done | bytes 131104 | tf_op jit(solution)/shard_map/ppermute | solution.py:222
  44.8 1.8 %collective-permute-start.12 = (bf16[512,128]{1,0:T(8,128)(2,1)S(1)}, bf16[512,128]{1,0:T(8,128)(2,1)S(1)}, u32[]{:S(2)}, u32[]{:S(2)}) collective-permute-start(bf16[512,128]{1,0:T(8,128)(2,1)S(1)} %collective-permute-done.10.refs_5_), channel_id=1, source_target_pairs={{0,2},{1,5},{2,0},{3,7},{4,6},{5,1},{6,4},{7,3},{8,10},{9,13},{10,... | collective-permute-start | bytes 393224 | tf_op jit(solution)/shard_map/ppermute | solution.py:222
  46.6 1.0 %collective-permute-done.15.refs_1_ = bf16[512,128]{1,0:T(8,128)(2,1)S(1)} collective-permute-done((bf16[512,128]{1,0:T(8,128)(2,1)S(1)}, bf16[512,128]{1,0:T(8,128)(2,1)S(1)}, u32[]{:S(2)}, u32[]{:S(2)}) %collective-permute-start.15) | collective-permute-done | bytes 131104 | tf_op jit(solution)/shard_map/ppermute | solution.py:222
  47.6 1.8 %collective-permute-start.17 = (bf16[512,128]{1,0:T(8,128)(2,1)S(1)}, bf16[512,128]{1,0:T(8,128)(2,1)S(1)}, u32[]{:S(2)}, u32[]{:S(2)}) collective-permute-start(bf16[512,128]{1,0:T(8,128)(2,1)S(1)} %collective-permute-done.15.refs_1_), channel_id=1, source_target_pairs={{0,2},{1,5},{2,0},{3,7},{4,6},{5,1},{6,4},{7,3},{8,10},{9,13},{10,... | collective-permute-start | bytes 393224 | tf_op jit(solution)/shard_map/ppermute | solution.py:222
  49.4 0.0 collective-permute-done.11.refs_6_
  49.4 0.3 collective-permute-done.12.refs_7_
  49.7 2.8 %collective-permute-done.17.refs_3_ = bf16[512,128]{1,0:T(8,128)(2,1)S(1)} collective-permute-done((bf16[512,128]{1,0:T(8,128)(2,1)S(1)}, bf16[512,128]{1,0:T(8,128)(2,1)S(1)}, u32[]{:S(2)}, u32[]{:S(2)}) %collective-permute-start.17) | collective-permute-done | bytes 131104 | tf_op jit(solution)/shard_map/ppermute | solution.py:222
  52.5 5.0 %shard_map.71.refs_4_.own = bf16[2,512,512]{2,1,0:T(8,128)(2,1)S(1)} custom-call(bf16[3,512,512]{2,1,0:T(8,128)(2,1)S(1)} %get-tuple-element.31.mine, bf16[512,128]{1,0:T(8,128)(2,1)S(1)} %add_convert_fusion.4.refs_0_, bf16[512,128]{1,0:T(8,128)(2,1)S(1)} %collective-permute-done.5.refs_1_, bf16[512,128]{1,0:T(8,128)(2,1)S(1)} %collective-permute-done.6.refs_2_, ...), custom_call_target="tpu_custom_call" | custom-call | tf_op jit(solution)/shard_map/pallas_call | solution.py:169
  57.6 0.1 collective-permute-start.18
  57.6 2.9 %shard_map.72 = (bf16[1,512,512]{2,1,0:T(8,128)(2,1)S(1)}, bf16[2,3,512,512]{3,2,1,0:T(8,128)(2,1)}) custom-call(bf16[3,512,512]{2,1,0:T(8,128)(2,1)S(1)} %get-tuple-element.31.mine, bf16[512,128]{1,0:T(8,128)(2,1)S(1)} %add_convert_fusion.refs_0_, bf16[512,128]{1,0:T(8,128)(2,1)S(1)} %collective-permute-done.15.refs_1_, ...), custom_call_target="tpu_custom_call" | custom-call | tf_op jit(solution)/shard_map/pallas_call | solution.py:169
  60.5 0.6 collective-permute-start.19
  61.1 0.0 collective-permute-done.18.other
  61.1 1.5 %shard_map.73 = (bf16[128,1024]{1,0:T(8,128)(2,1)S(1)}, bf16[2,3,512,512]{3,2,1,0:T(8,128)(2,1)}) custom-call(bf16[128,1024]{1,0:T(8,128)(2,1)S(1)} %copy-done.2, bf16[2,512,512]{2,1,0:T(8,128)(2,1)S(1)} %shard_map.71.refs_4_.own, bf16[2,512,512]{2,1,0:T(8,128)(2,1)S(1)} %collective-permute-done.18.other, ...), custom_call_target="tpu_custom_call", output_to_operand_aliasing={{1}: (4, {})} | custom-call | tf_op jit(solution)/shard_map/pallas_call | solution.py:278
  62.6 0.1 collective-permute-done.19.other
  62.6 1.6 %shard_map.74 = (bf16[128,1024]{1,0:T(8,128)(2,1)}, bf16[2,3,512,512]{3,2,1,0:T(8,128)(2,1)}) custom-call(bf16[128,1024]{1,0:T(8,128)(2,1)S(1)} %get-tuple-element.54.hidden, bf16[1,512,512]{2,1,0:T(8,128)(2,1)S(1)} %get-tuple-element.52.own_down.own, bf16[1,512,512]{2,1,0:T(8,128)(2,1)S(1)} %collective-permute-done.19.other, ...), custom_call_target="tpu_custom_call", output_to_operand_aliasing={{1}: (3, {})} | custom-call | tf_op jit(solution)/shard_map/pallas_call | solution.py:292
  (11 shorter events, 0.2 us)
Async XLA Ops:
  2.7 3.2 %collective-permute-start = (bf16[2,128,512]{2,1,0:T(8,128)(2,1)}, bf16[2,128,512]{2,1,0:T(8,128)(2,1)S(1)}, u32[]{:S(2)}, u32[]{:S(2)}) collective-permute-start(bf16[2,128,512]{2,1,0:T(8,128)(2,1)} %get-tuple-element.30), channel_id=1, source_target_pairs={{0,1},{1,0},{2,3},{3,2},{4,5},{5,4},{6,7},{7,6},{8,9},{9,8},{10,11... | collective-permute-start | bytes 786440 | tf_op jit(solution)/shard_map/ppermute | solution.py:222
  3.2 9.1 %collective-permute-start.1 = (bf16[2,128,512]{2,1,0:T(8,128)(2,1)}, bf16[2,128,512]{2,1,0:T(8,128)(2,1)S(1)}, u32[]{:S(2)}, u32[]{:S(2)}) collective-permute-start(bf16[2,128,512]{2,1,0:T(8,128)(2,1)} %get-tuple-element.29.t0), channel_id=1, source_target_pairs={{0,2},{1,5},{2,0},{3,7},{4,6},{5,1},{6,4},{7,3},{8,10},{9,13},{10,... | collective-permute-start | bytes 786440 | tf_op jit(solution)/shard_map/ppermute | solution.py:222
  5.8 7.4 %collective-permute-start.2 = (bf16[2,128,512]{2,1,0:T(8,128)(2,1)}, bf16[2,128,512]{2,1,0:T(8,128)(2,1)S(1)}, u32[]{:S(2)}, u32[]{:S(2)}) collective-permute-start(bf16[2,128,512]{2,1,0:T(8,128)(2,1)} %get-tuple-element.30), channel_id=1, source_target_pairs={{0,5},{1,2},{2,7},{3,0},{4,1},{5,6},{6,3},{7,4},{8,13},{9,10},{10,... | collective-permute-start | bytes 786440 | tf_op jit(solution)/shard_map/ppermute | solution.py:222
  5.9 1.9 %copy-start = (bf16[2,3,512,512]{3,2,1,0:T(8,128)(2,1)S(1)}, bf16[2,3,512,512]{3,2,1,0:T(8,128)(2,1)}, u32[]{:S(2)}) copy-start(bf16[2,3,512,512]{3,2,1,0:T(8,128)(2,1)} %weights.1) | copy-start | bytes 9437188
  7.8 0.9 %copy-start.1 = (bf16[2,128,512]{2,1,0:T(8,128)(2,1)S(1)}, bf16[2,128,512]{2,1,0:T(8,128)(2,1)}, u32[]{:S(2)}) copy-start(bf16[2,128,512]{2,1,0:T(8,128)(2,1)} %get-tuple-element.29.t0) | copy-start | bytes 786436
  14.6 5.1 %collective-permute-start.3 = (bf16[512,128]{1,0:T(8,128)(2,1)S(1)}, bf16[512,128]{1,0:T(8,128)(2,1)S(1)}, u32[]{:S(2)}, u32[]{:S(2)}) collective-permute-start(bf16[512,128]{1,0:T(8,128)(2,1)S(1)} %get-tuple-element.35), channel_id=1, source_target_pairs={{0,4},{1,3},{2,6},{3,1},{4,0},{5,7},{6,2},{7,5},{8,12},{9,11},{10,... | collective-permute-start | bytes 393224 | tf_op jit(solution)/shard_map/ppermute | solution.py:222
  16.7 6.1 %collective-permute-start.8 = (bf16[512,128]{1,0:T(8,128)(2,1)S(1)}, bf16[512,128]{1,0:T(8,128)(2,1)S(1)}, u32[]{:S(2)}, u32[]{:S(2)}) collective-permute-start(bf16[512,128]{1,0:T(8,128)(2,1)S(1)} %get-tuple-element.37), channel_id=1, source_target_pairs={{0,4},{1,3},{2,6},{3,1},{4,0},{5,7},{6,2},{7,5},{8,12},{9,11},{10,... | collective-permute-start | bytes 393224 | tf_op jit(solution)/shard_map/ppermute | solution.py:222
  16.8 7.9 %collective-permute-start.13 = (bf16[512,128]{1,0:T(8,128)(2,1)S(1)}, bf16[512,128]{1,0:T(8,128)(2,1)S(1)}, u32[]{:S(2)}, u32[]{:S(2)}) collective-permute-start(bf16[512,128]{1,0:T(8,128)(2,1)S(1)} %get-tuple-element.39), channel_id=1, source_target_pairs={{0,4},{1,3},{2,6},{3,1},{4,0},{5,7},{6,2},{7,5},{8,12},{9,11},{10,... | collective-permute-start | bytes 393224 | tf_op jit(solution)/shard_map/ppermute | solution.py:222
  19.7 15.2 %collective-permute-start.4 = (bf16[512,128]{1,0:T(8,128)(2,1)S(1)}, bf16[512,128]{1,0:T(8,128)(2,1)S(1)}, u32[]{:S(2)}, u32[]{:S(2)}) collective-permute-start(bf16[512,128]{1,0:T(8,128)(2,1)S(1)} %add_convert_fusion.5), channel_id=1, source_target_pairs={{0,8},{1,9},{2,10},{3,11},{4,12},{5,13},{6,14},{7,15},{8,0},{9,1},... | collective-permute-start | bytes 393224 | tf_op jit(solution)/shard_map/ppermute | solution.py:222
  22.9 15.0 %collective-permute-start.9 = (bf16[512,128]{1,0:T(8,128)(2,1)S(1)}, bf16[512,128]{1,0:T(8,128)(2,1)S(1)}, u32[]{:S(2)}, u32[]{:S(2)}) collective-permute-start(bf16[512,128]{1,0:T(8,128)(2,1)S(1)} %add_convert_fusion.3), channel_id=1, source_target_pairs={{0,8},{1,9},{2,10},{3,11},{4,12},{5,13},{6,14},{7,15},{8,0},{9,1},... | collective-permute-start | bytes 393224 | tf_op jit(solution)/shard_map/ppermute | solution.py:222
  24.7 14.8 %collective-permute-start.14 = (bf16[512,128]{1,0:T(8,128)(2,1)S(1)}, bf16[512,128]{1,0:T(8,128)(2,1)S(1)}, u32[]{:S(2)}, u32[]{:S(2)}) collective-permute-start(bf16[512,128]{1,0:T(8,128)(2,1)S(1)} %add_convert_fusion.1), channel_id=1, source_target_pairs={{0,8},{1,9},{2,10},{3,11},{4,12},{5,13},{6,14},{7,15},{8,0},{9,1},... | collective-permute-start | bytes 393224 | tf_op jit(solution)/shard_map/ppermute | solution.py:222
  34.9 6.8 %collective-permute-start.6 = (bf16[512,128]{1,0:T(8,128)(2,1)S(1)}, bf16[512,128]{1,0:T(8,128)(2,1)S(1)}, u32[]{:S(2)}, u32[]{:S(2)}) collective-permute-start(bf16[512,128]{1,0:T(8,128)(2,1)S(1)} %add_convert_fusion.4.refs_0_), channel_id=1, source_target_pairs={{0,2},{1,5},{2,0},{3,7},{4,6},{5,1},{6,4},{7,3},{8,10},{9,13},{10,... | collective-permute-start | bytes 393224 | tf_op jit(solution)/shard_map/ppermute | solution.py:222
  36.5 6.1 %collective-permute-start.5 = (bf16[512,128]{1,0:T(8,128)(2,1)S(1)}, bf16[512,128]{1,0:T(8,128)(2,1)S(1)}, u32[]{:S(2)}, u32[]{:S(2)}) collective-permute-start(bf16[512,128]{1,0:T(8,128)(2,1)S(1)} %add_convert_fusion.4.refs_0_), channel_id=1, source_target_pairs={{0,4},{1,3},{2,6},{3,1},{4,0},{5,7},{6,2},{7,5},{8,12},{9,11},{10,... | collective-permute-start | bytes 393224 | tf_op jit(solution)/shard_map/ppermute | solution.py:222
  37.9 6.9 %collective-permute-start.10 = (bf16[512,128]{1,0:T(8,128)(2,1)S(1)}, bf16[512,128]{1,0:T(8,128)(2,1)S(1)}, u32[]{:S(2)}, u32[]{:S(2)}) collective-permute-start(bf16[512,128]{1,0:T(8,128)(2,1)S(1)} %add_convert_fusion.2.refs_4_), channel_id=1, source_target_pairs={{0,4},{1,3},{2,6},{3,1},{4,0},{5,7},{6,2},{7,5},{8,12},{9,11},{10,... | collective-permute-start | bytes 393224 | tf_op jit(solution)/shard_map/ppermute | solution.py:222
  39.5 21.6 %copy-start.2 = (bf16[128,1024]{1,0:T(8,128)(2,1)S(1)}, bf16[128,1024]{1,0:T(8,128)(2,1)}, u32[]{:S(2)}) copy-start(bf16[128,1024]{1,0:T(8,128)(2,1)} %queries.1) | copy-start | bytes 786436
  39.5 8.0 %collective-permute-start.15 = (bf16[512,128]{1,0:T(8,128)(2,1)S(1)}, bf16[512,128]{1,0:T(8,128)(2,1)S(1)}, u32[]{:S(2)}, u32[]{:S(2)}) collective-permute-start(bf16[512,128]{1,0:T(8,128)(2,1)S(1)} %add_convert_fusion.refs_0_), channel_id=1, source_target_pairs={{0,4},{1,3},{2,6},{3,1},{4,0},{5,7},{6,2},{7,5},{8,12},{9,11},{10,... | collective-permute-start | bytes 393224 | tf_op jit(solution)/shard_map/ppermute | solution.py:222
  40.2 9.2 %collective-permute-start.11 = (bf16[512,128]{1,0:T(8,128)(2,1)S(1)}, bf16[512,128]{1,0:T(8,128)(2,1)S(1)}, u32[]{:S(2)}, u32[]{:S(2)}) collective-permute-start(bf16[512,128]{1,0:T(8,128)(2,1)S(1)} %add_convert_fusion.2.refs_4_), channel_id=1, source_target_pairs={{0,2},{1,5},{2,0},{3,7},{4,6},{5,1},{6,4},{7,3},{8,10},{9,13},{10,... | collective-permute-start | bytes 393224 | tf_op jit(solution)/shard_map/ppermute | solution.py:222
  41.8 7.6 %collective-permute-start.16 = (bf16[512,128]{1,0:T(8,128)(2,1)S(1)}, bf16[512,128]{1,0:T(8,128)(2,1)S(1)}, u32[]{:S(2)}, u32[]{:S(2)}) collective-permute-start(bf16[512,128]{1,0:T(8,128)(2,1)S(1)} %add_convert_fusion.refs_0_), channel_id=1, source_target_pairs={{0,2},{1,5},{2,0},{3,7},{4,6},{5,1},{6,4},{7,3},{8,10},{9,13},{10,... | collective-permute-start | bytes 393224 | tf_op jit(solution)/shard_map/ppermute | solution.py:222
  42.6 6.8 %collective-permute-start.7 = (bf16[512,128]{1,0:T(8,128)(2,1)S(1)}, bf16[512,128]{1,0:T(8,128)(2,1)S(1)}, u32[]{:S(2)}, u32[]{:S(2)}) collective-permute-start(bf16[512,128]{1,0:T(8,128)(2,1)S(1)} %collective-permute-done.5.refs_1_), channel_id=1, source_target_pairs={{0,2},{1,5},{2,0},{3,7},{4,6},{5,1},{6,4},{7,3},{8,10},{9,13},{10,... | collective-permute-start | bytes 393224 | tf_op jit(solution)/shard_map/ppermute | solution.py:222
  44.8 5.0 %collective-permute-start.12 = (bf16[512,128]{1,0:T(8,128)(2,1)S(1)}, bf16[512,128]{1,0:T(8,128)(2,1)S(1)}, u32[]{:S(2)}, u32[]{:S(2)}) collective-permute-start(bf16[512,128]{1,0:T(8,128)(2,1)S(1)} %collective-permute-done.10.refs_5_), channel_id=1, source_target_pairs={{0,2},{1,5},{2,0},{3,7},{4,6},{5,1},{6,4},{7,3},{8,10},{9,13},{10,... | collective-permute-start | bytes 393224 | tf_op jit(solution)/shard_map/ppermute | solution.py:222
  47.6 5.0 %collective-permute-start.17 = (bf16[512,128]{1,0:T(8,128)(2,1)S(1)}, bf16[512,128]{1,0:T(8,128)(2,1)S(1)}, u32[]{:S(2)}, u32[]{:S(2)}) collective-permute-start(bf16[512,128]{1,0:T(8,128)(2,1)S(1)} %collective-permute-done.15.refs_1_), channel_id=1, source_target_pairs={{0,2},{1,5},{2,0},{3,7},{4,6},{5,1},{6,4},{7,3},{8,10},{9,13},{10,... | collective-permute-start | bytes 393224 | tf_op jit(solution)/shard_map/ppermute | solution.py:222
  57.6 3.5 %collective-permute-start.18 = (bf16[2,512,512]{2,1,0:T(8,128)(2,1)S(1)}, bf16[2,512,512]{2,1,0:T(8,128)(2,1)S(1)}, u32[]{:S(2)}, u32[]{:S(2)}) collective-permute-start(bf16[2,512,512]{2,1,0:T(8,128)(2,1)S(1)} %shard_map.71.refs_4_.own), channel_id=1, source_target_pairs={{0,1},{1,0},{2,3},{3,2},{4,5},{5,4},{6,7},{7,6},{8,9},{9,8},{10,11... | collective-permute-start | bytes 3145736 | tf_op jit(solution)/shard_map/ppermute | solution.py:222
  60.5 2.1 %collective-permute-start.19 = (bf16[1,512,512]{2,1,0:T(8,128)(2,1)S(1)}, bf16[1,512,512]{2,1,0:T(8,128)(2,1)S(1)}, u32[]{:S(2)}, u32[]{:S(2)}) collective-permute-start(bf16[1,512,512]{2,1,0:T(8,128)(2,1)S(1)} %get-tuple-element.52.own_down.own), channel_id=1, source_target_pairs={{0,1},{1,0},{2,3},{3,2},{4,5},{5,4},{6,7},{7,6},{8,9},{9,8},{10,11... | collective-permute-start | bytes 1572872 | tf_op jit(solution)/shard_map/ppermute | solution.py:222

commit v3 on v2

--- a/solution.py
+++ b/solution.py
@@ -107,9 +107,13 @@
 def newton_schulz(matrix):
     wide = matrix.astype(F32)
     norm = jnp.sqrt(jnp.sum(wide * wide)) + 1e-07
-    iterate = (wide / norm).astype(BF16)
+    iterate = (wide * (1.0 / norm)).astype(BF16)
+    half = matrix.shape[0] // 2
     for _ in range(NS_STEPS):
-        gram = dot(iterate, iterate, 1, 1).astype(BF16)
+        upper = dot(iterate[:half], iterate, 1, 1).astype(BF16)
+        corner = dot(iterate[half:], iterate[half:], 1, 1).astype(BF16)
+        lower = jnp.concatenate([upper[:, half:].T, corner], axis=1)
+        gram = jnp.concatenate([upper, lower], axis=0)
         mixed = (-4.775 * gram.astype(F32) + 2.0315 * dot(gram, gram)).astype(BF16)
         iterate = (3.4445 * iterate.astype(F32) + dot(mixed, iterate)).astype(BF16)
     return iterate
@@ -129,7 +133,7 @@
     count = len(which)
     pieces, (total, sems) = refs[: 4 * count], refs[-2:]
     if earlier:
-        before, new, new_weights = refs[4 * count : -2]
+        before, new, new_weights = refs[4 * count], *refs[-4:-2]
     else:
         new = refs[4 * count]
     _, width, _ = new.shape
@@ -158,7 +162,7 @@
         copy.wait()
 
 
-def updated(which, pieces, mine, earlier=(), before=None):
+def updated(which, pieces, mine, earlier=(), before=None, held=None):
     heads, width = 2, mine.shape[2]
     count = len(which)
     flat = [piece for four in pieces for piece in four]
@@ -166,16 +170,24 @@
     if earlier:
         flat.append(before)
         out.append(jax.ShapeDtypeStruct((heads, *mine.shape), BF16))
+    specs = [VMEM_SPEC] * (len(flat) + 1)
+    if held is not None:
+        flat.append(held)
+        specs.append(ANY_SPEC)
     return pl.pallas_call(
         functools.partial(ns_kernel, which, earlier),
         out_shape=out,
-        in_specs=[VMEM_SPEC] * (len(flat) + 1),
+        in_specs=specs,
+        input_output_aliases={} if held is None else {len(flat): 1},
         out_specs=[VMEM_SPEC, ANY_SPEC][: len(out)],
         scratch_shapes=[
             pltpu.VMEM((count, width, width), BF16),
             pltpu.SemaphoreType.DMA((max(1, len(earlier)),)),
         ],
         compiler_params=PARAMS,
+        cost_estimate=pl.CostEstimate(
+            flops=120 * NS_STEPS * count * width**3, bytes_accessed=64 * count * width**2, transcendentals=0
+        ),
     )(mine, *flat)
 
 
@@ -271,10 +283,12 @@
         over = move(part, second)
         return part, over, move(part, first), move(over, first)
 
-    four = [pieces(crossed(reduced(at))) for at in range(3)]
-    flat = tie(*four[0], *four[1], *four[2])
-    (new_a,) = updated((0, 1), (flat[0:4], flat[4:8]), mine)
-    new_d, new_weights = updated((2,), (flat[8:12],), mine, (0, 1), new_a)
+    parts = [reduced(at) for at in range(3)]
+    sums = [crossed(parts[0]), crossed(parts[1])]
+    sums[0], part_d = tie(sums[0], parts[2])
+    four = [pieces(s) for s in (*sums, crossed(part_d))]
+    (new_a,) = updated((0, 1), four[:2], mine)
+    new_d, new_weights = updated((2,), four[2:], mine, (0, 1), new_a)
     hidden, new_weights = pl.pallas_call(
         gate_up_kernel,
         out_shape=(

time: 64.5 us -> 61 us (0.946)
  waiting for transfers between devices: 18.6 us -> 15.6 us
    ppermute x20, waiting for transfers between devices: 18.6 us -> 15.6 us  [move(): return lax.ppermute(value, 'tok', pairs)]
  transfers between devices with their start and end apart: 20 -> 20, of which waited for: 11 -> 10; matrix products, arithmetic and copies ran while one was open for 0% -> 0% of each run, Pallas kernels for 9% -> 17%
where the time goes in v3:
time: 61 us; the launch traced here: 60.8 us
  starting transfers between devices  25.9 us (42%)
  waiting for transfers between devices  15.6 us (26%)
  Pallas kernels  15.5 us (25%)
  local copies, waits for them, and re-layouts  2.85 us (5%)
  between operations  0.75 us (1%)
    ppermute x20, starting transfers between devices, move(): return lax.ppermute(value, 'tok', pairs)  25.9 us
    ppermute x20, waiting for transfers between devices, move(): return lax.ppermute(value, 'tok', pairs)  15.6 us
    pallas_call x2, Pallas kernels, updated(): pl.pallas_call(functools.partial(ns_kernel, which, earlier), out_shape=ou...  7.39 us
    unnamed x6, local copies, waits for them, and re-layouts  2.85 us
    pallas_call x1, Pallas kernels, body(): pl.pallas_call(pack_kernel, out_shape=(pair, pair), in_specs=[ANY_SPEC] *...  2.06 us
    pallas_call x1, Pallas kernels, body(): pl.pallas_call(down_kernel, out_shape=(jax.ShapeDtypeStruct(queries.shape...  1.64 us
    pallas_call x1, Pallas kernels, body(): pl.pallas_call(near_kernel, out_shape=(three32, three32, jax.ShapeDtypeSt...  1.55 us
    pallas_call x1, Pallas kernels, body(): pl.pallas_call(gate_up_kernel, out_shape=(jax.ShapeDtypeStruct(queries.sh...  1.47 us
  transfers between devices with their start and end apart: 20, of which 10 were waited for; matrix products, arithmetic and copies ran while one was open for 0% of the time, Pallas kernels for 17%

profile of v3, /device:TPU:0, one launch (start us, length us, event | category | flops | bytes accessed | tf_op | source)
XLA Modules:
  0.0 60.8 jit_solution(13464633578490206015)
XLA Ops:
  0.6 2.1 %shard_map.68 = (bf16[2,128,512]{2,1,0:T(8,128)(2,1)}, bf16[2,128,512]{2,1,0:T(8,128)(2,1)}) custom-call(bf16[128,1024]{1,0:T(8,128)(2,1)} %keys.1, bf16[128,1024]{1,0:T(8,128)(2,1)} %values.1, f32[2,128]{1,0:T(2,128)} %rates.1), custom_call_target="tpu_custom_call" | custom-call | tf_op jit(solution)/shard_map/pallas_call | solution.py:240
  2.7 0.5 collective-permute-start
  3.2 2.6 %collective-permute-start.1 = (bf16[2,128,512]{2,1,0:T(8,128)(2,1)}, bf16[2,128,512]{2,1,0:T(8,128)(2,1)S(1)}, u32[]{:S(2)}, u32[]{:S(2)}) collective-permute-start(bf16[2,128,512]{2,1,0:T(8,128)(2,1)} %get-tuple-element.19.t0), channel_id=1, source_target_pairs={{0,2},{1,5},{2,0},{3,7},{4,6},{5,1},{6,4},{7,3},{8,10},{9,13},{10,... | collective-permute-start | bytes 786440 | tf_op jit(solution)/shard_map/ppermute | solution.py:234
  5.8 0.1 collective-permute-start.2
  5.9 0.0 collective-permute-done.t1
  5.9 1.9 %copy-done = bf16[2,3,512,512]{3,2,1,0:T(8,128)(2,1)S(1)} copy-done((bf16[2,3,512,512]{3,2,1,0:T(8,128)(2,1)S(1)}, bf16[2,3,512,512]{3,2,1,0:T(8,128)(2,1)}, u32[]{:S(2)}) %copy-start) | copy-done | bytes 3145752
  7.8 0.9 %copy-done.1 = bf16[2,128,512]{2,1,0:T(8,128)(2,1)S(1)} copy-done((bf16[2,128,512]{2,1,0:T(8,128)(2,1)S(1)}, bf16[2,128,512]{2,1,0:T(8,128)(2,1)}, u32[]{:S(2)}) %copy-start.1) | copy-done | bytes 262168
  8.8 1.5 %shard_map.69 = (f32[3,512,128]{2,1,0:T(8,128)S(1)}, f32[3,512,128]{2,1,0:T(8,128)S(1)}, bf16[3,512,512]{2,1,0:T(8,128)(2,1)S(1)}) custom-call(bf16[2,128,512]{2,1,0:T(8,128)(2,1)S(1)} %copy-done.1, bf16[2,128,512]{2,1,0:T(8,128)(2,1)S(1)} %collective-permute-done.t1, bf16[2,3,512,512]{3,2,1,0:T(8,128)(2,1)S(1)} %copy-done), custom_call_target="tpu_custom_call" | custom-call | tf_op jit(solution)/shard_map/pallas_call | solution.py:256
  10.3 2.0 %collective-permute-done.1.t2 = bf16[2,128,512]{2,1,0:T(8,128)(2,1)S(1)} collective-permute-done((bf16[2,128,512]{2,1,0:T(8,128)(2,1)}, bf16[2,128,512]{2,1,0:T(8,128)(2,1)S(1)}, u32[]{:S(2)}, u32[]{:S(2)}) %collective-permute-start.1) | collective-permute-done | bytes 262176 | tf_op jit(solution)/shard_map/ppermute | solution.py:234
  12.3 0.8 %collective-permute-done.2.t3 = bf16[2,128,512]{2,1,0:T(8,128)(2,1)S(1)} collective-permute-done((bf16[2,128,512]{2,1,0:T(8,128)(2,1)}, bf16[2,128,512]{2,1,0:T(8,128)(2,1)S(1)}, u32[]{:S(2)}, u32[]{:S(2)}) %collective-permute-start.2) | collective-permute-done | bytes 262176 | tf_op jit(solution)/shard_map/ppermute | solution.py:234
  13.2 1.4 %shard_map.70 = (bf16[512,128]{1,0:T(8,128)(2,1)S(1)}, bf16[512,128]{1,0:T(8,128)(2,1)S(1)}, bf16[512,128]{1,0:T(8,128)(2,1)S(1)}, f32[512,128]{1,0:T(8,128)S(1)...) custom-call(bf16[2,128,512]{2,1,0:T(8,128)(2,1)S(1)} %collective-permute-done.1.t2, ...), custom_call_target="tpu_custom_call" | custom-call | tf_op jit(solution)/shard_map/pallas_call | solution.py:264
  14.6 2.1 %collective-permute-start.3 = (bf16[512,128]{1,0:T(8,128)(2,1)S(1)}, bf16[512,128]{1,0:T(8,128)(2,1)S(1)}, u32[]{:S(2)}, u32[]{:S(2)}) collective-permute-start(bf16[512,128]{1,0:T(8,128)(2,1)S(1)} %get-tuple-element.25), channel_id=1, source_target_pairs={{0,4},{1,3},{2,6},{3,1},{4,0},{5,7},{6,2},{7,5},{8,12},{9,11},{10,... | collective-permute-start | bytes 393224 | tf_op jit(solution)/shard_map/ppermute | solution.py:234
  16.7 0.1 collective-permute-start.5
  16.8 1.9 %collective-permute-start.9 = (bf16[512,128]{1,0:T(8,128)(2,1)S(1)}, bf16[512,128]{1,0:T(8,128)(2,1)S(1)}, u32[]{:S(2)}, u32[]{:S(2)}) collective-permute-start(bf16[512,128]{1,0:T(8,128)(2,1)S(1)} %get-tuple-element.30), channel_id=1, source_target_pairs={{0,4},{1,3},{2,6},{3,1},{4,0},{5,7},{6,2},{7,5},{8,12},{9,11},{10,... | collective-permute-start | bytes 393224 | tf_op jit(solution)/shard_map/ppermute | solution.py:234
  18.8 0.9 %collective-permute-done.3 = bf16[512,128]{1,0:T(8,128)(2,1)S(1)} collective-permute-done((bf16[512,128]{1,0:T(8,128)(2,1)S(1)}, bf16[512,128]{1,0:T(8,128)(2,1)S(1)}, u32[]{:S(2)}, u32[]{:S(2)}) %collective-permute-start.3) | collective-permute-done | bytes 131104 | tf_op jit(solution)/shard_map/ppermute | solution.py:234
  19.7 3.1 %collective-permute-start.4 = (bf16[512,128]{1,0:T(8,128)(2,1)S(1)}, bf16[512,128]{1,0:T(8,128)(2,1)S(1)}, u32[]{:S(2)}, u32[]{:S(2)}) collective-permute-start(bf16[512,128]{1,0:T(8,128)(2,1)S(1)} %add_convert_fusion.5), channel_id=1, source_target_pairs={{0,8},{1,9},{2,10},{3,11},{4,12},{5,13},{6,14},{7,15},{8,0},{9,1},... | collective-permute-start | bytes 393224 | tf_op jit(solution)/shard_map/ppermute | solution.py:234
  22.8 1.9 %collective-permute-done.9 = bf16[512,128]{1,0:T(8,128)(2,1)S(1)} collective-permute-done((bf16[512,128]{1,0:T(8,128)(2,1)S(1)}, bf16[512,128]{1,0:T(8,128)(2,1)S(1)}, u32[]{:S(2)}, u32[]{:S(2)}) %collective-permute-start.9) | collective-permute-done | bytes 131104 | tf_op jit(solution)/shard_map/ppermute | solution.py:234
  24.7 2.7 %collective-permute-start.10 = (bf16[512,128]{1,0:T(8,128)(2,1)S(1)}, bf16[512,128]{1,0:T(8,128)(2,1)S(1)}, u32[]{:S(2)}, u32[]{:S(2)}) collective-permute-start(bf16[512,128]{1,0:T(8,128)(2,1)S(1)} %add_convert_fusion.2), channel_id=1, source_target_pairs={{0,8},{1,9},{2,10},{3,11},{4,12},{5,13},{6,14},{7,15},{8,0},{9,1},... | collective-permute-start | bytes 393224 | tf_op jit(solution)/shard_map/ppermute | solution.py:234
  27.5 0.0 collective-permute-done.5
  27.5 4.6 %collective-permute-done.4 = bf16[512,128]{1,0:T(8,128)(2,1)S(1)} collective-permute-done((bf16[512,128]{1,0:T(8,128)(2,1)S(1)}, bf16[512,128]{1,0:T(8,128)(2,1)S(1)}, u32[]{:S(2)}, u32[]{:S(2)}) %collective-permute-start.4) | collective-permute-done | bytes 131104 | tf_op jit(solution)/shard_map/ppermute | solution.py:234
  32.1 1.5 %collective-permute-start.7 = (bf16[512,128]{1,0:T(8,128)(2,1)S(1)}, bf16[512,128]{1,0:T(8,128)(2,1)S(1)}, u32[]{:S(2)}, u32[]{:S(2)}) collective-permute-start(bf16[512,128]{1,0:T(8,128)(2,1)S(1)} %add_convert_fusion.4.refs_0_), channel_id=1, source_target_pairs={{0,2},{1,5},{2,0},{3,7},{4,6},{5,1},{6,4},{7,3},{8,10},{9,13},{10,... | collective-permute-start | bytes 393224 | tf_op jit(solution)/shard_map/ppermute | solution.py:234
  33.6 0.4 collective-permute-start.6
  34.0 3.4 %collective-permute-start.15 = (bf16[512,128]{1,0:T(8,128)(2,1)S(1)}, bf16[512,128]{1,0:T(8,128)(2,1)S(1)}, u32[]{:S(2)}, u32[]{:S(2)}) collective-permute-start(bf16[512,128]{1,0:T(8,128)(2,1)S(1)} %add_convert_fusion.3), channel_id=1, source_target_pairs={{0,8},{1,9},{2,10},{3,11},{4,12},{5,13},{6,14},{7,15},{8,0},{9,1},... | collective-permute-start | bytes 393224 | tf_op jit(solution)/shard_map/ppermute | solution.py:234
  37.4 0.0 collective-permute-done.10
  37.5 0.6 %collective-permute-start.12 = (bf16[512,128]{1,0:T(8,128)(2,1)S(1)}, bf16[512,128]{1,0:T(8,128)(2,1)S(1)}, u32[]{:S(2)}, u32[]{:S(2)}) collective-permute-start(bf16[512,128]{1,0:T(8,128)(2,1)S(1)} %add_convert_fusion.1.refs_4_), channel_id=1, source_target_pairs={{0,2},{1,5},{2,0},{3,7},{4,6},{5,1},{6,4},{7,3},{8,10},{9,13},{10,... | collective-permute-start | bytes 393224 | tf_op jit(solution)/shard_map/ppermute | solution.py:234
  38.1 0.0 collective-permute-start.11
  38.1 2.9 %collective-permute-done.15 = bf16[512,128]{1,0:T(8,128)(2,1)S(1)} collective-permute-done((bf16[512,128]{1,0:T(8,128)(2,1)S(1)}, bf16[512,128]{1,0:T(8,128)(2,1)S(1)}, u32[]{:S(2)}, u32[]{:S(2)}) %collective-permute-start.15) | collective-permute-done | bytes 131104 | tf_op jit(solution)/shard_map/ppermute | solution.py:234
  41.0 1.4 %collective-permute-start.16 = (bf16[512,128]{1,0:T(8,128)(2,1)S(1)}, bf16[512,128]{1,0:T(8,128)(2,1)S(1)}, u32[]{:S(2)}, u32[]{:S(2)}) collective-permute-start(bf16[512,128]{1,0:T(8,128)(2,1)S(1)} %add_convert_fusion.refs_0_), channel_id=1, source_target_pairs={{0,4},{1,3},{2,6},{3,1},{4,0},{5,7},{6,2},{7,5},{8,12},{9,11},{10,... | collective-permute-start | bytes 393224 | tf_op jit(solution)/shard_map/ppermute | solution.py:234
  42.5 0.0 collective-permute-done.6.refs_1_
  42.5 1.4 %collective-permute-start.8 = (bf16[512,128]{1,0:T(8,128)(2,1)S(1)}, bf16[512,128]{1,0:T(8,128)(2,1)S(1)}, u32[]{:S(2)}, u32[]{:S(2)}) collective-permute-start(bf16[512,128]{1,0:T(8,128)(2,1)S(1)} %collective-permute-done.6.refs_1_), channel_id=1, source_target_pairs={{0,2},{1,5},{2,0},{3,7},{4,6},{5,1},{6,4},{7,3},{8,10},{9,13},{10,... | collective-permute-start | bytes 393224 | tf_op jit(solution)/shard_map/ppermute | solution.py:234
  43.8 0.8 %collective-permute-done.11.refs_5_ = bf16[512,128]{1,0:T(8,128)(2,1)S(1)} collective-permute-done((bf16[512,128]{1,0:T(8,128)(2,1)S(1)}, bf16[512,128]{1,0:T(8,128)(2,1)S(1)}, u32[]{:S(2)}, u32[]{:S(2)}) %collective-permute-start.11) | collective-permute-done | bytes 131104 | tf_op jit(solution)/shard_map/ppermute | solution.py:234
  44.6 1.3 %collective-permute-start.13 = (bf16[512,128]{1,0:T(8,128)(2,1)S(1)}, bf16[512,128]{1,0:T(8,128)(2,1)S(1)}, u32[]{:S(2)}, u32[]{:S(2)}) collective-permute-start(bf16[512,128]{1,0:T(8,128)(2,1)S(1)} %collective-permute-done.11.refs_5_), channel_id=1, source_target_pairs={{0,2},{1,5},{2,0},{3,7},{4,6},{5,1},{6,4},{7,3},{8,10},{9,13},{10,... | collective-permute-start | bytes 393224 | tf_op jit(solution)/shard_map/ppermute | solution.py:234
  45.9 0.0 collective-permute-done.7.refs_2_
  45.9 0.7 %collective-permute-start.17 = (bf16[512,128]{1,0:T(8,128)(2,1)S(1)}, bf16[512,128]{1,0:T(8,128)(2,1)S(1)}, u32[]{:S(2)}, u32[]{:S(2)}) collective-permute-start(bf16[512,128]{1,0:T(8,128)(2,1)S(1)} %add_convert_fusion.refs_0_), channel_id=1, source_target_pairs={{0,2},{1,5},{2,0},{3,7},{4,6},{5,1},{6,4},{7,3},{8,10},{9,13},{10,... | collective-permute-start | bytes 393224 | tf_op jit(solution)/shard_map/ppermute | solution.py:234
  46.6 0.9 %collective-permute-done.16.refs_1_ = bf16[512,128]{1,0:T(8,128)(2,1)S(1)} collective-permute-done((bf16[512,128]{1,0:T(8,128)(2,1)S(1)}, bf16[512,128]{1,0:T(8,128)(2,1)S(1)}, u32[]{:S(2)}, u32[]{:S(2)}) %collective-permute-start.16) | collective-permute-done | bytes 131104 | tf_op jit(solution)/shard_map/ppermute | solution.py:234
  47.5 1.2 %collective-permute-start.18 = (bf16[512,128]{1,0:T(8,128)(2,1)S(1)}, bf16[512,128]{1,0:T(8,128)(2,1)S(1)}, u32[]{:S(2)}, u32[]{:S(2)}) collective-permute-start(bf16[512,128]{1,0:T(8,128)(2,1)S(1)} %collective-permute-done.16.refs_1_), channel_id=1, source_target_pairs={{0,2},{1,5},{2,0},{3,7},{4,6},{5,1},{6,4},{7,3},{8,10},{9,13},{10,... | collective-permute-start | bytes 393224 | tf_op jit(solution)/shard_map/ppermute | solution.py:234
  48.8 0.0 collective-permute-done.12.refs_6_
  48.8 0.8 %collective-permute-done.13.refs_7_ = bf16[512,128]{1,0:T(8,128)(2,1)S(1)} collective-permute-done((bf16[512,128]{1,0:T(8,128)(2,1)S(1)}, bf16[512,128]{1,0:T(8,128)(2,1)S(1)}, u32[]{:S(2)}, u32[]{:S(2)}) %collective-permute-start.13) | collective-permute-done | bytes 131104 | tf_op jit(solution)/shard_map/ppermute | solution.py:234
  49.6 4.6 %shard_map.71.refs_4_.own = bf16[2,512,512]{2,1,0:T(8,128)(2,1)S(1)} custom-call(bf16[3,512,512]{2,1,0:T(8,128)(2,1)S(1)} %get-tuple-element.21.mine, bf16[512,128]{1,0:T(8,128)(2,1)S(1)} %add_convert_fusion.4.refs_0_, bf16[512,128]{1,0:T(8,128)(2,1)S(1)} %collective-permute-done.6.refs_1_, bf16[512,128]{1,0:T(8,128)(2,1)S(1)} %collective-permute-done.7.refs_2_, ...), custom_call_target="tpu_custom_call" | custom-call | flops 64424509440 | bytes 33554432 | tf_op jit(solution)/shard_map/pallas_call | solution.py:177
  54.2 0.0 copy-start.2
  54.2 0.1 collective-permute-start.14
  54.3 0.0 collective-permute-done.17.refs_2_
  54.3 2.7 %shard_map.72 = (bf16[1,512,512]{2,1,0:T(8,128)(2,1)S(1)}, bf16[2,3,512,512]{3,2,1,0:T(8,128)(2,1)}) custom-call(bf16[3,512,512]{2,1,0:T(8,128)(2,1)S(1)} %get-tuple-element.21.mine, bf16[512,128]{1,0:T(8,128)(2,1)S(1)} %add_convert_fusion.refs_0_, bf16[512,128]{1,0:T(8,128)(2,1)S(1)} %collective-permute-done.16.refs_1_, ...), custom_call_target="tpu_custom_call" | custom-call | flops 32212254720 | bytes 16777216 | tf_op jit(solution)/shard_map/pallas_call | solution.py:177
  57.1 0.5 collective-permute-start.19
  57.6 0.0 collective-permute-done.14.other
  57.6 1.5 %shard_map.73 = (bf16[128,1024]{1,0:T(8,128)(2,1)S(1)}, bf16[2,3,512,512]{3,2,1,0:T(8,128)(2,1)}) custom-call(bf16[128,1024]{1,0:T(8,128)(2,1)S(1)} %copy-done.2, bf16[2,512,512]{2,1,0:T(8,128)(2,1)S(1)} %shard_map.71.refs_4_.own, bf16[2,512,512]{2,1,0:T(8,128)(2,1)S(1)} %collective-permute-done.14.other, ...), custom_call_target="tpu_custom_call", output_to_operand_aliasing={{1}: (4, {})} | custom-call | tf_op jit(solution)/shard_map/pallas_call | solution.py:292
  59.1 0.1 collective-permute-done.19.other
  59.2 1.6 %shard_map.74 = (bf16[128,1024]{1,0:T(8,128)(2,1)}, bf16[2,3,512,512]{3,2,1,0:T(8,128)(2,1)}) custom-call(bf16[128,1024]{1,0:T(8,128)(2,1)S(1)} %get-tuple-element.34.hidden, bf16[1,512,512]{2,1,0:T(8,128)(2,1)S(1)} %get-tuple-element.32.own_down.own, bf16[1,512,512]{2,1,0:T(8,128)(2,1)S(1)} %collective-permute-done.19.other, ...), custom_call_target="tpu_custom_call", output_to_operand_aliasing={{1}: (3, {})} | custom-call | tf_op jit(solution)/shard_map/pallas_call | solution.py:306
  (11 shorter events, 0.2 us)
Async XLA Ops:
  2.7 3.2 %collective-permute-start = (bf16[2,128,512]{2,1,0:T(8,128)(2,1)}, bf16[2,128,512]{2,1,0:T(8,128)(2,1)S(1)}, u32[]{:S(2)}, u32[]{:S(2)}) collective-permute-start(bf16[2,128,512]{2,1,0:T(8,128)(2,1)} %get-tuple-element.20), channel_id=1, source_target_pairs={{0,1},{1,0},{2,3},{3,2},{4,5},{5,4},{6,7},{7,6},{8,9},{9,8},{10,11... | collective-permute-start | bytes 786440 | tf_op jit(solution)/shard_map/ppermute | solution.py:234
  3.2 9.1 %collective-permute-start.1 = (bf16[2,128,512]{2,1,0:T(8,128)(2,1)}, bf16[2,128,512]{2,1,0:T(8,128)(2,1)S(1)}, u32[]{:S(2)}, u32[]{:S(2)}) collective-permute-start(bf16[2,128,512]{2,1,0:T(8,128)(2,1)} %get-tuple-element.19.t0), channel_id=1, source_target_pairs={{0,2},{1,5},{2,0},{3,7},{4,6},{5,1},{6,4},{7,3},{8,10},{9,13},{10,... | collective-permute-start | bytes 786440 | tf_op jit(solution)/shard_map/ppermute | solution.py:234
  5.8 7.4 %collective-permute-start.2 = (bf16[2,128,512]{2,1,0:T(8,128)(2,1)}, bf16[2,128,512]{2,1,0:T(8,128)(2,1)S(1)}, u32[]{:S(2)}, u32[]{:S(2)}) collective-permute-start(bf16[2,128,512]{2,1,0:T(8,128)(2,1)} %get-tuple-element.20), channel_id=1, source_target_pairs={{0,5},{1,2},{2,7},{3,0},{4,1},{5,6},{6,3},{7,4},{8,13},{9,10},{10,... | collective-permute-start | bytes 786440 | tf_op jit(solution)/shard_map/ppermute | solution.py:234
  5.9 1.9 %copy-start = (bf16[2,3,512,512]{3,2,1,0:T(8,128)(2,1)S(1)}, bf16[2,3,512,512]{3,2,1,0:T(8,128)(2,1)}, u32[]{:S(2)}) copy-start(bf16[2,3,512,512]{3,2,1,0:T(8,128)(2,1)} %weights.1) | copy-start | bytes 9437188
  7.8 0.9 %copy-start.1 = (bf16[2,128,512]{2,1,0:T(8,128)(2,1)S(1)}, bf16[2,128,512]{2,1,0:T(8,128)(2,1)}, u32[]{:S(2)}) copy-start(bf16[2,128,512]{2,1,0:T(8,128)(2,1)} %get-tuple-element.19.t0) | copy-start | bytes 786436
  14.6 5.1 %collective-permute-start.3 = (bf16[512,128]{1,0:T(8,128)(2,1)S(1)}, bf16[512,128]{1,0:T(8,128)(2,1)S(1)}, u32[]{:S(2)}, u32[]{:S(2)}) collective-permute-start(bf16[512,128]{1,0:T(8,128)(2,1)S(1)} %get-tuple-element.25), channel_id=1, source_target_pairs={{0,4},{1,3},{2,6},{3,1},{4,0},{5,7},{6,2},{7,5},{8,12},{9,11},{10,... | collective-permute-start | bytes 393224 | tf_op jit(solution)/shard_map/ppermute | solution.py:234
  16.7 10.7 %collective-permute-start.5 = (bf16[512,128]{1,0:T(8,128)(2,1)S(1)}, bf16[512,128]{1,0:T(8,128)(2,1)S(1)}, u32[]{:S(2)}, u32[]{:S(2)}) collective-permute-start(bf16[512,128]{1,0:T(8,128)(2,1)S(1)} %get-tuple-element.27), channel_id=1, source_target_pairs={{0,4},{1,3},{2,6},{3,1},{4,0},{5,7},{6,2},{7,5},{8,12},{9,11},{10,... | collective-permute-start | bytes 393224 | tf_op jit(solution)/shard_map/ppermute | solution.py:234
  16.8 7.9 %collective-permute-start.9 = (bf16[512,128]{1,0:T(8,128)(2,1)S(1)}, bf16[512,128]{1,0:T(8,128)(2,1)S(1)}, u32[]{:S(2)}, u32[]{:S(2)}) collective-permute-start(bf16[512,128]{1,0:T(8,128)(2,1)S(1)} %get-tuple-element.30), channel_id=1, source_target_pairs={{0,4},{1,3},{2,6},{3,1},{4,0},{5,7},{6,2},{7,5},{8,12},{9,11},{10,... | collective-permute-start | bytes 393224 | tf_op jit(solution)/shard_map/ppermute | solution.py:234
  19.7 12.3 %collective-permute-start.4 = (bf16[512,128]{1,0:T(8,128)(2,1)S(1)}, bf16[512,128]{1,0:T(8,128)(2,1)S(1)}, u32[]{:S(2)}, u32[]{:S(2)}) collective-permute-start(bf16[512,128]{1,0:T(8,128)(2,1)S(1)} %add_convert_fusion.5), channel_id=1, source_target_pairs={{0,8},{1,9},{2,10},{3,11},{4,12},{5,13},{6,14},{7,15},{8,0},{9,1},... | collective-permute-start | bytes 393224 | tf_op jit(solution)/shard_map/ppermute | solution.py:234
  24.7 12.7 %collective-permute-start.10 = (bf16[512,128]{1,0:T(8,128)(2,1)S(1)}, bf16[512,128]{1,0:T(8,128)(2,1)S(1)}, u32[]{:S(2)}, u32[]{:S(2)}) collective-permute-start(bf16[512,128]{1,0:T(8,128)(2,1)S(1)} %add_convert_fusion.2), channel_id=1, source_target_pairs={{0,8},{1,9},{2,10},{3,11},{4,12},{5,13},{6,14},{7,15},{8,0},{9,1},... | collective-permute-start | bytes 393224 | tf_op jit(solution)/shard_map/ppermute | solution.py:234
  32.1 13.9 %collective-permute-start.7 = (bf16[512,128]{1,0:T(8,128)(2,1)S(1)}, bf16[512,128]{1,0:T(8,128)(2,1)S(1)}, u32[]{:S(2)}, u32[]{:S(2)}) collective-permute-start(bf16[512,128]{1,0:T(8,128)(2,1)S(1)} %add_convert_fusion.4.refs_0_), channel_id=1, source_target_pairs={{0,2},{1,5},{2,0},{3,7},{4,6},{5,1},{6,4},{7,3},{8,10},{9,13},{10,... | collective-permute-start | bytes 393224 | tf_op jit(solution)/shard_map/ppermute | solution.py:234
  33.6 8.9 %collective-permute-start.6 = (bf16[512,128]{1,0:T(8,128)(2,1)S(1)}, bf16[512,128]{1,0:T(8,128)(2,1)S(1)}, u32[]{:S(2)}, u32[]{:S(2)}) collective-permute-start(bf16[512,128]{1,0:T(8,128)(2,1)S(1)} %add_convert_fusion.4.refs_0_), channel_id=1, source_target_pairs={{0,4},{1,3},{2,6},{3,1},{4,0},{5,7},{6,2},{7,5},{8,12},{9,11},{10,... | collective-permute-start | bytes 393224 | tf_op jit(solution)/shard_map/ppermute | solution.py:234
  34.0 7.0 %collective-permute-start.15 = (bf16[512,128]{1,0:T(8,128)(2,1)S(1)}, bf16[512,128]{1,0:T(8,128)(2,1)S(1)}, u32[]{:S(2)}, u32[]{:S(2)}) collective-permute-start(bf16[512,128]{1,0:T(8,128)(2,1)S(1)} %add_convert_fusion.3), channel_id=1, source_target_pairs={{0,8},{1,9},{2,10},{3,11},{4,12},{5,13},{6,14},{7,15},{8,0},{9,1},... | collective-permute-start | bytes 393224 | tf_op jit(solution)/shard_map/ppermute | solution.py:234
  37.5 11.3 %collective-permute-start.12 = (bf16[512,128]{1,0:T(8,128)(2,1)S(1)}, bf16[512,128]{1,0:T(8,128)(2,1)S(1)}, u32[]{:S(2)}, u32[]{:S(2)}) collective-permute-start(bf16[512,128]{1,0:T(8,128)(2,1)S(1)} %add_convert_fusion.1.refs_4_), channel_id=1, source_target_pairs={{0,2},{1,5},{2,0},{3,7},{4,6},{5,1},{6,4},{7,3},{8,10},{9,13},{10,... | collective-permute-start | bytes 393224 | tf_op jit(solution)/shard_map/ppermute | solution.py:234
  38.1 6.5 %collective-permute-start.11 = (bf16[512,128]{1,0:T(8,128)(2,1)S(1)}, bf16[512,128]{1,0:T(8,128)(2,1)S(1)}, u32[]{:S(2)}, u32[]{:S(2)}) collective-permute-start(bf16[512,128]{1,0:T(8,128)(2,1)S(1)} %add_convert_fusion.1.refs_4_), channel_id=1, source_target_pairs={{0,4},{1,3},{2,6},{3,1},{4,0},{5,7},{6,2},{7,5},{8,12},{9,11},{10,... | collective-permute-start | bytes 393224 | tf_op jit(solution)/shard_map/ppermute | solution.py:234
  41.0 6.5 %collective-permute-start.16 = (bf16[512,128]{1,0:T(8,128)(2,1)S(1)}, bf16[512,128]{1,0:T(8,128)(2,1)S(1)}, u32[]{:S(2)}, u32[]{:S(2)}) collective-permute-start(bf16[512,128]{1,0:T(8,128)(2,1)S(1)} %add_convert_fusion.refs_0_), channel_id=1, source_target_pairs={{0,4},{1,3},{2,6},{3,1},{4,0},{5,7},{6,2},{7,5},{8,12},{9,11},{10,... | collective-permute-start | bytes 393224 | tf_op jit(solution)/shard_map/ppermute | solution.py:234
  42.5 6.3 %collective-permute-start.8 = (bf16[512,128]{1,0:T(8,128)(2,1)S(1)}, bf16[512,128]{1,0:T(8,128)(2,1)S(1)}, u32[]{:S(2)}, u32[]{:S(2)}) collective-permute-start(bf16[512,128]{1,0:T(8,128)(2,1)S(1)} %collective-permute-done.6.refs_1_), channel_id=1, source_target_pairs={{0,2},{1,5},{2,0},{3,7},{4,6},{5,1},{6,4},{7,3},{8,10},{9,13},{10,... | collective-permute-start | bytes 393224 | tf_op jit(solution)/shard_map/ppermute | solution.py:234
  44.6 5.0 %collective-permute-start.13 = (bf16[512,128]{1,0:T(8,128)(2,1)S(1)}, bf16[512,128]{1,0:T(8,128)(2,1)S(1)}, u32[]{:S(2)}, u32[]{:S(2)}) collective-permute-start(bf16[512,128]{1,0:T(8,128)(2,1)S(1)} %collective-permute-done.11.refs_5_), channel_id=1, source_target_pairs={{0,2},{1,5},{2,0},{3,7},{4,6},{5,1},{6,4},{7,3},{8,10},{9,13},{10,... | collective-permute-start | bytes 393224 | tf_op jit(solution)/shard_map/ppermute | solution.py:234
  45.9 8.4 %collective-permute-start.17 = (bf16[512,128]{1,0:T(8,128)(2,1)S(1)}, bf16[512,128]{1,0:T(8,128)(2,1)S(1)}, u32[]{:S(2)}, u32[]{:S(2)}) collective-permute-start(bf16[512,128]{1,0:T(8,128)(2,1)S(1)} %add_convert_fusion.refs_0_), channel_id=1, source_target_pairs={{0,2},{1,5},{2,0},{3,7},{4,6},{5,1},{6,4},{7,3},{8,10},{9,13},{10,... | collective-permute-start | bytes 393224 | tf_op jit(solution)/shard_map/ppermute | solution.py:234
  47.5 6.8 %collective-permute-start.18 = (bf16[512,128]{1,0:T(8,128)(2,1)S(1)}, bf16[512,128]{1,0:T(8,128)(2,1)S(1)}, u32[]{:S(2)}, u32[]{:S(2)}) collective-permute-start(bf16[512,128]{1,0:T(8,128)(2,1)S(1)} %collective-permute-done.16.refs_1_), channel_id=1, source_target_pairs={{0,2},{1,5},{2,0},{3,7},{4,6},{5,1},{6,4},{7,3},{8,10},{9,13},{10,... | collective-permute-start | bytes 393224 | tf_op jit(solution)/shard_map/ppermute | solution.py:234
  54.2 3.4 %copy-start.2 = (bf16[128,1024]{1,0:T(8,128)(2,1)S(1)}, bf16[128,1024]{1,0:T(8,128)(2,1)}, u32[]{:S(2)}) copy-start(bf16[128,1024]{1,0:T(8,128)(2,1)} %queries.1) | copy-start | bytes 786436
  54.2 3.4 %collective-permute-start.14 = (bf16[2,512,512]{2,1,0:T(8,128)(2,1)S(1)}, bf16[2,512,512]{2,1,0:T(8,128)(2,1)S(1)}, u32[]{:S(2)}, u32[]{:S(2)}) collective-permute-start(bf16[2,512,512]{2,1,0:T(8,128)(2,1)S(1)} %shard_map.71.refs_4_.own), channel_id=1, source_target_pairs={{0,1},{1,0},{2,3},{3,2},{4,5},{5,4},{6,7},{7,6},{8,9},{9,8},{10,11... | collective-permute-start | bytes 3145736 | tf_op jit(solution)/shard_map/ppermute | solution.py:234
  57.1 2.1 %collective-permute-start.19 = (bf16[1,512,512]{2,1,0:T(8,128)(2,1)S(1)}, bf16[1,512,512]{2,1,0:T(8,128)(2,1)S(1)}, u32[]{:S(2)}, u32[]{:S(2)}) collective-permute-start(bf16[1,512,512]{2,1,0:T(8,128)(2,1)S(1)} %get-tuple-element.32.own_down.own), channel_id=1, source_target_pairs={{0,1},{1,0},{2,3},{3,2},{4,5},{5,4},{6,7},{7,6},{8,9},{9,8},{10,11... | collective-permute-start | bytes 1572872 | tf_op jit(solution)/shard_map/ppermute | solution.py:234

commit v4 on v3

--- a/solution.py
+++ b/solution.py
@@ -45,15 +45,17 @@
         copies.append(pltpu.make_async_copy(keys.at[:, span(head, width)], out.at[0], sems.at[2 + at]))
     for copy in copies:
         copy.start()
-    for copy in copies:
+    for copy in copies[:2]:
         copy.wait()
     for head, out in ((core, own), (1 - core, other)):
         row = jnp.where(head == 0, rate[0:1, :], rate[1:2, :])
         column = jnp.broadcast_to(row, (tokens, tokens)).T[:, 0:1]
         out[1] = (-column * held[:, span(head, width)].astype(F32)).astype(BF16)
-
-
-def token_grads(k, o, weights, cut):
+    for copy in copies[2:]:
+        copy.wait()
+
+
+def token_parts(k, o, weights, cut):
     gate = dot(k, weights[0, :, cut])
     upper = dot(k, weights[1, :, cut])
     back = dot(o, weights[2, cut, :], 1, 1)
@@ -62,6 +64,11 @@
     hidden = (silu_gate * upper).astype(BF16)
     d_gate = (back * upper * sigma * (1.0 + gate * (1.0 - sigma))).astype(BF16)
     d_upper = (back * silu_gate).astype(BF16)
+    return hidden, d_gate, d_upper
+
+
+def token_grads(k, o, weights, cut):
+    hidden, d_gate, d_upper = token_parts(k, o, weights, cut)
     return dot(k, d_gate, 0, 0), dot(k, d_upper, 0, 0), dot(hidden, o, 0, 0)
 
 
@@ -88,20 +95,29 @@
             out[2, at * piece : (at + 1) * piece, :] = down[:, at * piece : (at + 1) * piece]
 
 
-def far_kernel(t2, t3, mine, near_send, near_keep, *refs):
-    outs, (keys, outer) = refs[:6], refs[6:]
+def far_gate_kernel(t2, t3, mine, near_send, near_keep, send, keep, hidden, d_upper, keys, outer):
     tokens, width = t2.shape[1:]
     piece = width // 4
     for at, src in enumerate((t2, t3)):
         keys[at * tokens : (at + 1) * tokens, :] = src[0]
         outer[at * tokens : (at + 1) * tokens, :] = src[1]
-    for out, near, cut in zip((outs[:3], outs[3:]), (near_send, near_keep), cuts(width)):
-        gate, upper, down = token_grads(keys[...], outer[...], mine, cut)
-        out[0][...] = (near[0] + gate).astype(out[0].dtype)
-        out[1][...] = (near[1] + upper).astype(out[1].dtype)
-        for at in range(width // piece):
-            rows = slice(at * piece, (at + 1) * piece)
-            out[2][rows, :] = (near[2, rows, :] + down[:, rows]).astype(out[2].dtype)
+    for at, (out, near, cut) in enumerate(zip((send, keep), (near_send, near_keep), cuts(width))):
+        h, dg, du = token_parts(keys[...], outer[...], mine, cut)
+        out[...] = (near[0] + dot(keys[...], dg, 0, 0)).astype(out.dtype)
+        hidden[:, at * piece : (at + 1) * piece] = h
+        d_upper[:, at * piece : (at + 1) * piece] = du
+
+
+def far_rest_kernel(keys, outer, hidden, d_upper, near_send, near_keep, *outs):
+    width = keys.shape[1]
+    piece = width // 4
+    for at, (out, near) in enumerate(zip((outs[:2], outs[2:]), (near_send, near_keep))):
+        cut = slice(at * piece, (at + 1) * piece)
+        out[0][...] = (near[1] + dot(keys[...], d_upper[:, cut], 0, 0)).astype(out[0].dtype)
+        down = dot(hidden[:, cut], outer[...], 0, 0)
+        for block in range(width // piece):
+            rows = slice(block * piece, (block + 1) * piece)
+            out[1][rows, :] = (near[2, rows, :] + down[:, rows]).astype(out[1].dtype)
 
 
 def newton_schulz(matrix):
@@ -191,33 +207,42 @@
     )(mine, *flat)
 
 
-def gate_up_kernel(queries, own, other, own_down, held, hidden, new_weights, sems):
+def gate_up_kernel(queries, own, other, own_down, held, hidden, new_weights, readout, product, sems):
     width = own.shape[2]
     core, _, _ = place()
     copies = [
         pltpu.make_async_copy(other, new_weights.at[1 - core, pl.ds(0, 2)], sems.at[0]),
         pltpu.make_async_copy(own_down, new_weights.at[core, pl.ds(2, 1)], sems.at[1]),
+        pltpu.make_async_copy(product, readout.at[:, span(core, width)], sems.at[2]),
     ]
-    for copy in copies:
+    for copy in copies[:2]:
         copy.start()
-    for head, part in ((core, own), (1 - core, other)):
+
+    def units(head, part):
         cols = span(head, width)
         gate = dot(queries[:, cols], part[0])
         upper = dot(queries[:, cols], part[1])
-        hidden[:, cols] = (gate * jax.nn.sigmoid(gate) * upper).astype(BF16)
+        return (gate * jax.nn.sigmoid(gate) * upper).astype(BF16)
+
+    product[...] = dot(units(core, own), own_down[0]).astype(BF16)
+    copies[2].start()
+    hidden[...] = units(1 - core, other)
     for copy in copies:
         copy.wait()
 
 
-def down_kernel(hidden, own, other, held, readout, new_weights, sems):
-    width = own.shape[2]
+def down_kernel(hidden, other, held, held_readout, new_weights, readout, product, sems):
+    width = other.shape[2]
     core, _, _ = place()
-    copy = pltpu.make_async_copy(other, new_weights.at[1 - core, pl.ds(2, 1)], sems.at[0])
-    copy.start()
-    for head, part in ((core, own), (1 - core, other)):
-        cols = span(head, width)
-        readout[:, cols] = dot(hidden[:, cols], part[0]).astype(BF16)
-    copy.wait()
+    copies = [
+        pltpu.make_async_copy(other, new_weights.at[1 - core, pl.ds(2, 1)], sems.at[0]),
+        pltpu.make_async_copy(product, readout.at[:, span(1 - core, width)], sems.at[1]),
+    ]
+    copies[0].start()
+    product[...] = dot(hidden[...], other[0]).astype(BF16)
+    copies[1].start()
+    for copy in copies:
+        copy.wait()
 
 
 def body(size, keys, values, queries, rates, fast_weights):
@@ -261,15 +286,24 @@
         scratch_shapes=rows_scratch + [pltpu.SemaphoreType.DMA],
         compiler_params=PARAMS,
     )(own, move(other, sibling), fast_weights)
-    outs = pl.pallas_call(
-        far_kernel,
-        out_shape=(part16,) * 3 + (part32,) * 3,
+    rows = jax.ShapeDtypeStruct((2 * tokens, width), BF16)
+    units = jax.ShapeDtypeStruct((2 * tokens, width // 2), BF16)
+    send_g, keep_g, hidden, d_upper, far_keys, far_outer = pl.pallas_call(
+        far_gate_kernel,
+        out_shape=(part16, part32, units, units, rows, rows),
         in_specs=[VMEM_SPEC] * 5,
         out_specs=(VMEM_SPEC,) * 6,
-        scratch_shapes=rows_scratch,
         compiler_params=PARAMS,
     )(move(own, first), move(other, across), mine, near_send, near_keep)
-    send, keep = outs[:3], outs[3:]
+    send_u, send_d, keep_u, keep_d = pl.pallas_call(
+        far_rest_kernel,
+        out_shape=(part16,) * 2 + (part32,) * 2,
+        in_specs=[VMEM_SPEC] * 6,
+        out_specs=(VMEM_SPEC,) * 4,
+        compiler_params=PARAMS,
+        cost_estimate=pl.CostEstimate(flops=400 * tokens * width**2, bytes_accessed=64 * width**2, transcendentals=0),
+    )(far_keys, far_outer, hidden, d_upper, near_send, near_keep)
+    send, keep = (send_g, send_u, send_d), (keep_g, keep_u, keep_d)
 
     def reduced(at):
         return (keep[at] + move(send[at], second).astype(F32)).astype(BF16)
@@ -285,36 +319,34 @@
 
     parts = [reduced(at) for at in range(3)]
     sums = [crossed(parts[0]), crossed(parts[1])]
-    sums[0], part_d = tie(sums[0], parts[2])
-    four = [pieces(s) for s in (*sums, crossed(part_d))]
+    sums[0], parts[2] = tie(sums[0], parts[2])
+    sums.append(crossed(parts[2]))
+    four = [pieces(sums[0]), pieces(sums[1]), pieces(sums[2])]
     (new_a,) = updated((0, 1), four[:2], mine)
     new_d, new_weights = updated((2,), four[2:], mine, (0, 1), new_a)
-    hidden, new_weights = pl.pallas_call(
+
+    out_weights = jax.ShapeDtypeStruct(fast_weights.shape, BF16)
+    out_readout = jax.ShapeDtypeStruct(queries.shape, BF16)
+    half_readout = (tokens, width)
+    hidden, new_weights, readout = pl.pallas_call(
         gate_up_kernel,
-        out_shape=(
-            jax.ShapeDtypeStruct(queries.shape, BF16),
-            jax.ShapeDtypeStruct(fast_weights.shape, BF16),
-        ),
+        out_shape=(jax.ShapeDtypeStruct(half_readout, BF16), out_weights, out_readout),
         in_specs=[VMEM_SPEC] * 4 + [ANY_SPEC],
-        out_specs=(VMEM_SPEC, ANY_SPEC),
-        scratch_shapes=[pltpu.SemaphoreType.DMA((2,))],
+        out_specs=(VMEM_SPEC, ANY_SPEC, ANY_SPEC),
+        scratch_shapes=[pltpu.VMEM(half_readout, BF16), pltpu.SemaphoreType.DMA((3,))],
         input_output_aliases={4: 1},
         compiler_params=PARAMS,
     )(queries, new_a, move(new_a, sibling), new_d, new_weights)
-
-
-    return pl.pallas_call(
+    new_weights, readout = pl.pallas_call(
         down_kernel,
-        out_shape=(
-            jax.ShapeDtypeStruct(queries.shape, BF16),
-            jax.ShapeDtypeStruct(fast_weights.shape, BF16),
-        ),
-        in_specs=[VMEM_SPEC] * 3 + [ANY_SPEC],
-        out_specs=(VMEM_SPEC, ANY_SPEC),
-        scratch_shapes=[pltpu.SemaphoreType.DMA((1,))],
-        input_output_aliases={3: 1},
-        compiler_params=PARAMS,
-    )(hidden, new_d, move(new_d, sibling), new_weights)
+        out_shape=(out_weights, out_readout),
+        in_specs=[VMEM_SPEC] * 2 + [ANY_SPEC] * 2,
+        out_specs=(ANY_SPEC, ANY_SPEC),
+        scratch_shapes=[pltpu.VMEM(half_readout, BF16), pltpu.SemaphoreType.DMA((2,))],
+        input_output_aliases={2: 0, 3: 1},
+        compiler_params=PARAMS,
+    )(hidden, move(new_d, sibling), new_weights, readout)
+    return readout, new_weights
 
 
 def solution(mesh):

time: 61 us -> 60 us (0.984)
  starting transfers between devices: 25.9 us -> 24.6 us
  waiting for transfers between devices: 15.6 us -> 16.4 us
    ppermute x20, starting transfers between devices: 25.9 us -> 24.6 us  [move(): return lax.ppermute(value, 'tok', pairs)]
    ppermute x20, waiting for transfers between devices: 15.6 us -> 16.4 us  [move(): return lax.ppermute(value, 'tok', pairs)]
    pallas_call x3 -> x4, Pallas kernels: 4.52 us -> 4.04 us  [the longest x1 1.62 us: body(): pl.pallas_call(gate_up_kernel, out_shape=(jax.ShapeDtypeStruct(half_reado...]
  transfers between devices with their start and end apart: 20 -> 20, of which waited for: 10 -> 9; matrix products, arithmetic and copies ran while one was open for 0% -> 0% of each run, Pallas kernels for 17% -> 18%
where the time goes in v4:
time: 60 us; the launch traced here: 59.8 us
  starting transfers between devices  24.6 us (41%)
  waiting for transfers between devices  16.4 us (27%)
  Pallas kernels  14.9 us (25%)
  local copies, waits for them, and re-layouts  2.85 us (5%)
  between operations  0.76 us (1%)
    ppermute x20, starting transfers between devices, move(): return lax.ppermute(value, 'tok', pairs)  24.6 us
    ppermute x20, waiting for transfers between devices, move(): return lax.ppermute(value, 'tok', pairs)  16.4 us
    pallas_call x2, Pallas kernels, updated(): pl.pallas_call(functools.partial(ns_kernel, which, earlier), out_shape=ou...  7.39 us
    unnamed x6, local copies, waits for them, and re-layouts  2.85 us
    pallas_call x1, Pallas kernels, body(): pl.pallas_call(pack_kernel, out_shape=(pair, pair), in_specs=[ANY_SPEC] *...  1.96 us
    pallas_call x1, Pallas kernels, body(): pl.pallas_call(gate_up_kernel, out_shape=(jax.ShapeDtypeStruct(half_reado...  1.62 us
    pallas_call x1, Pallas kernels, body(): pl.pallas_call(near_kernel, out_shape=(three32, three32, jax.ShapeDtypeSt...  1.55 us
  transfers between devices with their start and end apart: 20, of which 9 were waited for; matrix products, arithmetic and copies ran while one was open for 0% of the time, Pallas kernels for 18%

profile of v4, /device:TPU:0, one launch (start us, length us, event | category | flops | bytes accessed | tf_op | source)
XLA Modules:
  0.0 59.8 jit_solution(524660478840197089)
XLA Ops:
  0.6 2.0 %shard_map.68 = (bf16[2,128,512]{2,1,0:T(8,128)(2,1)}, bf16[2,128,512]{2,1,0:T(8,128)(2,1)}) custom-call(bf16[128,1024]{1,0:T(8,128)(2,1)} %keys.1, bf16[128,1024]{1,0:T(8,128)(2,1)} %values.1, f32[2,128]{1,0:T(2,128)} %rates.1), custom_call_target="tpu_custom_call" | custom-call | tf_op jit(solution)/shard_map/pallas_call | solution.py:265
  2.6 0.5 collective-permute-start
  3.1 2.6 %collective-permute-start.1 = (bf16[2,128,512]{2,1,0:T(8,128)(2,1)}, bf16[2,128,512]{2,1,0:T(8,128)(2,1)S(1)}, u32[]{:S(2)}, u32[]{:S(2)}) collective-permute-start(bf16[2,128,512]{2,1,0:T(8,128)(2,1)} %get-tuple-element.26.t0), channel_id=1, source_target_pairs={{0,2},{1,5},{2,0},{3,7},{4,6},{5,1},{6,4},{7,3},{8,10},{9,13},{10,... | collective-permute-start | bytes 786440 | tf_op jit(solution)/shard_map/ppermute | solution.py:259
  5.7 0.1 collective-permute-start.2
  5.8 0.0 collective-permute-done.t1
  5.8 1.9 %copy-done = bf16[2,3,512,512]{3,2,1,0:T(8,128)(2,1)S(1)} copy-done((bf16[2,3,512,512]{3,2,1,0:T(8,128)(2,1)S(1)}, bf16[2,3,512,512]{3,2,1,0:T(8,128)(2,1)}, u32[]{:S(2)}) %copy-start) | copy-done | bytes 3145752
  7.7 0.9 %copy-done.1 = bf16[2,128,512]{2,1,0:T(8,128)(2,1)S(1)} copy-done((bf16[2,128,512]{2,1,0:T(8,128)(2,1)S(1)}, bf16[2,128,512]{2,1,0:T(8,128)(2,1)}, u32[]{:S(2)}) %copy-start.1) | copy-done | bytes 262168
  8.7 1.5 %shard_map.69 = (f32[3,512,128]{2,1,0:T(8,128)S(1)}, f32[3,512,128]{2,1,0:T(8,128)S(1)}, bf16[3,512,512]{2,1,0:T(8,128)(2,1)S(1)}) custom-call(bf16[2,128,512]{2,1,0:T(8,128)(2,1)S(1)} %copy-done.1, bf16[2,128,512]{2,1,0:T(8,128)(2,1)S(1)} %collective-permute-done.t1, bf16[2,3,512,512]{3,2,1,0:T(8,128)(2,1)S(1)} %copy-done), custom_call_target="tpu_custom_call" | custom-call | tf_op jit(solution)/shard_map/pallas_call | solution.py:281
  10.2 2.0 %collective-permute-done.1.t2 = bf16[2,128,512]{2,1,0:T(8,128)(2,1)S(1)} collective-permute-done((bf16[2,128,512]{2,1,0:T(8,128)(2,1)}, bf16[2,128,512]{2,1,0:T(8,128)(2,1)S(1)}, u32[]{:S(2)}, u32[]{:S(2)}) %collective-permute-start.1) | collective-permute-done | bytes 262176 | tf_op jit(solution)/shard_map/ppermute | solution.py:259
  12.2 0.8 %collective-permute-done.2.t3 = bf16[2,128,512]{2,1,0:T(8,128)(2,1)S(1)} collective-permute-done((bf16[2,128,512]{2,1,0:T(8,128)(2,1)}, bf16[2,128,512]{2,1,0:T(8,128)(2,1)S(1)}, u32[]{:S(2)}, u32[]{:S(2)}) %collective-permute-start.2) | collective-permute-done | bytes 262176 | tf_op jit(solution)/shard_map/ppermute | solution.py:259
  13.1 1.1 %shard_map.70 = (bf16[512,128]{1,0:T(8,128)(2,1)S(1)}, f32[512,128]{1,0:T(8,128)S(1)}, bf16[256,256]{1,0:T(8,128)(2,1)S(1)}, bf16[256,256]{1,0:T(8,128)(2,1)S(1)...) custom-call(bf16[2,128,512]{2,1,0:T(8,128)(2,1)S(1)} %collective-permute-done.1.t2, ...), custom_call_target="tpu_custom_call" | custom-call | tf_op jit(solution)/shard_map/pallas_call | solution.py:291
  14.2 2.1 %collective-permute-start.3 = (bf16[512,128]{1,0:T(8,128)(2,1)S(1)}, bf16[512,128]{1,0:T(8,128)(2,1)S(1)}, u32[]{:S(2)}, u32[]{:S(2)}) collective-permute-start(bf16[512,128]{1,0:T(8,128)(2,1)S(1)} %get-tuple-element.32), channel_id=1, source_target_pairs={{0,4},{1,3},{2,6},{3,1},{4,0},{5,7},{6,2},{7,5},{8,12},{9,11},{10,... | collective-permute-start | bytes 393224 | tf_op jit(solution)/shard_map/ppermute | solution.py:259
  16.3 0.4 shard_map.71
  16.7 0.1 collective-permute-start.5
  16.8 2.0 %collective-permute-start.9 = (bf16[512,128]{1,0:T(8,128)(2,1)S(1)}, bf16[512,128]{1,0:T(8,128)(2,1)S(1)}, u32[]{:S(2)}, u32[]{:S(2)}) collective-permute-start(bf16[512,128]{1,0:T(8,128)(2,1)S(1)} %get-tuple-element.41), channel_id=1, source_target_pairs={{0,4},{1,3},{2,6},{3,1},{4,0},{5,7},{6,2},{7,5},{8,12},{9,11},{10,... | collective-permute-start | bytes 393224 | tf_op jit(solution)/shard_map/ppermute | solution.py:259
  18.8 0.4 collective-permute-done.3
  19.3 3.1 %collective-permute-start.4 = (bf16[512,128]{1,0:T(8,128)(2,1)S(1)}, bf16[512,128]{1,0:T(8,128)(2,1)S(1)}, u32[]{:S(2)}, u32[]{:S(2)}) collective-permute-start(bf16[512,128]{1,0:T(8,128)(2,1)S(1)} %add_convert_fusion.5), channel_id=1, source_target_pairs={{0,8},{1,9},{2,10},{3,11},{4,12},{5,13},{6,14},{7,15},{8,0},{9,1},... | collective-permute-start | bytes 393224 | tf_op jit(solution)/shard_map/ppermute | solution.py:259
  22.4 2.8 %collective-permute-done.9 = bf16[512,128]{1,0:T(8,128)(2,1)S(1)} collective-permute-done((bf16[512,128]{1,0:T(8,128)(2,1)S(1)}, bf16[512,128]{1,0:T(8,128)(2,1)S(1)}, u32[]{:S(2)}, u32[]{:S(2)}) %collective-permute-start.9) | collective-permute-done | bytes 131104 | tf_op jit(solution)/shard_map/ppermute | solution.py:259
  25.3 2.4 %collective-permute-start.10 = (bf16[512,128]{1,0:T(8,128)(2,1)S(1)}, bf16[512,128]{1,0:T(8,128)(2,1)S(1)}, u32[]{:S(2)}, u32[]{:S(2)}) collective-permute-start(bf16[512,128]{1,0:T(8,128)(2,1)S(1)} %add_convert_fusion.2), channel_id=1, source_target_pairs={{0,8},{1,9},{2,10},{3,11},{4,12},{5,13},{6,14},{7,15},{8,0},{9,1},... | collective-permute-start | bytes 393224 | tf_op jit(solution)/shard_map/ppermute | solution.py:259
  27.6 0.0 collective-permute-done.5
  27.7 3.7 %collective-permute-done.4 = bf16[512,128]{1,0:T(8,128)(2,1)S(1)} collective-permute-done((bf16[512,128]{1,0:T(8,128)(2,1)S(1)}, bf16[512,128]{1,0:T(8,128)(2,1)S(1)}, u32[]{:S(2)}, u32[]{:S(2)}) %collective-permute-start.4) | collective-permute-done | bytes 131104 | tf_op jit(solution)/shard_map/ppermute | solution.py:259
  31.4 1.8 %collective-permute-start.7 = (bf16[512,128]{1,0:T(8,128)(2,1)S(1)}, bf16[512,128]{1,0:T(8,128)(2,1)S(1)}, u32[]{:S(2)}, u32[]{:S(2)}) collective-permute-start(bf16[512,128]{1,0:T(8,128)(2,1)S(1)} %add_convert_fusion.4.refs_0_), channel_id=1, source_target_pairs={{0,2},{1,5},{2,0},{3,7},{4,6},{5,1},{6,4},{7,3},{8,10},{9,13},{10,... | collective-permute-start | bytes 393224 | tf_op jit(solution)/shard_map/ppermute | solution.py:259
  33.2 0.0 collective-permute-start.6
  33.2 3.0 %collective-permute-start.15 = (bf16[512,128]{1,0:T(8,128)(2,1)S(1)}, bf16[512,128]{1,0:T(8,128)(2,1)S(1)}, u32[]{:S(2)}, u32[]{:S(2)}) collective-permute-start(bf16[512,128]{1,0:T(8,128)(2,1)S(1)} %add_convert_fusion.3), channel_id=1, source_target_pairs={{0,8},{1,9},{2,10},{3,11},{4,12},{5,13},{6,14},{7,15},{8,0},{9,1},... | collective-permute-start | bytes 393224 | tf_op jit(solution)/shard_map/ppermute | solution.py:259
  36.2 0.0 collective-permute-done.10
  36.2 1.0 %collective-permute-start.12 = (bf16[512,128]{1,0:T(8,128)(2,1)S(1)}, bf16[512,128]{1,0:T(8,128)(2,1)S(1)}, u32[]{:S(2)}, u32[]{:S(2)}) collective-permute-start(bf16[512,128]{1,0:T(8,128)(2,1)S(1)} %add_convert_fusion.1.refs_4_), channel_id=1, source_target_pairs={{0,2},{1,5},{2,0},{3,7},{4,6},{5,1},{6,4},{7,3},{8,10},{9,13},{10,... | collective-permute-start | bytes 393224 | tf_op jit(solution)/shard_map/ppermute | solution.py:259
  37.2 0.0 collective-permute-start.11
  37.2 2.9 %collective-permute-done.15 = bf16[512,128]{1,0:T(8,128)(2,1)S(1)} collective-permute-done((bf16[512,128]{1,0:T(8,128)(2,1)S(1)}, bf16[512,128]{1,0:T(8,128)(2,1)S(1)}, u32[]{:S(2)}, u32[]{:S(2)}) %collective-permute-start.15) | collective-permute-done | bytes 131104 | tf_op jit(solution)/shard_map/ppermute | solution.py:259
  40.2 1.8 %collective-permute-start.16 = (bf16[512,128]{1,0:T(8,128)(2,1)S(1)}, bf16[512,128]{1,0:T(8,128)(2,1)S(1)}, u32[]{:S(2)}, u32[]{:S(2)}) collective-permute-start(bf16[512,128]{1,0:T(8,128)(2,1)S(1)} %add_convert_fusion.refs_0_), channel_id=1, source_target_pairs={{0,4},{1,3},{2,6},{3,1},{4,0},{5,7},{6,2},{7,5},{8,12},{9,11},{10,... | collective-permute-start | bytes 393224 | tf_op jit(solution)/shard_map/ppermute | solution.py:259
  42.0 0.0 collective-permute-done.6.refs_1_
  42.0 1.0 %collective-permute-start.8 = (bf16[512,128]{1,0:T(8,128)(2,1)S(1)}, bf16[512,128]{1,0:T(8,128)(2,1)S(1)}, u32[]{:S(2)}, u32[]{:S(2)}) collective-permute-start(bf16[512,128]{1,0:T(8,128)(2,1)S(1)} %collective-permute-done.6.refs_1_), channel_id=1, source_target_pairs={{0,2},{1,5},{2,0},{3,7},{4,6},{5,1},{6,4},{7,3},{8,10},{9,13},{10,... | collective-permute-start | bytes 393224 | tf_op jit(solution)/shard_map/ppermute | solution.py:259
  43.0 1.2 %collective-permute-done.11.refs_5_ = bf16[512,128]{1,0:T(8,128)(2,1)S(1)} collective-permute-done((bf16[512,128]{1,0:T(8,128)(2,1)S(1)}, bf16[512,128]{1,0:T(8,128)(2,1)S(1)}, u32[]{:S(2)}, u32[]{:S(2)}) %collective-permute-start.11) | collective-permute-done | bytes 131104 | tf_op jit(solution)/shard_map/ppermute | solution.py:259
  44.2 0.4 collective-permute-start.13
  44.6 1.6 %collective-permute-start.17 = (bf16[512,128]{1,0:T(8,128)(2,1)S(1)}, bf16[512,128]{1,0:T(8,128)(2,1)S(1)}, u32[]{:S(2)}, u32[]{:S(2)}) collective-permute-start(bf16[512,128]{1,0:T(8,128)(2,1)S(1)} %add_convert_fusion.refs_0_), channel_id=1, source_target_pairs={{0,2},{1,5},{2,0},{3,7},{4,6},{5,1},{6,4},{7,3},{8,10},{9,13},{10,... | collective-permute-start | bytes 393224 | tf_op jit(solution)/shard_map/ppermute | solution.py:259
  46.2 0.8 %collective-permute-done.16.refs_1_ = bf16[512,128]{1,0:T(8,128)(2,1)S(1)} collective-permute-done((bf16[512,128]{1,0:T(8,128)(2,1)S(1)}, bf16[512,128]{1,0:T(8,128)(2,1)S(1)}, u32[]{:S(2)}, u32[]{:S(2)}) %collective-permute-start.16) | collective-permute-done | bytes 131104 | tf_op jit(solution)/shard_map/ppermute | solution.py:259
  47.0 0.4 collective-permute-start.18
  47.4 0.0 collective-permute-done.12.refs_6_
  47.4 1.7 %collective-permute-done.13.refs_7_ = bf16[512,128]{1,0:T(8,128)(2,1)S(1)} collective-permute-done((bf16[512,128]{1,0:T(8,128)(2,1)S(1)}, bf16[512,128]{1,0:T(8,128)(2,1)S(1)}, u32[]{:S(2)}, u32[]{:S(2)}) %collective-permute-start.13) | collective-permute-done | bytes 131104 | tf_op jit(solution)/shard_map/ppermute | solution.py:259
  49.2 4.6 %shard_map.72.refs_4_.own = bf16[2,512,512]{2,1,0:T(8,128)(2,1)S(1)} custom-call(bf16[3,512,512]{2,1,0:T(8,128)(2,1)S(1)} %get-tuple-element.28.mine, bf16[512,128]{1,0:T(8,128)(2,1)S(1)} %add_convert_fusion.4.refs_0_, bf16[512,128]{1,0:T(8,128)(2,1)S(1)} %collective-permute-done.6.refs_1_, bf16[512,128]{1,0:T(8,128)(2,1)S(1)} %collective-permute-done.7.refs_2_, ...), custom_call_target="tpu_custom_call" | custom-call | flops 64424509440 | bytes 33554432 | tf_op jit(solution)/shard_map/pallas_call | solution.py:193
  53.8 0.0 copy-start.2
  53.8 0.1 collective-permute-start.14
  53.9 0.0 collective-permute-done.18.refs_3_
  53.9 2.7 %shard_map.73 = (bf16[1,512,512]{2,1,0:T(8,128)(2,1)S(1)}, bf16[2,3,512,512]{3,2,1,0:T(8,128)(2,1)}) custom-call(bf16[3,512,512]{2,1,0:T(8,128)(2,1)S(1)} %get-tuple-element.28.mine, bf16[512,128]{1,0:T(8,128)(2,1)S(1)} %add_convert_fusion.refs_0_, bf16[512,128]{1,0:T(8,128)(2,1)S(1)} %collective-permute-done.16.refs_1_, ...), custom_call_target="tpu_custom_call" | custom-call | flops 32212254720 | bytes 16777216 | tf_op jit(solution)/shard_map/pallas_call | solution.py:193
  56.7 0.5 collective-permute-start.19
  57.2 0.0 collective-permute-done.14.other
  57.2 1.6 %shard_map.74 = (bf16[128,512]{1,0:T(8,128)(2,1)S(1)}, bf16[2,3,512,512]{3,2,1,0:T(8,128)(2,1)}, bf16[128,1024]{1,0:T(8,128)(2,1)}) custom-call(bf16[128,1024]{1,0:T(8,128)(2,1)S(1)} %copy-done.2, bf16[2,512,512]{2,1,0:T(8,128)(2,1)S(1)} %shard_map.72.refs_4_.own, ...), custom_call_target="tpu_custom_call", output_to_operand_aliasing={{1}: (4, {})} | custom-call | tf_op jit(solution)/shard_map/pallas_call | solution.py:331
  58.9 0.0 collective-permute-done.19.other
  58.9 0.9 %shard_map.75 = (bf16[2,3,512,512]{3,2,1,0:T(8,128)(2,1)}, bf16[128,1024]{1,0:T(8,128)(2,1)}) custom-call(bf16[128,512]{1,0:T(8,128)(2,1)S(1)} %get-tuple-element.45.hidden, bf16[1,512,512]{2,1,0:T(8,128)(2,1)S(1)} %collective-permute-done.19.other, bf16[2,3,512,512]{3,2,1,0:T(8,128)(2,1)} %get-tuple-element.46.held, ...), custom_call_target="tpu_custom_call", output_to_operand_aliasing={{0}: (2, {}), {1}: (3, {})} | custom-call | tf_op jit(solution)/shard_map/pallas_call | solution.py:340
  (12 shorter events, 0.2 us)
Async XLA Ops:
  2.6 3.2 %collective-permute-start = (bf16[2,128,512]{2,1,0:T(8,128)(2,1)}, bf16[2,128,512]{2,1,0:T(8,128)(2,1)S(1)}, u32[]{:S(2)}, u32[]{:S(2)}) collective-permute-start(bf16[2,128,512]{2,1,0:T(8,128)(2,1)} %get-tuple-element.27), channel_id=1, source_target_pairs={{0,1},{1,0},{2,3},{3,2},{4,5},{5,4},{6,7},{7,6},{8,9},{9,8},{10,11... | collective-permute-start | bytes 786440 | tf_op jit(solution)/shard_map/ppermute | solution.py:259
  3.1 9.1 %collective-permute-start.1 = (bf16[2,128,512]{2,1,0:T(8,128)(2,1)}, bf16[2,128,512]{2,1,0:T(8,128)(2,1)S(1)}, u32[]{:S(2)}, u32[]{:S(2)}) collective-permute-start(bf16[2,128,512]{2,1,0:T(8,128)(2,1)} %get-tuple-element.26.t0), channel_id=1, source_target_pairs={{0,2},{1,5},{2,0},{3,7},{4,6},{5,1},{6,4},{7,3},{8,10},{9,13},{10,... | collective-permute-start | bytes 786440 | tf_op jit(solution)/shard_map/ppermute | solution.py:259
  5.7 7.4 %collective-permute-start.2 = (bf16[2,128,512]{2,1,0:T(8,128)(2,1)}, bf16[2,128,512]{2,1,0:T(8,128)(2,1)S(1)}, u32[]{:S(2)}, u32[]{:S(2)}) collective-permute-start(bf16[2,128,512]{2,1,0:T(8,128)(2,1)} %get-tuple-element.27), channel_id=1, source_target_pairs={{0,5},{1,2},{2,7},{3,0},{4,1},{5,6},{6,3},{7,4},{8,13},{9,10},{10,... | collective-permute-start | bytes 786440 | tf_op jit(solution)/shard_map/ppermute | solution.py:259
  5.8 1.9 %copy-start = (bf16[2,3,512,512]{3,2,1,0:T(8,128)(2,1)S(1)}, bf16[2,3,512,512]{3,2,1,0:T(8,128)(2,1)}, u32[]{:S(2)}) copy-start(bf16[2,3,512,512]{3,2,1,0:T(8,128)(2,1)} %weights.1) | copy-start | bytes 9437188
  7.7 0.9 %copy-start.1 = (bf16[2,128,512]{2,1,0:T(8,128)(2,1)S(1)}, bf16[2,128,512]{2,1,0:T(8,128)(2,1)}, u32[]{:S(2)}) copy-start(bf16[2,128,512]{2,1,0:T(8,128)(2,1)} %get-tuple-element.26.t0) | copy-start | bytes 786436
  14.2 5.1 %collective-permute-start.3 = (bf16[512,128]{1,0:T(8,128)(2,1)S(1)}, bf16[512,128]{1,0:T(8,128)(2,1)S(1)}, u32[]{:S(2)}, u32[]{:S(2)}) collective-permute-start(bf16[512,128]{1,0:T(8,128)(2,1)S(1)} %get-tuple-element.32), channel_id=1, source_target_pairs={{0,4},{1,3},{2,6},{3,1},{4,0},{5,7},{6,2},{7,5},{8,12},{9,11},{10,... | collective-permute-start | bytes 393224 | tf_op jit(solution)/shard_map/ppermute | solution.py:259
  16.7 10.9 %collective-permute-start.5 = (bf16[512,128]{1,0:T(8,128)(2,1)S(1)}, bf16[512,128]{1,0:T(8,128)(2,1)S(1)}, u32[]{:S(2)}, u32[]{:S(2)}) collective-permute-start(bf16[512,128]{1,0:T(8,128)(2,1)S(1)} %get-tuple-element.38), channel_id=1, source_target_pairs={{0,4},{1,3},{2,6},{3,1},{4,0},{5,7},{6,2},{7,5},{8,12},{9,11},{10,... | collective-permute-start | bytes 393224 | tf_op jit(solution)/shard_map/ppermute | solution.py:259
  16.8 8.4 %collective-permute-start.9 = (bf16[512,128]{1,0:T(8,128)(2,1)S(1)}, bf16[512,128]{1,0:T(8,128)(2,1)S(1)}, u32[]{:S(2)}, u32[]{:S(2)}) collective-permute-start(bf16[512,128]{1,0:T(8,128)(2,1)S(1)} %get-tuple-element.41), channel_id=1, source_target_pairs={{0,4},{1,3},{2,6},{3,1},{4,0},{5,7},{6,2},{7,5},{8,12},{9,11},{10,... | collective-permute-start | bytes 393224 | tf_op jit(solution)/shard_map/ppermute | solution.py:259
  19.3 12.1 %collective-permute-start.4 = (bf16[512,128]{1,0:T(8,128)(2,1)S(1)}, bf16[512,128]{1,0:T(8,128)(2,1)S(1)}, u32[]{:S(2)}, u32[]{:S(2)}) collective-permute-start(bf16[512,128]{1,0:T(8,128)(2,1)S(1)} %add_convert_fusion.5), channel_id=1, source_target_pairs={{0,8},{1,9},{2,10},{3,11},{4,12},{5,13},{6,14},{7,15},{8,0},{9,1},... | collective-permute-start | bytes 393224 | tf_op jit(solution)/shard_map/ppermute | solution.py:259
  25.3 10.9 %collective-permute-start.10 = (bf16[512,128]{1,0:T(8,128)(2,1)S(1)}, bf16[512,128]{1,0:T(8,128)(2,1)S(1)}, u32[]{:S(2)}, u32[]{:S(2)}) collective-permute-start(bf16[512,128]{1,0:T(8,128)(2,1)S(1)} %add_convert_fusion.2), channel_id=1, source_target_pairs={{0,8},{1,9},{2,10},{3,11},{4,12},{5,13},{6,14},{7,15},{8,0},{9,1},... | collective-permute-start | bytes 393224 | tf_op jit(solution)/shard_map/ppermute | solution.py:259
  31.4 13.2 %collective-permute-start.7 = (bf16[512,128]{1,0:T(8,128)(2,1)S(1)}, bf16[512,128]{1,0:T(8,128)(2,1)S(1)}, u32[]{:S(2)}, u32[]{:S(2)}) collective-permute-start(bf16[512,128]{1,0:T(8,128)(2,1)S(1)} %add_convert_fusion.4.refs_0_), channel_id=1, source_target_pairs={{0,2},{1,5},{2,0},{3,7},{4,6},{5,1},{6,4},{7,3},{8,10},{9,13},{10,... | collective-permute-start | bytes 393224 | tf_op jit(solution)/shard_map/ppermute | solution.py:259
  33.2 8.8 %collective-permute-start.6 = (bf16[512,128]{1,0:T(8,128)(2,1)S(1)}, bf16[512,128]{1,0:T(8,128)(2,1)S(1)}, u32[]{:S(2)}, u32[]{:S(2)}) collective-permute-start(bf16[512,128]{1,0:T(8,128)(2,1)S(1)} %add_convert_fusion.4.refs_0_), channel_id=1, source_target_pairs={{0,4},{1,3},{2,6},{3,1},{4,0},{5,7},{6,2},{7,5},{8,12},{9,11},{10,... | collective-permute-start | bytes 393224 | tf_op jit(solution)/shard_map/ppermute | solution.py:259
  33.2 6.9 %collective-permute-start.15 = (bf16[512,128]{1,0:T(8,128)(2,1)S(1)}, bf16[512,128]{1,0:T(8,128)(2,1)S(1)}, u32[]{:S(2)}, u32[]{:S(2)}) collective-permute-start(bf16[512,128]{1,0:T(8,128)(2,1)S(1)} %add_convert_fusion.3), channel_id=1, source_target_pairs={{0,8},{1,9},{2,10},{3,11},{4,12},{5,13},{6,14},{7,15},{8,0},{9,1},... | collective-permute-start | bytes 393224 | tf_op jit(solution)/shard_map/ppermute | solution.py:259
  36.2 11.2 %collective-permute-start.12 = (bf16[512,128]{1,0:T(8,128)(2,1)S(1)}, bf16[512,128]{1,0:T(8,128)(2,1)S(1)}, u32[]{:S(2)}, u32[]{:S(2)}) collective-permute-start(bf16[512,128]{1,0:T(8,128)(2,1)S(1)} %add_convert_fusion.1.refs_4_), channel_id=1, source_target_pairs={{0,2},{1,5},{2,0},{3,7},{4,6},{5,1},{6,4},{7,3},{8,10},{9,13},{10,... | collective-permute-start | bytes 393224 | tf_op jit(solution)/shard_map/ppermute | solution.py:259
  37.2 7.0 %collective-permute-start.11 = (bf16[512,128]{1,0:T(8,128)(2,1)S(1)}, bf16[512,128]{1,0:T(8,128)(2,1)S(1)}, u32[]{:S(2)}, u32[]{:S(2)}) collective-permute-start(bf16[512,128]{1,0:T(8,128)(2,1)S(1)} %add_convert_fusion.1.refs_4_), channel_id=1, source_target_pairs={{0,4},{1,3},{2,6},{3,1},{4,0},{5,7},{6,2},{7,5},{8,12},{9,11},{10,... | collective-permute-start | bytes 393224 | tf_op jit(solution)/shard_map/ppermute | solution.py:259
  40.2 6.8 %collective-permute-start.16 = (bf16[512,128]{1,0:T(8,128)(2,1)S(1)}, bf16[512,128]{1,0:T(8,128)(2,1)S(1)}, u32[]{:S(2)}, u32[]{:S(2)}) collective-permute-start(bf16[512,128]{1,0:T(8,128)(2,1)S(1)} %add_convert_fusion.refs_0_), channel_id=1, source_target_pairs={{0,4},{1,3},{2,6},{3,1},{4,0},{5,7},{6,2},{7,5},{8,12},{9,11},{10,... | collective-permute-start | bytes 393224 | tf_op jit(solution)/shard_map/ppermute | solution.py:259
  42.0 5.4 %collective-permute-start.8 = (bf16[512,128]{1,0:T(8,128)(2,1)S(1)}, bf16[512,128]{1,0:T(8,128)(2,1)S(1)}, u32[]{:S(2)}, u32[]{:S(2)}) collective-permute-start(bf16[512,128]{1,0:T(8,128)(2,1)S(1)} %collective-permute-done.6.refs_1_), channel_id=1, source_target_pairs={{0,2},{1,5},{2,0},{3,7},{4,6},{5,1},{6,4},{7,3},{8,10},{9,13},{10,... | collective-permute-start | bytes 393224 | tf_op jit(solution)/shard_map/ppermute | solution.py:259
  44.2 5.0 %collective-permute-start.13 = (bf16[512,128]{1,0:T(8,128)(2,1)S(1)}, bf16[512,128]{1,0:T(8,128)(2,1)S(1)}, u32[]{:S(2)}, u32[]{:S(2)}) collective-permute-start(bf16[512,128]{1,0:T(8,128)(2,1)S(1)} %collective-permute-done.11.refs_5_), channel_id=1, source_target_pairs={{0,2},{1,5},{2,0},{3,7},{4,6},{5,1},{6,4},{7,3},{8,10},{9,13},{10,... | collective-permute-start | bytes 393224 | tf_op jit(solution)/shard_map/ppermute | solution.py:259
  44.6 9.3 %collective-permute-start.17 = (bf16[512,128]{1,0:T(8,128)(2,1)S(1)}, bf16[512,128]{1,0:T(8,128)(2,1)S(1)}, u32[]{:S(2)}, u32[]{:S(2)}) collective-permute-start(bf16[512,128]{1,0:T(8,128)(2,1)S(1)} %add_convert_fusion.refs_0_), channel_id=1, source_target_pairs={{0,2},{1,5},{2,0},{3,7},{4,6},{5,1},{6,4},{7,3},{8,10},{9,13},{10,... | collective-permute-start | bytes 393224 | tf_op jit(solution)/shard_map/ppermute | solution.py:259
  47.0 6.9 %collective-permute-start.18 = (bf16[512,128]{1,0:T(8,128)(2,1)S(1)}, bf16[512,128]{1,0:T(8,128)(2,1)S(1)}, u32[]{:S(2)}, u32[]{:S(2)}) collective-permute-start(bf16[512,128]{1,0:T(8,128)(2,1)S(1)} %collective-permute-done.16.refs_1_), channel_id=1, source_target_pairs={{0,2},{1,5},{2,0},{3,7},{4,6},{5,1},{6,4},{7,3},{8,10},{9,13},{10,... | collective-permute-start | bytes 393224 | tf_op jit(solution)/shard_map/ppermute | solution.py:259
  53.8 3.4 %copy-start.2 = (bf16[128,1024]{1,0:T(8,128)(2,1)S(1)}, bf16[128,1024]{1,0:T(8,128)(2,1)}, u32[]{:S(2)}) copy-start(bf16[128,1024]{1,0:T(8,128)(2,1)} %queries.1) | copy-start | bytes 786436
  53.8 3.4 %collective-permute-start.14 = (bf16[2,512,512]{2,1,0:T(8,128)(2,1)S(1)}, bf16[2,512,512]{2,1,0:T(8,128)(2,1)S(1)}, u32[]{:S(2)}, u32[]{:S(2)}) collective-permute-start(bf16[2,512,512]{2,1,0:T(8,128)(2,1)S(1)} %shard_map.72.refs_4_.own), channel_id=1, source_target_pairs={{0,1},{1,0},{2,3},{3,2},{4,5},{5,4},{6,7},{7,6},{8,9},{9,8},{10,11... | collective-permute-start | bytes 3145736 | tf_op jit(solution)/shard_map/ppermute | solution.py:259
  56.7 2.2 %collective-permute-start.19 = (bf16[1,512,512]{2,1,0:T(8,128)(2,1)S(1)}, bf16[1,512,512]{2,1,0:T(8,128)(2,1)S(1)}, u32[]{:S(2)}, u32[]{:S(2)}) collective-permute-start(bf16[1,512,512]{2,1,0:T(8,128)(2,1)S(1)} %get-tuple-element.43.own_down), channel_id=1, source_target_pairs={{0,1},{1,0},{2,3},{3,2},{4,5},{5,4},{6,7},{7,6},{8,9},{9,8},{10,11... | collective-permute-start | bytes 1572872 | tf_op jit(solution)/shard_map/ppermute | solution.py:259

commit v5 on v4

--- a/solution.py
+++ b/solution.py
@@ -313,15 +313,24 @@
             part = (part.astype(F32) + move(part, pairs).astype(F32)).astype(BF16)
         return part
 
+    along_1 = [(i, i ^ 2) for i in range(size)]
+    on_0 = place()[0] == 0
+
+    def mixed(part):
+        over_second, over_first = move(part, second), move(part, first)
+        last = move(jnp.where(on_0, over_second, over_first), along_1)
+        return part, over_second, over_first, last
+
     def pieces(part):
         over = move(part, second)
         return part, over, move(part, first), move(over, first)
 
-    parts = [reduced(at) for at in range(3)]
+    pair = move(jnp.stack(send[1:]), second)
+    parts = [reduced(0)] + [(keep[1 + at] + pair[at].astype(F32)).astype(BF16) for at in range(2)]
     sums = [crossed(parts[0]), crossed(parts[1])]
     sums[0], parts[2] = tie(sums[0], parts[2])
     sums.append(crossed(parts[2]))
-    four = [pieces(sums[0]), pieces(sums[1]), pieces(sums[2])]
+    four = [mixed(sums[0]), mixed(sums[1]), pieces(sums[2])]
     (new_a,) = updated((0, 1), four[:2], mine)
     new_d, new_weights = updated((2,), four[2:], mine, (0, 1), new_a)
 

time: 60 us -> 59.2 us (0.987)
  starting transfers between devices: 24.6 us -> 23.9 us
    ppermute x20 -> x19, starting transfers between devices: 24.6 us -> 23.9 us  [move(): return lax.ppermute(value, 'tok', pairs)]
    ppermute x20 -> x19, waiting for transfers between devices: 16.4 us -> 16.3 us  [move(): return lax.ppermute(value, 'tok', pairs)]
  transfers between devices with their start and end apart: 20 -> 19, of which waited for: 9 -> 9; matrix products, arithmetic and copies ran while one was open for 0% -> 0% of each run, Pallas kernels for 18% -> 19%
where the time goes in v5:
time: 59.2 us; the launch traced here: 59 us
  starting transfers between devices  23.9 us (40%)
  waiting for transfers between devices  16.3 us (28%)
  Pallas kernels  14.9 us (25%)
  local copies, waits for them, and re-layouts  2.85 us (5%)
  between operations  0.79 us (1%)
    ppermute x19, starting transfers between devices, move(): return lax.ppermute(value, 'tok', pairs)  23.9 us
    ppermute x19, waiting for transfers between devices, move(): return lax.ppermute(value, 'tok', pairs)  16.3 us
    pallas_call x2, Pallas kernels, updated(): pl.pallas_call(functools.partial(ns_kernel, which, earlier), out_shape=ou...  7.39 us
    unnamed x6, local copies, waits for them, and re-layouts  2.85 us
    pallas_call x1, Pallas kernels, body(): pl.pallas_call(pack_kernel, out_shape=(pair, pair), in_specs=[ANY_SPEC] *...  1.96 us
    pallas_call x1, Pallas kernels, body(): pl.pallas_call(gate_up_kernel, out_shape=(jax.ShapeDtypeStruct(half_reado...  1.63 us
    pallas_call x1, Pallas kernels, body(): pl.pallas_call(near_kernel, out_shape=(three32, three32, jax.ShapeDtypeSt...  1.55 us
  transfers between devices with their start and end apart: 19, of which 9 were waited for; matrix products, arithmetic and copies ran while one was open for 0% of the time, Pallas kernels for 19%

profile of v5, /device:TPU:0, one launch (start us, length us, event | category | flops | bytes accessed | tf_op | source)
XLA Modules:
  0.0 59.0 jit_solution(11133564055053280163)
XLA Ops:
  0.6 2.0 %shard_map.68 = (bf16[2,128,512]{2,1,0:T(8,128)(2,1)}, bf16[2,128,512]{2,1,0:T(8,128)(2,1)}) custom-call(bf16[128,1024]{1,0:T(8,128)(2,1)} %keys.1, bf16[128,1024]{1,0:T(8,128)(2,1)} %values.1, f32[2,128]{1,0:T(2,128)} %rates.1), custom_call_target="tpu_custom_call" | custom-call | tf_op jit(solution)/shard_map/pallas_call | solution.py:265
  2.6 0.5 collective-permute-start
  3.1 2.6 %collective-permute-start.1 = (bf16[2,128,512]{2,1,0:T(8,128)(2,1)}, bf16[2,128,512]{2,1,0:T(8,128)(2,1)S(1)}, u32[]{:S(2)}, u32[]{:S(2)}) collective-permute-start(bf16[2,128,512]{2,1,0:T(8,128)(2,1)} %get-tuple-element.26.t0), channel_id=1, source_target_pairs={{0,2},{1,5},{2,0},{3,7},{4,6},{5,1},{6,4},{7,3},{8,10},{9,13},{10,... | collective-permute-start | bytes 786440 | tf_op jit(solution)/shard_map/ppermute | solution.py:259
  5.7 0.1 collective-permute-start.2
  5.8 1.9 %copy-done = bf16[2,3,512,512]{3,2,1,0:T(8,128)(2,1)S(1)} copy-done((bf16[2,3,512,512]{3,2,1,0:T(8,128)(2,1)S(1)}, bf16[2,3,512,512]{3,2,1,0:T(8,128)(2,1)}, u32[]{:S(2)}) %copy-start) | copy-done | bytes 3145752
  7.7 0.9 %copy-done.1 = bf16[2,128,512]{2,1,0:T(8,128)(2,1)S(1)} copy-done((bf16[2,128,512]{2,1,0:T(8,128)(2,1)S(1)}, bf16[2,128,512]{2,1,0:T(8,128)(2,1)}, u32[]{:S(2)}) %copy-start.1) | copy-done | bytes 262168
  8.7 1.5 %shard_map.69 = (f32[3,512,128]{2,1,0:T(8,128)S(1)}, f32[3,512,128]{2,1,0:T(8,128)S(1)}, bf16[3,512,512]{2,1,0:T(8,128)(2,1)S(1)}) custom-call(bf16[2,128,512]{2,1,0:T(8,128)(2,1)S(1)} %copy-done.1, bf16[2,128,512]{2,1,0:T(8,128)(2,1)S(1)} %collective-permute-done.t1, bf16[2,3,512,512]{3,2,1,0:T(8,128)(2,1)S(1)} %copy-done), custom_call_target="tpu_custom_call" | custom-call | tf_op jit(solution)/shard_map/pallas_call | solution.py:281
  10.2 2.0 %collective-permute-done.1.t2 = bf16[2,128,512]{2,1,0:T(8,128)(2,1)S(1)} collective-permute-done((bf16[2,128,512]{2,1,0:T(8,128)(2,1)}, bf16[2,128,512]{2,1,0:T(8,128)(2,1)S(1)}, u32[]{:S(2)}, u32[]{:S(2)}) %collective-permute-start.1) | collective-permute-done | bytes 262176 | tf_op jit(solution)/shard_map/ppermute | solution.py:259
  12.2 0.8 %collective-permute-done.2.t3 = bf16[2,128,512]{2,1,0:T(8,128)(2,1)S(1)} collective-permute-done((bf16[2,128,512]{2,1,0:T(8,128)(2,1)}, bf16[2,128,512]{2,1,0:T(8,128)(2,1)S(1)}, u32[]{:S(2)}, u32[]{:S(2)}) %collective-permute-start.2) | collective-permute-done | bytes 262176 | tf_op jit(solution)/shard_map/ppermute | solution.py:259
  13.1 1.1 %shard_map.70 = (bf16[512,128]{1,0:T(8,128)(2,1)S(1)}, f32[512,128]{1,0:T(8,128)S(1)}, bf16[256,256]{1,0:T(8,128)(2,1)S(1)}, bf16[256,256]{1,0:T(8,128)(2,1)S(1)...) custom-call(bf16[2,128,512]{2,1,0:T(8,128)(2,1)S(1)} %collective-permute-done.1.t2, ...), custom_call_target="tpu_custom_call" | custom-call | tf_op jit(solution)/shard_map/pallas_call | solution.py:291
  14.2 2.1 %collective-permute-start.3 = (bf16[512,128]{1,0:T(8,128)(2,1)S(1)}, bf16[512,128]{1,0:T(8,128)(2,1)S(1)}, u32[]{:S(2)}, u32[]{:S(2)}) collective-permute-start(bf16[512,128]{1,0:T(8,128)(2,1)S(1)} %get-tuple-element.32), channel_id=1, source_target_pairs={{0,4},{1,3},{2,6},{3,1},{4,0},{5,7},{6,2},{7,5},{8,12},{9,11},{10,... | collective-permute-start | bytes 393224 | tf_op jit(solution)/shard_map/ppermute | solution.py:259
  16.3 0.4 shard_map.71
  16.8 0.1 collective-permute-start.5
  16.9 2.4 %collective-permute-done.3 = bf16[512,128]{1,0:T(8,128)(2,1)S(1)} collective-permute-done((bf16[512,128]{1,0:T(8,128)(2,1)S(1)}, bf16[512,128]{1,0:T(8,128)(2,1)S(1)}, u32[]{:S(2)}, u32[]{:S(2)}) %collective-permute-start.3) | collective-permute-done | bytes 131104 | tf_op jit(solution)/shard_map/ppermute | solution.py:259
  19.3 3.1 %collective-permute-start.4 = (bf16[512,128]{1,0:T(8,128)(2,1)S(1)}, bf16[512,128]{1,0:T(8,128)(2,1)S(1)}, u32[]{:S(2)}, u32[]{:S(2)}) collective-permute-start(bf16[512,128]{1,0:T(8,128)(2,1)S(1)} %add_convert_fusion.3), channel_id=1, source_target_pairs={{0,8},{1,9},{2,10},{3,11},{4,12},{5,13},{6,14},{7,15},{8,0},{9,1},... | collective-permute-start | bytes 393224 | tf_op jit(solution)/shard_map/ppermute | solution.py:259
  22.4 2.9 %collective-permute-done.5 = bf16[2,512,128]{2,1,0:T(8,128)(2,1)S(1)} collective-permute-done((bf16[2,512,128]{2,1,0:T(8,128)(2,1)S(1)}, bf16[2,512,128]{2,1,0:T(8,128)(2,1)S(1)}, u32[]{:S(2)}, u32[]{:S(2)}) %collective-permute-start.5) | collective-permute-done | bytes 262176 | tf_op jit(solution)/shard_map/ppermute | solution.py:259
  25.3 0.1 fusion
  25.4 2.3 %collective-permute-start.9 = (bf16[512,128]{1,0:T(8,128)(2,1)S(1)}, bf16[512,128]{1,0:T(8,128)(2,1)S(1)}, u32[]{:S(2)}, u32[]{:S(2)}) collective-permute-start(bf16[512,128]{1,0:T(8,128)(2,1)S(1)} %get-tuple-element.50), channel_id=1, source_target_pairs={{0,8},{1,9},{2,10},{3,11},{4,12},{5,13},{6,14},{7,15},{8,0},{9,1},... | collective-permute-start | bytes 393224 | tf_op jit(solution)/shard_map/ppermute | solution.py:259
  27.7 3.6 %collective-permute-done.4 = bf16[512,128]{1,0:T(8,128)(2,1)S(1)} collective-permute-done((bf16[512,128]{1,0:T(8,128)(2,1)S(1)}, bf16[512,128]{1,0:T(8,128)(2,1)S(1)}, u32[]{:S(2)}, u32[]{:S(2)}) %collective-permute-start.4) | collective-permute-done | bytes 131104 | tf_op jit(solution)/shard_map/ppermute | solution.py:259
  31.4 1.8 %collective-permute-start.7 = (bf16[512,128]{1,0:T(8,128)(2,1)S(1)}, bf16[512,128]{1,0:T(8,128)(2,1)S(1)}, u32[]{:S(2)}, u32[]{:S(2)}) collective-permute-start(bf16[512,128]{1,0:T(8,128)(2,1)S(1)} %add_convert_fusion.2.refs_0_), channel_id=1, source_target_pairs={{0,2},{1,5},{2,0},{3,7},{4,6},{5,1},{6,4},{7,3},{8,10},{9,13},{10,... | collective-permute-start | bytes 393224 | tf_op jit(solution)/shard_map/ppermute | solution.py:259
  33.2 0.0 collective-permute-start.6
  33.2 2.8 %collective-permute-start.14 = (bf16[512,128]{1,0:T(8,128)(2,1)S(1)}, bf16[512,128]{1,0:T(8,128)(2,1)S(1)}, u32[]{:S(2)}, u32[]{:S(2)}) collective-permute-start(bf16[512,128]{1,0:T(8,128)(2,1)S(1)} %get-tuple-element.42), channel_id=1, source_target_pairs={{0,8},{1,9},{2,10},{3,11},{4,12},{5,13},{6,14},{7,15},{8,0},{9,1},... | collective-permute-start | bytes 393224 | tf_op jit(solution)/shard_map/ppermute | solution.py:259
  36.0 0.0 collective-permute-done.9
  36.1 1.1 %collective-permute-start.11 = (bf16[512,128]{1,0:T(8,128)(2,1)S(1)}, bf16[512,128]{1,0:T(8,128)(2,1)S(1)}, u32[]{:S(2)}, u32[]{:S(2)}) collective-permute-start(bf16[512,128]{1,0:T(8,128)(2,1)S(1)} %add_convert_fusion.1.refs_4_), channel_id=1, source_target_pairs={{0,2},{1,5},{2,0},{3,7},{4,6},{5,1},{6,4},{7,3},{8,10},{9,13},{10,... | collective-permute-start | bytes 393224 | tf_op jit(solution)/shard_map/ppermute | solution.py:259
  37.2 0.0 collective-permute-start.10
  37.2 2.2 %collective-permute-done.14 = bf16[512,128]{1,0:T(8,128)(2,1)S(1)} collective-permute-done((bf16[512,128]{1,0:T(8,128)(2,1)S(1)}, bf16[512,128]{1,0:T(8,128)(2,1)S(1)}, u32[]{:S(2)}, u32[]{:S(2)}) %collective-permute-start.14) | collective-permute-done | bytes 131104 | tf_op jit(solution)/shard_map/ppermute | solution.py:259
  39.4 2.5 %collective-permute-start.15 = (bf16[512,128]{1,0:T(8,128)(2,1)S(1)}, bf16[512,128]{1,0:T(8,128)(2,1)S(1)}, u32[]{:S(2)}, u32[]{:S(2)}) collective-permute-start(bf16[512,128]{1,0:T(8,128)(2,1)S(1)} %add_convert_fusion.refs_0_), channel_id=1, source_target_pairs={{0,4},{1,3},{2,6},{3,1},{4,0},{5,7},{6,2},{7,5},{8,12},{9,11},{10,... | collective-permute-start | bytes 393224 | tf_op jit(solution)/shard_map/ppermute | solution.py:259
  41.9 0.0 collective-permute-done.7.refs_2_
  41.9 0.0 collective-permute-done.6.refs_1_
  41.9 1.1 %collective-permute-start.8 = (bf16[512,128]{1,0:T(8,128)(2,1)S(1)}, bf16[512,128]{1,0:T(8,128)(2,1)S(1)}, u32[]{:S(2)}, u32[]{:S(2)}) collective-permute-start(bf16[512,128]{1,0:T(8,128)(2,1)S(1)} %broadcast_select_fusion.1), channel_id=1, source_target_pairs={{0,2},{1,3},{2,0},{3,1},{4,6},{5,7},{6,4},{7,5},{8,10},{9,11},{10,... | collective-permute-start | bytes 393224 | tf_op jit(solution)/shard_map/ppermute | solution.py:259
  43.0 0.0 collective-permute-done.11.refs_6_
  43.0 0.0 collective-permute-done.10.refs_5_
  43.0 1.1 %collective-permute-start.12 = (bf16[512,128]{1,0:T(8,128)(2,1)S(1)}, bf16[512,128]{1,0:T(8,128)(2,1)S(1)}, u32[]{:S(2)}, u32[]{:S(2)}) collective-permute-start(bf16[512,128]{1,0:T(8,128)(2,1)S(1)} %broadcast_select_fusion), channel_id=1, source_target_pairs={{0,2},{1,3},{2,0},{3,1},{4,6},{5,7},{6,4},{7,5},{8,10},{9,11},{10,... | collective-permute-start | bytes 393224 | tf_op jit(solution)/shard_map/ppermute | solution.py:259
  44.1 1.0 %collective-permute-start.16 = (bf16[512,128]{1,0:T(8,128)(2,1)S(1)}, bf16[512,128]{1,0:T(8,128)(2,1)S(1)}, u32[]{:S(2)}, u32[]{:S(2)}) collective-permute-start(bf16[512,128]{1,0:T(8,128)(2,1)S(1)} %add_convert_fusion.refs_0_), channel_id=1, source_target_pairs={{0,2},{1,5},{2,0},{3,7},{4,6},{5,1},{6,4},{7,3},{8,10},{9,13},{10,... | collective-permute-start | bytes 393224 | tf_op jit(solution)/shard_map/ppermute | solution.py:259
  45.1 0.7 %collective-permute-done.15.refs_1_ = bf16[512,128]{1,0:T(8,128)(2,1)S(1)} collective-permute-done((bf16[512,128]{1,0:T(8,128)(2,1)S(1)}, bf16[512,128]{1,0:T(8,128)(2,1)S(1)}, u32[]{:S(2)}, u32[]{:S(2)}) %collective-permute-start.15) | collective-permute-done | bytes 131104 | tf_op jit(solution)/shard_map/ppermute | solution.py:259
  45.8 0.9 %collective-permute-start.17 = (bf16[512,128]{1,0:T(8,128)(2,1)S(1)}, bf16[512,128]{1,0:T(8,128)(2,1)S(1)}, u32[]{:S(2)}, u32[]{:S(2)}) collective-permute-start(bf16[512,128]{1,0:T(8,128)(2,1)S(1)} %collective-permute-done.15.refs_1_), channel_id=1, source_target_pairs={{0,2},{1,5},{2,0},{3,7},{4,6},{5,1},{6,4},{7,3},{8,10},{9,13},{10,... | collective-permute-start | bytes 393224 | tf_op jit(solution)/shard_map/ppermute | solution.py:259
  46.7 0.2 collective-permute-done.8.refs_3_
  46.9 1.4 %collective-permute-done.12.refs_7_ = bf16[512,128]{1,0:T(8,128)(2,1)S(1)} collective-permute-done((bf16[512,128]{1,0:T(8,128)(2,1)S(1)}, bf16[512,128]{1,0:T(8,128)(2,1)S(1)}, u32[]{:S(2)}, u32[]{:S(2)}) %collective-permute-start.12) | collective-permute-done | bytes 131104 | tf_op jit(solution)/shard_map/ppermute | solution.py:259
  48.3 4.6 %shard_map.72.refs_4_.own = bf16[2,512,512]{2,1,0:T(8,128)(2,1)S(1)} custom-call(bf16[3,512,512]{2,1,0:T(8,128)(2,1)S(1)} %get-tuple-element.28.mine, bf16[512,128]{1,0:T(8,128)(2,1)S(1)} %add_convert_fusion.2.refs_0_, bf16[512,128]{1,0:T(8,128)(2,1)S(1)} %collective-permute-done.6.refs_1_, bf16[512,128]{1,0:T(8,128)(2,1)S(1)} %collective-permute-done.7.refs_2_, ...), custom_call_target="tpu_custom_call" | custom-call | flops 64424509440 | bytes 33554432 | tf_op jit(solution)/shard_map/pallas_call | solution.py:193
  53.0 0.0 copy-start.2
  53.0 0.1 collective-permute-start.13
  53.1 0.0 collective-permute-done.16.refs_2_
  53.1 0.0 collective-permute-done.17.refs_3_
  53.1 2.7 %shard_map.73 = (bf16[1,512,512]{2,1,0:T(8,128)(2,1)S(1)}, bf16[2,3,512,512]{3,2,1,0:T(8,128)(2,1)}) custom-call(bf16[3,512,512]{2,1,0:T(8,128)(2,1)S(1)} %get-tuple-element.28.mine, bf16[512,128]{1,0:T(8,128)(2,1)S(1)} %add_convert_fusion.refs_0_, bf16[512,128]{1,0:T(8,128)(2,1)S(1)} %collective-permute-done.15.refs_1_, ...), custom_call_target="tpu_custom_call" | custom-call | flops 32212254720 | bytes 16777216 | tf_op jit(solution)/shard_map/pallas_call | solution.py:193
  55.9 0.5 collective-permute-start.18
  56.4 0.0 collective-permute-done.13.other
  56.4 1.6 %shard_map.74 = (bf16[128,512]{1,0:T(8,128)(2,1)S(1)}, bf16[2,3,512,512]{3,2,1,0:T(8,128)(2,1)}, bf16[128,1024]{1,0:T(8,128)(2,1)}) custom-call(bf16[128,1024]{1,0:T(8,128)(2,1)S(1)} %copy-done.2, bf16[2,512,512]{2,1,0:T(8,128)(2,1)S(1)} %shard_map.72.refs_4_.own, ...), custom_call_target="tpu_custom_call", output_to_operand_aliasing={{1}: (4, {})} | custom-call | tf_op jit(solution)/shard_map/pallas_call | solution.py:340
  58.1 0.9 %shard_map.75 = (bf16[2,3,512,512]{3,2,1,0:T(8,128)(2,1)}, bf16[128,1024]{1,0:T(8,128)(2,1)}) custom-call(bf16[128,512]{1,0:T(8,128)(2,1)S(1)} %get-tuple-element.45.hidden, bf16[1,512,512]{2,1,0:T(8,128)(2,1)S(1)} %collective-permute-done.18.other, bf16[2,3,512,512]{3,2,1,0:T(8,128)(2,1)} %get-tuple-element.46.held, ...), custom_call_target="tpu_custom_call", output_to_operand_aliasing={{0}: (2, {}), {1}: (3, {})} | custom-call | tf_op jit(solution)/shard_map/pallas_call | solution.py:349
  (12 shorter events, 0.2 us)
Async XLA Ops:
  2.6 3.2 %collective-permute-start = (bf16[2,128,512]{2,1,0:T(8,128)(2,1)}, bf16[2,128,512]{2,1,0:T(8,128)(2,1)S(1)}, u32[]{:S(2)}, u32[]{:S(2)}) collective-permute-start(bf16[2,128,512]{2,1,0:T(8,128)(2,1)} %get-tuple-element.27), channel_id=1, source_target_pairs={{0,1},{1,0},{2,3},{3,2},{4,5},{5,4},{6,7},{7,6},{8,9},{9,8},{10,11... | collective-permute-start | bytes 786440 | tf_op jit(solution)/shard_map/ppermute | solution.py:259
  3.1 9.1 %collective-permute-start.1 = (bf16[2,128,512]{2,1,0:T(8,128)(2,1)}, bf16[2,128,512]{2,1,0:T(8,128)(2,1)S(1)}, u32[]{:S(2)}, u32[]{:S(2)}) collective-permute-start(bf16[2,128,512]{2,1,0:T(8,128)(2,1)} %get-tuple-element.26.t0), channel_id=1, source_target_pairs={{0,2},{1,5},{2,0},{3,7},{4,6},{5,1},{6,4},{7,3},{8,10},{9,13},{10,... | collective-permute-start | bytes 786440 | tf_op jit(solution)/shard_map/ppermute | solution.py:259
  5.7 7.4 %collective-permute-start.2 = (bf16[2,128,512]{2,1,0:T(8,128)(2,1)}, bf16[2,128,512]{2,1,0:T(8,128)(2,1)S(1)}, u32[]{:S(2)}, u32[]{:S(2)}) collective-permute-start(bf16[2,128,512]{2,1,0:T(8,128)(2,1)} %get-tuple-element.27), channel_id=1, source_target_pairs={{0,5},{1,2},{2,7},{3,0},{4,1},{5,6},{6,3},{7,4},{8,13},{9,10},{10,... | collective-permute-start | bytes 786440 | tf_op jit(solution)/shard_map/ppermute | solution.py:259
  5.8 1.9 %copy-start = (bf16[2,3,512,512]{3,2,1,0:T(8,128)(2,1)S(1)}, bf16[2,3,512,512]{3,2,1,0:T(8,128)(2,1)}, u32[]{:S(2)}) copy-start(bf16[2,3,512,512]{3,2,1,0:T(8,128)(2,1)} %weights.1) | copy-start | bytes 9437188
  7.7 0.9 %copy-start.1 = (bf16[2,128,512]{2,1,0:T(8,128)(2,1)S(1)}, bf16[2,128,512]{2,1,0:T(8,128)(2,1)}, u32[]{:S(2)}) copy-start(bf16[2,128,512]{2,1,0:T(8,128)(2,1)} %get-tuple-element.26.t0) | copy-start | bytes 786436
  14.2 5.1 %collective-permute-start.3 = (bf16[512,128]{1,0:T(8,128)(2,1)S(1)}, bf16[512,128]{1,0:T(8,128)(2,1)S(1)}, u32[]{:S(2)}, u32[]{:S(2)}) collective-permute-start(bf16[512,128]{1,0:T(8,128)(2,1)S(1)} %get-tuple-element.32), channel_id=1, source_target_pairs={{0,4},{1,3},{2,6},{3,1},{4,0},{5,7},{6,2},{7,5},{8,12},{9,11},{10,... | collective-permute-start | bytes 393224 | tf_op jit(solution)/shard_map/ppermute | solution.py:259
  16.8 8.5 %collective-permute-start.5 = (bf16[2,512,128]{2,1,0:T(8,128)(2,1)S(1)}, bf16[2,512,128]{2,1,0:T(8,128)(2,1)S(1)}, u32[]{:S(2)}, u32[]{:S(2)}) collective-permute-start(bf16[2,512,128]{2,1,0:T(8,128)(2,1)S(1)} %pad_maximum_fusion), channel_id=1, source_target_pairs={{0,4},{1,3},{2,6},{3,1},{4,0},{5,7},{6,2},{7,5},{8,12},{9,11},{10,... | collective-permute-start | bytes 786440 | tf_op jit(solution)/shard_map/ppermute | solution.py:259
  19.3 12.0 %collective-permute-start.4 = (bf16[512,128]{1,0:T(8,128)(2,1)S(1)}, bf16[512,128]{1,0:T(8,128)(2,1)S(1)}, u32[]{:S(2)}, u32[]{:S(2)}) collective-permute-start(bf16[512,128]{1,0:T(8,128)(2,1)S(1)} %add_convert_fusion.3), channel_id=1, source_target_pairs={{0,8},{1,9},{2,10},{3,11},{4,12},{5,13},{6,14},{7,15},{8,0},{9,1},... | collective-permute-start | bytes 393224 | tf_op jit(solution)/shard_map/ppermute | solution.py:259
  25.4 10.7 %collective-permute-start.9 = (bf16[512,128]{1,0:T(8,128)(2,1)S(1)}, bf16[512,128]{1,0:T(8,128)(2,1)S(1)}, u32[]{:S(2)}, u32[]{:S(2)}) collective-permute-start(bf16[512,128]{1,0:T(8,128)(2,1)S(1)} %get-tuple-element.50), channel_id=1, source_target_pairs={{0,8},{1,9},{2,10},{3,11},{4,12},{5,13},{6,14},{7,15},{8,0},{9,1},... | collective-permute-start | bytes 393224 | tf_op jit(solution)/shard_map/ppermute | solution.py:259
  31.4 10.5 %collective-permute-start.7 = (bf16[512,128]{1,0:T(8,128)(2,1)S(1)}, bf16[512,128]{1,0:T(8,128)(2,1)S(1)}, u32[]{:S(2)}, u32[]{:S(2)}) collective-permute-start(bf16[512,128]{1,0:T(8,128)(2,1)S(1)} %add_convert_fusion.2.refs_0_), channel_id=1, source_target_pairs={{0,2},{1,5},{2,0},{3,7},{4,6},{5,1},{6,4},{7,3},{8,10},{9,13},{10,... | collective-permute-start | bytes 393224 | tf_op jit(solution)/shard_map/ppermute | solution.py:259
  33.2 8.7 %collective-permute-start.6 = (bf16[512,128]{1,0:T(8,128)(2,1)S(1)}, bf16[512,128]{1,0:T(8,128)(2,1)S(1)}, u32[]{:S(2)}, u32[]{:S(2)}) collective-permute-start(bf16[512,128]{1,0:T(8,128)(2,1)S(1)} %add_convert_fusion.2.refs_0_), channel_id=1, source_target_pairs={{0,4},{1,3},{2,6},{3,1},{4,0},{5,7},{6,2},{7,5},{8,12},{9,11},{10,... | collective-permute-start | bytes 393224 | tf_op jit(solution)/shard_map/ppermute | solution.py:259
  33.2 6.1 %collective-permute-start.14 = (bf16[512,128]{1,0:T(8,128)(2,1)S(1)}, bf16[512,128]{1,0:T(8,128)(2,1)S(1)}, u32[]{:S(2)}, u32[]{:S(2)}) collective-permute-start(bf16[512,128]{1,0:T(8,128)(2,1)S(1)} %get-tuple-element.42), channel_id=1, source_target_pairs={{0,8},{1,9},{2,10},{3,11},{4,12},{5,13},{6,14},{7,15},{8,0},{9,1},... | collective-permute-start | bytes 393224 | tf_op jit(solution)/shard_map/ppermute | solution.py:259
  36.1 6.9 %collective-permute-start.11 = (bf16[512,128]{1,0:T(8,128)(2,1)S(1)}, bf16[512,128]{1,0:T(8,128)(2,1)S(1)}, u32[]{:S(2)}, u32[]{:S(2)}) collective-permute-start(bf16[512,128]{1,0:T(8,128)(2,1)S(1)} %add_convert_fusion.1.refs_4_), channel_id=1, source_target_pairs={{0,2},{1,5},{2,0},{3,7},{4,6},{5,1},{6,4},{7,3},{8,10},{9,13},{10,... | collective-permute-start | bytes 393224 | tf_op jit(solution)/shard_map/ppermute | solution.py:259
  37.2 5.8 %collective-permute-start.10 = (bf16[512,128]{1,0:T(8,128)(2,1)S(1)}, bf16[512,128]{1,0:T(8,128)(2,1)S(1)}, u32[]{:S(2)}, u32[]{:S(2)}) collective-permute-start(bf16[512,128]{1,0:T(8,128)(2,1)S(1)} %add_convert_fusion.1.refs_4_), channel_id=1, source_target_pairs={{0,4},{1,3},{2,6},{3,1},{4,0},{5,7},{6,2},{7,5},{8,12},{9,11},{10,... | collective-permute-start | bytes 393224 | tf_op jit(solution)/shard_map/ppermute | solution.py:259
  39.4 6.4 %collective-permute-start.15 = (bf16[512,128]{1,0:T(8,128)(2,1)S(1)}, bf16[512,128]{1,0:T(8,128)(2,1)S(1)}, u32[]{:S(2)}, u32[]{:S(2)}) collective-permute-start(bf16[512,128]{1,0:T(8,128)(2,1)S(1)} %add_convert_fusion.refs_0_), channel_id=1, source_target_pairs={{0,4},{1,3},{2,6},{3,1},{4,0},{5,7},{6,2},{7,5},{8,12},{9,11},{10,... | collective-permute-start | bytes 393224 | tf_op jit(solution)/shard_map/ppermute | solution.py:259
  41.9 5.0 %collective-permute-start.8 = (bf16[512,128]{1,0:T(8,128)(2,1)S(1)}, bf16[512,128]{1,0:T(8,128)(2,1)S(1)}, u32[]{:S(2)}, u32[]{:S(2)}) collective-permute-start(bf16[512,128]{1,0:T(8,128)(2,1)S(1)} %broadcast_select_fusion.1), channel_id=1, source_target_pairs={{0,2},{1,3},{2,0},{3,1},{4,6},{5,7},{6,4},{7,5},{8,10},{9,11},{10,... | collective-permute-start | bytes 393224 | tf_op jit(solution)/shard_map/ppermute | solution.py:259
  43.0 5.3 %collective-permute-start.12 = (bf16[512,128]{1,0:T(8,128)(2,1)S(1)}, bf16[512,128]{1,0:T(8,128)(2,1)S(1)}, u32[]{:S(2)}, u32[]{:S(2)}) collective-permute-start(bf16[512,128]{1,0:T(8,128)(2,1)S(1)} %broadcast_select_fusion), channel_id=1, source_target_pairs={{0,2},{1,3},{2,0},{3,1},{4,6},{5,7},{6,4},{7,5},{8,10},{9,11},{10,... | collective-permute-start | bytes 393224 | tf_op jit(solution)/shard_map/ppermute | solution.py:259
  44.1 9.0 %collective-permute-start.16 = (bf16[512,128]{1,0:T(8,128)(2,1)S(1)}, bf16[512,128]{1,0:T(8,128)(2,1)S(1)}, u32[]{:S(2)}, u32[]{:S(2)}) collective-permute-start(bf16[512,128]{1,0:T(8,128)(2,1)S(1)} %add_convert_fusion.refs_0_), channel_id=1, source_target_pairs={{0,2},{1,5},{2,0},{3,7},{4,6},{5,1},{6,4},{7,3},{8,10},{9,13},{10,... | collective-permute-start | bytes 393224 | tf_op jit(solution)/shard_map/ppermute | solution.py:259
  45.8 7.3 %collective-permute-start.17 = (bf16[512,128]{1,0:T(8,128)(2,1)S(1)}, bf16[512,128]{1,0:T(8,128)(2,1)S(1)}, u32[]{:S(2)}, u32[]{:S(2)}) collective-permute-start(bf16[512,128]{1,0:T(8,128)(2,1)S(1)} %collective-permute-done.15.refs_1_), channel_id=1, source_target_pairs={{0,2},{1,5},{2,0},{3,7},{4,6},{5,1},{6,4},{7,3},{8,10},{9,13},{10,... | collective-permute-start | bytes 393224 | tf_op jit(solution)/shard_map/ppermute | solution.py:259
  53.0 3.4 %copy-start.2 = (bf16[128,1024]{1,0:T(8,128)(2,1)S(1)}, bf16[128,1024]{1,0:T(8,128)(2,1)}, u32[]{:S(2)}) copy-start(bf16[128,1024]{1,0:T(8,128)(2,1)} %queries.1) | copy-start | bytes 786436
  53.0 3.4 %collective-permute-start.13 = (bf16[2,512,512]{2,1,0:T(8,128)(2,1)S(1)}, bf16[2,512,512]{2,1,0:T(8,128)(2,1)S(1)}, u32[]{:S(2)}, u32[]{:S(2)}) collective-permute-start(bf16[2,512,512]{2,1,0:T(8,128)(2,1)S(1)} %shard_map.72.refs_4_.own), channel_id=1, source_target_pairs={{0,1},{1,0},{2,3},{3,2},{4,5},{5,4},{6,7},{7,6},{8,9},{9,8},{10,11... | collective-permute-start | bytes 3145736 | tf_op jit(solution)/shard_map/ppermute | solution.py:259
  55.9 2.2 %collective-permute-start.18 = (bf16[1,512,512]{2,1,0:T(8,128)(2,1)S(1)}, bf16[1,512,512]{2,1,0:T(8,128)(2,1)S(1)}, u32[]{:S(2)}, u32[]{:S(2)}) collective-permute-start(bf16[1,512,512]{2,1,0:T(8,128)(2,1)S(1)} %get-tuple-element.43.own_down), channel_id=1, source_target_pairs={{0,1},{1,0},{2,3},{3,2},{4,5},{5,4},{6,7},{7,6},{8,9},{9,8},{10,11... | collective-permute-start | bytes 1572872 | tf_op jit(solution)/shard_map/ppermute | solution.py:259

commit v6 on v5

--- a/solution.py
+++ b/solution.py
@@ -74,7 +74,8 @@
 
 def cuts(width):
     _, half, quarter = place()
-    return span(2 * half + 1 - quarter, width // 4), span(2 * half + quarter, width // 4)
+    yield span(2 * half + 1 - quarter, width // 4)
+    yield span(2 * half + quarter, width // 4)
 
 
 def near_kernel(t0, t1, weights, send, keep, mine, keys, outer, sem):
@@ -95,29 +96,32 @@
             out[2, at * piece : (at + 1) * piece, :] = down[:, at * piece : (at + 1) * piece]
 
 
-def far_gate_kernel(t2, t3, mine, near_send, near_keep, send, keep, hidden, d_upper, keys, outer):
+def far_gate_kernel(t2, t3, mine, near_send, send, hidden, d_upper, keys, outer):
     tokens, width = t2.shape[1:]
-    piece = width // 4
     for at, src in enumerate((t2, t3)):
         keys[at * tokens : (at + 1) * tokens, :] = src[0]
         outer[at * tokens : (at + 1) * tokens, :] = src[1]
-    for at, (out, near, cut) in enumerate(zip((send, keep), (near_send, near_keep), cuts(width))):
-        h, dg, du = token_parts(keys[...], outer[...], mine, cut)
-        out[...] = (near[0] + dot(keys[...], dg, 0, 0)).astype(out.dtype)
-        hidden[:, at * piece : (at + 1) * piece] = h
-        d_upper[:, at * piece : (at + 1) * piece] = du
-
-
-def far_rest_kernel(keys, outer, hidden, d_upper, near_send, near_keep, *outs):
+    h, dg, du = token_parts(keys[...], outer[...], mine, next(cuts(width)))
+    send[...] = (near_send[0] + dot(keys[...], dg, 0, 0)).astype(send.dtype)
+    hidden[...] = h
+    d_upper[...] = du
+
+
+def far_rest_kernel(keys, outer, mine, hidden, d_upper, near_send, near_keep, send_u, send_d, keep_g, keep_u, keep_d):
     width = keys.shape[1]
     piece = width // 4
-    for at, (out, near) in enumerate(zip((outs[:2], outs[2:]), (near_send, near_keep))):
-        cut = slice(at * piece, (at + 1) * piece)
-        out[0][...] = (near[1] + dot(keys[...], d_upper[:, cut], 0, 0)).astype(out[0].dtype)
-        down = dot(hidden[:, cut], outer[...], 0, 0)
+    _, cut = cuts(width)
+    h, dg, du = token_parts(keys[...], outer[...], mine, cut)
+    keep_g[...] = near_keep[0] + dot(keys[...], dg, 0, 0)
+    for h, du, near, out_u, out_d in (
+        (hidden[...], d_upper[...], near_send, send_u, send_d),
+        (h, du, near_keep, keep_u, keep_d),
+    ):
+        out_u[...] = (near[1] + dot(keys[...], du, 0, 0)).astype(out_u.dtype)
+        down = dot(h, outer[...], 0, 0)
         for block in range(width // piece):
             rows = slice(block * piece, (block + 1) * piece)
-            out[1][rows, :] = (near[2, rows, :] + down[:, rows]).astype(out[1].dtype)
+            out_d[rows, :] = (near[2, rows, :] + down[:, rows]).astype(out_d.dtype)
 
 
 def newton_schulz(matrix):
@@ -287,22 +291,22 @@
         compiler_params=PARAMS,
     )(own, move(other, sibling), fast_weights)
     rows = jax.ShapeDtypeStruct((2 * tokens, width), BF16)
-    units = jax.ShapeDtypeStruct((2 * tokens, width // 2), BF16)
-    send_g, keep_g, hidden, d_upper, far_keys, far_outer = pl.pallas_call(
+    units = jax.ShapeDtypeStruct((2 * tokens, quarter), BF16)
+    send_g, hidden, d_upper, far_keys, far_outer = pl.pallas_call(
         far_gate_kernel,
-        out_shape=(part16, part32, units, units, rows, rows),
-        in_specs=[VMEM_SPEC] * 5,
-        out_specs=(VMEM_SPEC,) * 6,
-        compiler_params=PARAMS,
-    )(move(own, first), move(other, across), mine, near_send, near_keep)
-    send_u, send_d, keep_u, keep_d = pl.pallas_call(
+        out_shape=(part16, units, units, rows, rows),
+        in_specs=[VMEM_SPEC] * 4,
+        out_specs=(VMEM_SPEC,) * 5,
+        compiler_params=PARAMS,
+    )(move(own, first), move(other, across), mine, near_send)
+    send_u, send_d, keep_g, keep_u, keep_d = pl.pallas_call(
         far_rest_kernel,
-        out_shape=(part16,) * 2 + (part32,) * 2,
-        in_specs=[VMEM_SPEC] * 6,
-        out_specs=(VMEM_SPEC,) * 4,
+        out_shape=(part16,) * 2 + (part32,) * 3,
+        in_specs=[VMEM_SPEC] * 7,
+        out_specs=(VMEM_SPEC,) * 5,
         compiler_params=PARAMS,
         cost_estimate=pl.CostEstimate(flops=400 * tokens * width**2, bytes_accessed=64 * width**2, transcendentals=0),
-    )(far_keys, far_outer, hidden, d_upper, near_send, near_keep)
+    )(far_keys, far_outer, mine, hidden, d_upper, near_send, near_keep)
     send, keep = (send_g, send_u, send_d), (keep_g, keep_u, keep_d)
 
     def reduced(at):

time: 59.2 us -> 58.7 us (level)
  transfers between devices with their start and end apart: 19 -> 19, of which waited for: 9 -> 9; matrix products, arithmetic and copies ran while one was open for 0% -> 0% of each run, Pallas kernels for 19% -> 20%
where the time goes in v6:
time: 58.7 us; the launch traced here: 58.5 us
  starting transfers between devices  23.5 us (40%)
  waiting for transfers between devices  16 us (27%)
  Pallas kernels  15 us (26%)
  local copies, waits for them, and re-layouts  2.85 us (5%)
  between operations  0.78 us (1%)
    ppermute x19, starting transfers between devices, move(): return lax.ppermute(value, 'tok', pairs)  23.5 us
    ppermute x19, waiting for transfers between devices, move(): return lax.ppermute(value, 'tok', pairs)  16 us
    pallas_call x2, Pallas kernels, updated(): pl.pallas_call(functools.partial(ns_kernel, which, earlier), out_shape=ou...  7.39 us
    unnamed x6, local copies, waits for them, and re-layouts  2.85 us
    pallas_call x1, Pallas kernels, body(): pl.pallas_call(pack_kernel, out_shape=(pair, pair), in_specs=[ANY_SPEC] *...  1.96 us
    pallas_call x1, Pallas kernels, body(): pl.pallas_call(gate_up_kernel, out_shape=(jax.ShapeDtypeStruct(half_reado...  1.62 us
    pallas_call x1, Pallas kernels, body(): pl.pallas_call(near_kernel, out_shape=(three32, three32, jax.ShapeDtypeSt...  1.55 us
  transfers between devices with their start and end apart: 19, of which 9 were waited for; matrix products, arithmetic and copies ran while one was open for 0% of the time, Pallas kernels for 20%

profile of v6, /device:TPU:0, one launch (start us, length us, event | category | flops | bytes accessed | tf_op | source)
XLA Modules:
  0.0 58.5 jit_solution(18446125321372380324)
XLA Ops:
  0.6 2.0 %shard_map.68 = (bf16[2,128,512]{2,1,0:T(8,128)(2,1)}, bf16[2,128,512]{2,1,0:T(8,128)(2,1)}) custom-call(bf16[128,1024]{1,0:T(8,128)(2,1)} %keys.1, bf16[128,1024]{1,0:T(8,128)(2,1)} %values.1, f32[2,128]{1,0:T(2,128)} %rates.1), custom_call_target="tpu_custom_call" | custom-call | tf_op jit(solution)/shard_map/pallas_call | solution.py:269
  2.6 0.5 collective-permute-start
  3.1 2.6 %collective-permute-start.1 = (bf16[2,128,512]{2,1,0:T(8,128)(2,1)}, bf16[2,128,512]{2,1,0:T(8,128)(2,1)S(1)}, u32[]{:S(2)}, u32[]{:S(2)}) collective-permute-start(bf16[2,128,512]{2,1,0:T(8,128)(2,1)} %get-tuple-element.26.t0), channel_id=1, source_target_pairs={{0,2},{1,5},{2,0},{3,7},{4,6},{5,1},{6,4},{7,3},{8,10},{9,13},{10,... | collective-permute-start | bytes 786440 | tf_op jit(solution)/shard_map/ppermute | solution.py:263
  5.7 0.1 collective-permute-start.2
  5.8 0.0 collective-permute-done.t1
  5.8 1.9 %copy-done = bf16[2,3,512,512]{3,2,1,0:T(8,128)(2,1)S(1)} copy-done((bf16[2,3,512,512]{3,2,1,0:T(8,128)(2,1)S(1)}, bf16[2,3,512,512]{3,2,1,0:T(8,128)(2,1)}, u32[]{:S(2)}) %copy-start) | copy-done | bytes 3145752
  7.7 0.9 %copy-done.1 = bf16[2,128,512]{2,1,0:T(8,128)(2,1)S(1)} copy-done((bf16[2,128,512]{2,1,0:T(8,128)(2,1)S(1)}, bf16[2,128,512]{2,1,0:T(8,128)(2,1)}, u32[]{:S(2)}) %copy-start.1) | copy-done | bytes 262168
  8.7 1.5 %shard_map.69 = (f32[3,512,128]{2,1,0:T(8,128)S(1)}, f32[3,512,128]{2,1,0:T(8,128)S(1)}, bf16[3,512,512]{2,1,0:T(8,128)(2,1)S(1)}) custom-call(bf16[2,128,512]{2,1,0:T(8,128)(2,1)S(1)} %copy-done.1, bf16[2,128,512]{2,1,0:T(8,128)(2,1)S(1)} %collective-permute-done.t1, bf16[2,3,512,512]{3,2,1,0:T(8,128)(2,1)S(1)} %copy-done), custom_call_target="tpu_custom_call" | custom-call | tf_op jit(solution)/shard_map/pallas_call | solution.py:285
  10.2 2.0 %collective-permute-done.1.t2 = bf16[2,128,512]{2,1,0:T(8,128)(2,1)S(1)} collective-permute-done((bf16[2,128,512]{2,1,0:T(8,128)(2,1)}, bf16[2,128,512]{2,1,0:T(8,128)(2,1)S(1)}, u32[]{:S(2)}, u32[]{:S(2)}) %collective-permute-start.1) | collective-permute-done | bytes 262176 | tf_op jit(solution)/shard_map/ppermute | solution.py:263
  12.2 0.8 %collective-permute-done.2.t3 = bf16[2,128,512]{2,1,0:T(8,128)(2,1)S(1)} collective-permute-done((bf16[2,128,512]{2,1,0:T(8,128)(2,1)}, bf16[2,128,512]{2,1,0:T(8,128)(2,1)S(1)}, u32[]{:S(2)}, u32[]{:S(2)}) %collective-permute-start.2) | collective-permute-done | bytes 262176 | tf_op jit(solution)/shard_map/ppermute | solution.py:263
  13.1 0.7 %shard_map.70 = (bf16[512,128]{1,0:T(8,128)(2,1)S(1)}, bf16[256,128]{1,0:T(8,128)(2,1)S(1)}, bf16[256,128]{1,0:T(8,128)(2,1)S(1)}, bf16[256,512]{1,0:T(8,128)(2,1)S(1)}, bf16[256,512]{1,0:T(8,128)(2,1)S(1)}) custom-call(bf16[2,128,512]{2,1,0:T(8,128)(2,1)S(1)} %collective-permute-done.1.t2, bf16[2,128,512]{2,1,0:T(8,128)(2,1)S(1)} %collective-permute-done.2.t3, ...), custom_call_target="tpu_custom_call" | custom-call | tf_op jit(solution)/shard_map/pallas_call | solution.py:295
  13.8 2.1 %collective-permute-start.3 = (bf16[512,128]{1,0:T(8,128)(2,1)S(1)}, bf16[512,128]{1,0:T(8,128)(2,1)S(1)}, u32[]{:S(2)}, u32[]{:S(2)}) collective-permute-start(bf16[512,128]{1,0:T(8,128)(2,1)S(1)} %get-tuple-element.36), channel_id=1, source_target_pairs={{0,4},{1,3},{2,6},{3,1},{4,0},{5,7},{6,2},{7,5},{8,12},{9,11},{10,... | collective-permute-start | bytes 393224 | tf_op jit(solution)/shard_map/ppermute | solution.py:263
  15.9 0.9 %shard_map.71 = (bf16[512,128]{1,0:T(8,128)(2,1)S(1)}, bf16[512,128]{1,0:T(8,128)(2,1)S(1)}, f32[512,128]{1,0:T(8,128)S(1)}, f32[512,128]{1,0:T(8,128)S(1)}, f32[512,128]{1,0:T(8,128)S(1)}) custom-call(bf16[256,512]{1,0:T(8,128)(2,1)S(1)} %get-tuple-element.30.keys, bf16[256,512]{1,0:T(8,128)(2,1)S(1)} %get-tuple-element.31.outer, ...), custom_call_target="tpu_custom_call" | custom-call | flops 13421772800 | bytes 16777216 | tf_op jit(solution)/shard_map/pallas_call | solution.py:302
  16.9 0.1 collective-permute-start.5
  17.0 1.9 %collective-permute-done.3 = bf16[512,128]{1,0:T(8,128)(2,1)S(1)} collective-permute-done((bf16[512,128]{1,0:T(8,128)(2,1)S(1)}, bf16[512,128]{1,0:T(8,128)(2,1)S(1)}, u32[]{:S(2)}, u32[]{:S(2)}) %collective-permute-start.3) | collective-permute-done | bytes 131104 | tf_op jit(solution)/shard_map/ppermute | solution.py:263
  18.9 3.1 %collective-permute-start.4 = (bf16[512,128]{1,0:T(8,128)(2,1)S(1)}, bf16[512,128]{1,0:T(8,128)(2,1)S(1)}, u32[]{:S(2)}, u32[]{:S(2)}) collective-permute-start(bf16[512,128]{1,0:T(8,128)(2,1)S(1)} %add_convert_fusion.3), channel_id=1, source_target_pairs={{0,8},{1,9},{2,10},{3,11},{4,12},{5,13},{6,14},{7,15},{8,0},{9,1},... | collective-permute-start | bytes 393224 | tf_op jit(solution)/shard_map/ppermute | solution.py:263
  22.0 4.9 %collective-permute-done.5 = bf16[2,512,128]{2,1,0:T(8,128)(2,1)S(1)} collective-permute-done((bf16[2,512,128]{2,1,0:T(8,128)(2,1)S(1)}, bf16[2,512,128]{2,1,0:T(8,128)(2,1)S(1)}, u32[]{:S(2)}, u32[]{:S(2)}) %collective-permute-start.5) | collective-permute-done | bytes 262176 | tf_op jit(solution)/shard_map/ppermute | solution.py:263
  26.9 0.1 fusion
  26.9 0.9 %collective-permute-start.9 = (bf16[512,128]{1,0:T(8,128)(2,1)S(1)}, bf16[512,128]{1,0:T(8,128)(2,1)S(1)}, u32[]{:S(2)}, u32[]{:S(2)}) collective-permute-start(bf16[512,128]{1,0:T(8,128)(2,1)S(1)} %get-tuple-element.50), channel_id=1, source_target_pairs={{0,8},{1,9},{2,10},{3,11},{4,12},{5,13},{6,14},{7,15},{8,0},{9,1},... | collective-permute-start | bytes 393224 | tf_op jit(solution)/shard_map/ppermute | solution.py:263
  27.8 0.0 collective-permute-done.4
  27.8 4.9 %collective-permute-start.7 = (bf16[512,128]{1,0:T(8,128)(2,1)S(1)}, bf16[512,128]{1,0:T(8,128)(2,1)S(1)}, u32[]{:S(2)}, u32[]{:S(2)}) collective-permute-start(bf16[512,128]{1,0:T(8,128)(2,1)S(1)} %add_convert_fusion.2.refs_0_), channel_id=1, source_target_pairs={{0,2},{1,5},{2,0},{3,7},{4,6},{5,1},{6,4},{7,3},{8,10},{9,13},{10,... | collective-permute-start | bytes 393224 | tf_op jit(solution)/shard_map/ppermute | solution.py:263
  32.8 0.0 collective-permute-start.6
  32.8 2.4 %collective-permute-start.14 = (bf16[512,128]{1,0:T(8,128)(2,1)S(1)}, bf16[512,128]{1,0:T(8,128)(2,1)S(1)}, u32[]{:S(2)}, u32[]{:S(2)}) collective-permute-start(bf16[512,128]{1,0:T(8,128)(2,1)S(1)} %get-tuple-element.42), channel_id=1, source_target_pairs={{0,8},{1,9},{2,10},{3,11},{4,12},{5,13},{6,14},{7,15},{8,0},{9,1},... | collective-permute-start | bytes 393224 | tf_op jit(solution)/shard_map/ppermute | solution.py:263
  35.2 0.0 collective-permute-done.9
  35.2 0.6 %collective-permute-start.11 = (bf16[512,128]{1,0:T(8,128)(2,1)S(1)}, bf16[512,128]{1,0:T(8,128)(2,1)S(1)}, u32[]{:S(2)}, u32[]{:S(2)}) collective-permute-start(bf16[512,128]{1,0:T(8,128)(2,1)S(1)} %add_convert_fusion.1.refs_4_), channel_id=1, source_target_pairs={{0,2},{1,5},{2,0},{3,7},{4,6},{5,1},{6,4},{7,3},{8,10},{9,13},{10,... | collective-permute-start | bytes 393224 | tf_op jit(solution)/shard_map/ppermute | solution.py:263
  35.9 0.0 collective-permute-start.10
  35.9 3.1 %collective-permute-done.14 = bf16[512,128]{1,0:T(8,128)(2,1)S(1)} collective-permute-done((bf16[512,128]{1,0:T(8,128)(2,1)S(1)}, bf16[512,128]{1,0:T(8,128)(2,1)S(1)}, u32[]{:S(2)}, u32[]{:S(2)}) %collective-permute-start.14) | collective-permute-done | bytes 131104 | tf_op jit(solution)/shard_map/ppermute | solution.py:263
  39.0 2.1 %collective-permute-start.15 = (bf16[512,128]{1,0:T(8,128)(2,1)S(1)}, bf16[512,128]{1,0:T(8,128)(2,1)S(1)}, u32[]{:S(2)}, u32[]{:S(2)}) collective-permute-start(bf16[512,128]{1,0:T(8,128)(2,1)S(1)} %add_convert_fusion.refs_0_), channel_id=1, source_target_pairs={{0,4},{1,3},{2,6},{3,1},{4,0},{5,7},{6,2},{7,5},{8,12},{9,11},{10,... | collective-permute-start | bytes 393224 | tf_op jit(solution)/shard_map/ppermute | solution.py:263
  41.0 0.0 collective-permute-done.7.refs_2_
  41.0 0.0 collective-permute-done.6.refs_1_
  41.1 0.8 %collective-permute-start.8 = (bf16[512,128]{1,0:T(8,128)(2,1)S(1)}, bf16[512,128]{1,0:T(8,128)(2,1)S(1)}, u32[]{:S(2)}, u32[]{:S(2)}) collective-permute-start(bf16[512,128]{1,0:T(8,128)(2,1)S(1)} %broadcast_select_fusion.1), channel_id=1, source_target_pairs={{0,2},{1,3},{2,0},{3,1},{4,6},{5,7},{6,4},{7,5},{8,10},{9,11},{10,... | collective-permute-start | bytes 393224 | tf_op jit(solution)/shard_map/ppermute | solution.py:263
  41.9 0.4 collective-permute-done.10.refs_5_
  42.3 0.9 %collective-permute-start.12 = (bf16[512,128]{1,0:T(8,128)(2,1)S(1)}, bf16[512,128]{1,0:T(8,128)(2,1)S(1)}, u32[]{:S(2)}, u32[]{:S(2)}) collective-permute-start(bf16[512,128]{1,0:T(8,128)(2,1)S(1)} %broadcast_select_fusion), channel_id=1, source_target_pairs={{0,2},{1,3},{2,0},{3,1},{4,6},{5,7},{6,4},{7,5},{8,10},{9,11},{10,... | collective-permute-start | bytes 393224 | tf_op jit(solution)/shard_map/ppermute | solution.py:263
  43.3 1.2 %collective-permute-start.16 = (bf16[512,128]{1,0:T(8,128)(2,1)S(1)}, bf16[512,128]{1,0:T(8,128)(2,1)S(1)}, u32[]{:S(2)}, u32[]{:S(2)}) collective-permute-start(bf16[512,128]{1,0:T(8,128)(2,1)S(1)} %add_convert_fusion.refs_0_), channel_id=1, source_target_pairs={{0,2},{1,5},{2,0},{3,7},{4,6},{5,1},{6,4},{7,3},{8,10},{9,13},{10,... | collective-permute-start | bytes 393224 | tf_op jit(solution)/shard_map/ppermute | solution.py:263
  44.4 0.4 collective-permute-done.15.refs_1_
  44.9 0.5 collective-permute-start.17
  45.4 1.1 %collective-permute-done.8.refs_3_ = bf16[512,128]{1,0:T(8,128)(2,1)S(1)} collective-permute-done((bf16[512,128]{1,0:T(8,128)(2,1)S(1)}, bf16[512,128]{1,0:T(8,128)(2,1)S(1)}, u32[]{:S(2)}, u32[]{:S(2)}) %collective-permute-start.8) | collective-permute-done | bytes 131104 | tf_op jit(solution)/shard_map/ppermute | solution.py:263
  46.5 1.4 %collective-permute-done.12.refs_7_ = bf16[512,128]{1,0:T(8,128)(2,1)S(1)} collective-permute-done((bf16[512,128]{1,0:T(8,128)(2,1)S(1)}, bf16[512,128]{1,0:T(8,128)(2,1)S(1)}, u32[]{:S(2)}, u32[]{:S(2)}) %collective-permute-start.12) | collective-permute-done | bytes 131104 | tf_op jit(solution)/shard_map/ppermute | solution.py:263
  47.9 4.6 %shard_map.72.refs_4_.own = bf16[2,512,512]{2,1,0:T(8,128)(2,1)S(1)} custom-call(bf16[3,512,512]{2,1,0:T(8,128)(2,1)S(1)} %get-tuple-element.28.mine, bf16[512,128]{1,0:T(8,128)(2,1)S(1)} %add_convert_fusion.2.refs_0_, bf16[512,128]{1,0:T(8,128)(2,1)S(1)} %collective-permute-done.6.refs_1_, bf16[512,128]{1,0:T(8,128)(2,1)S(1)} %collective-permute-done.7.refs_2_, ...), custom_call_target="tpu_custom_call" | custom-call | flops 64424509440 | bytes 33554432 | tf_op jit(solution)/shard_map/pallas_call | solution.py:197
  52.5 0.0 copy-start.2
  52.5 0.1 collective-permute-start.13
  52.6 0.0 collective-permute-done.17.refs_3_
  52.6 2.7 %shard_map.73 = (bf16[1,512,512]{2,1,0:T(8,128)(2,1)S(1)}, bf16[2,3,512,512]{3,2,1,0:T(8,128)(2,1)}) custom-call(bf16[3,512,512]{2,1,0:T(8,128)(2,1)S(1)} %get-tuple-element.28.mine, bf16[512,128]{1,0:T(8,128)(2,1)S(1)} %add_convert_fusion.refs_0_, bf16[512,128]{1,0:T(8,128)(2,1)S(1)} %collective-permute-done.15.refs_1_, ...), custom_call_target="tpu_custom_call" | custom-call | flops 32212254720 | bytes 16777216 | tf_op jit(solution)/shard_map/pallas_call | solution.py:197
  55.4 0.5 collective-permute-start.18
  55.9 0.0 collective-permute-done.13.other
  55.9 1.6 %shard_map.74 = (bf16[128,512]{1,0:T(8,128)(2,1)S(1)}, bf16[2,3,512,512]{3,2,1,0:T(8,128)(2,1)}, bf16[128,1024]{1,0:T(8,128)(2,1)}) custom-call(bf16[128,1024]{1,0:T(8,128)(2,1)S(1)} %copy-done.2, bf16[2,512,512]{2,1,0:T(8,128)(2,1)S(1)} %shard_map.72.refs_4_.own, ...), custom_call_target="tpu_custom_call", output_to_operand_aliasing={{1}: (4, {})} | custom-call | tf_op jit(solution)/shard_map/pallas_call | solution.py:344
  57.6 0.0 collective-permute-done.18.other
  57.6 0.9 %shard_map.75 = (bf16[2,3,512,512]{3,2,1,0:T(8,128)(2,1)}, bf16[128,1024]{1,0:T(8,128)(2,1)}) custom-call(bf16[128,512]{1,0:T(8,128)(2,1)S(1)} %get-tuple-element.45.hidden, bf16[1,512,512]{2,1,0:T(8,128)(2,1)S(1)} %collective-permute-done.18.other, bf16[2,3,512,512]{3,2,1,0:T(8,128)(2,1)} %get-tuple-element.46.held, ...), custom_call_target="tpu_custom_call", output_to_operand_aliasing={{0}: (2, {}), {1}: (3, {})} | custom-call | tf_op jit(solution)/shard_map/pallas_call | solution.py:353
  (12 shorter events, 0.2 us)
Async XLA Ops:
  2.6 3.2 %collective-permute-start = (bf16[2,128,512]{2,1,0:T(8,128)(2,1)}, bf16[2,128,512]{2,1,0:T(8,128)(2,1)S(1)}, u32[]{:S(2)}, u32[]{:S(2)}) collective-permute-start(bf16[2,128,512]{2,1,0:T(8,128)(2,1)} %get-tuple-element.27), channel_id=1, source_target_pairs={{0,1},{1,0},{2,3},{3,2},{4,5},{5,4},{6,7},{7,6},{8,9},{9,8},{10,11... | collective-permute-start | bytes 786440 | tf_op jit(solution)/shard_map/ppermute | solution.py:263
  3.1 9.1 %collective-permute-start.1 = (bf16[2,128,512]{2,1,0:T(8,128)(2,1)}, bf16[2,128,512]{2,1,0:T(8,128)(2,1)S(1)}, u32[]{:S(2)}, u32[]{:S(2)}) collective-permute-start(bf16[2,128,512]{2,1,0:T(8,128)(2,1)} %get-tuple-element.26.t0), channel_id=1, source_target_pairs={{0,2},{1,5},{2,0},{3,7},{4,6},{5,1},{6,4},{7,3},{8,10},{9,13},{10,... | collective-permute-start | bytes 786440 | tf_op jit(solution)/shard_map/ppermute | solution.py:263
  5.7 7.4 %collective-permute-start.2 = (bf16[2,128,512]{2,1,0:T(8,128)(2,1)}, bf16[2,128,512]{2,1,0:T(8,128)(2,1)S(1)}, u32[]{:S(2)}, u32[]{:S(2)}) collective-permute-start(bf16[2,128,512]{2,1,0:T(8,128)(2,1)} %get-tuple-element.27), channel_id=1, source_target_pairs={{0,5},{1,2},{2,7},{3,0},{4,1},{5,6},{6,3},{7,4},{8,13},{9,10},{10,... | collective-permute-start | bytes 786440 | tf_op jit(solution)/shard_map/ppermute | solution.py:263
  5.8 1.9 %copy-start = (bf16[2,3,512,512]{3,2,1,0:T(8,128)(2,1)S(1)}, bf16[2,3,512,512]{3,2,1,0:T(8,128)(2,1)}, u32[]{:S(2)}) copy-start(bf16[2,3,512,512]{3,2,1,0:T(8,128)(2,1)} %weights.1) | copy-start | bytes 9437188
  7.7 0.9 %copy-start.1 = (bf16[2,128,512]{2,1,0:T(8,128)(2,1)S(1)}, bf16[2,128,512]{2,1,0:T(8,128)(2,1)}, u32[]{:S(2)}) copy-start(bf16[2,128,512]{2,1,0:T(8,128)(2,1)} %get-tuple-element.26.t0) | copy-start | bytes 786436
  13.8 5.1 %collective-permute-start.3 = (bf16[512,128]{1,0:T(8,128)(2,1)S(1)}, bf16[512,128]{1,0:T(8,128)(2,1)S(1)}, u32[]{:S(2)}, u32[]{:S(2)}) collective-permute-start(bf16[512,128]{1,0:T(8,128)(2,1)S(1)} %get-tuple-element.36), channel_id=1, source_target_pairs={{0,4},{1,3},{2,6},{3,1},{4,0},{5,7},{6,2},{7,5},{8,12},{9,11},{10,... | collective-permute-start | bytes 393224 | tf_op jit(solution)/shard_map/ppermute | solution.py:263
  16.9 10.0 %collective-permute-start.5 = (bf16[2,512,128]{2,1,0:T(8,128)(2,1)S(1)}, bf16[2,512,128]{2,1,0:T(8,128)(2,1)S(1)}, u32[]{:S(2)}, u32[]{:S(2)}) collective-permute-start(bf16[2,512,128]{2,1,0:T(8,128)(2,1)S(1)} %pad_maximum_fusion), channel_id=1, source_target_pairs={{0,4},{1,3},{2,6},{3,1},{4,0},{5,7},{6,2},{7,5},{8,12},{9,11},{10,... | collective-permute-start | bytes 786440 | tf_op jit(solution)/shard_map/ppermute | solution.py:263
  18.9 8.9 %collective-permute-start.4 = (bf16[512,128]{1,0:T(8,128)(2,1)S(1)}, bf16[512,128]{1,0:T(8,128)(2,1)S(1)}, u32[]{:S(2)}, u32[]{:S(2)}) collective-permute-start(bf16[512,128]{1,0:T(8,128)(2,1)S(1)} %add_convert_fusion.3), channel_id=1, source_target_pairs={{0,8},{1,9},{2,10},{3,11},{4,12},{5,13},{6,14},{7,15},{8,0},{9,1},... | collective-permute-start | bytes 393224 | tf_op jit(solution)/shard_map/ppermute | solution.py:263
  26.9 8.3 %collective-permute-start.9 = (bf16[512,128]{1,0:T(8,128)(2,1)S(1)}, bf16[512,128]{1,0:T(8,128)(2,1)S(1)}, u32[]{:S(2)}, u32[]{:S(2)}) collective-permute-start(bf16[512,128]{1,0:T(8,128)(2,1)S(1)} %get-tuple-element.50), channel_id=1, source_target_pairs={{0,8},{1,9},{2,10},{3,11},{4,12},{5,13},{6,14},{7,15},{8,0},{9,1},... | collective-permute-start | bytes 393224 | tf_op jit(solution)/shard_map/ppermute | solution.py:263
  27.8 13.2 %collective-permute-start.7 = (bf16[512,128]{1,0:T(8,128)(2,1)S(1)}, bf16[512,128]{1,0:T(8,128)(2,1)S(1)}, u32[]{:S(2)}, u32[]{:S(2)}) collective-permute-start(bf16[512,128]{1,0:T(8,128)(2,1)S(1)} %add_convert_fusion.2.refs_0_), channel_id=1, source_target_pairs={{0,2},{1,5},{2,0},{3,7},{4,6},{5,1},{6,4},{7,3},{8,10},{9,13},{10,... | collective-permute-start | bytes 393224 | tf_op jit(solution)/shard_map/ppermute | solution.py:263
  32.8 8.3 %collective-permute-start.6 = (bf16[512,128]{1,0:T(8,128)(2,1)S(1)}, bf16[512,128]{1,0:T(8,128)(2,1)S(1)}, u32[]{:S(2)}, u32[]{:S(2)}) collective-permute-start(bf16[512,128]{1,0:T(8,128)(2,1)S(1)} %add_convert_fusion.2.refs_0_), channel_id=1, source_target_pairs={{0,4},{1,3},{2,6},{3,1},{4,0},{5,7},{6,2},{7,5},{8,12},{9,11},{10,... | collective-permute-start | bytes 393224 | tf_op jit(solution)/shard_map/ppermute | solution.py:263
  32.8 6.2 %collective-permute-start.14 = (bf16[512,128]{1,0:T(8,128)(2,1)S(1)}, bf16[512,128]{1,0:T(8,128)(2,1)S(1)}, u32[]{:S(2)}, u32[]{:S(2)}) collective-permute-start(bf16[512,128]{1,0:T(8,128)(2,1)S(1)} %get-tuple-element.42), channel_id=1, source_target_pairs={{0,8},{1,9},{2,10},{3,11},{4,12},{5,13},{6,14},{7,15},{8,0},{9,1},... | collective-permute-start | bytes 393224 | tf_op jit(solution)/shard_map/ppermute | solution.py:263
  35.2 6.7 %collective-permute-start.11 = (bf16[512,128]{1,0:T(8,128)(2,1)S(1)}, bf16[512,128]{1,0:T(8,128)(2,1)S(1)}, u32[]{:S(2)}, u32[]{:S(2)}) collective-permute-start(bf16[512,128]{1,0:T(8,128)(2,1)S(1)} %add_convert_fusion.1.refs_4_), channel_id=1, source_target_pairs={{0,2},{1,5},{2,0},{3,7},{4,6},{5,1},{6,4},{7,3},{8,10},{9,13},{10,... | collective-permute-start | bytes 393224 | tf_op jit(solution)/shard_map/ppermute | solution.py:263
  35.9 6.5 %collective-permute-start.10 = (bf16[512,128]{1,0:T(8,128)(2,1)S(1)}, bf16[512,128]{1,0:T(8,128)(2,1)S(1)}, u32[]{:S(2)}, u32[]{:S(2)}) collective-permute-start(bf16[512,128]{1,0:T(8,128)(2,1)S(1)} %add_convert_fusion.1.refs_4_), channel_id=1, source_target_pairs={{0,4},{1,3},{2,6},{3,1},{4,0},{5,7},{6,2},{7,5},{8,12},{9,11},{10,... | collective-permute-start | bytes 393224 | tf_op jit(solution)/shard_map/ppermute | solution.py:263
  39.0 5.9 %collective-permute-start.15 = (bf16[512,128]{1,0:T(8,128)(2,1)S(1)}, bf16[512,128]{1,0:T(8,128)(2,1)S(1)}, u32[]{:S(2)}, u32[]{:S(2)}) collective-permute-start(bf16[512,128]{1,0:T(8,128)(2,1)S(1)} %add_convert_fusion.refs_0_), channel_id=1, source_target_pairs={{0,4},{1,3},{2,6},{3,1},{4,0},{5,7},{6,2},{7,5},{8,12},{9,11},{10,... | collective-permute-start | bytes 393224 | tf_op jit(solution)/shard_map/ppermute | solution.py:263
  41.1 5.4 %collective-permute-start.8 = (bf16[512,128]{1,0:T(8,128)(2,1)S(1)}, bf16[512,128]{1,0:T(8,128)(2,1)S(1)}, u32[]{:S(2)}, u32[]{:S(2)}) collective-permute-start(bf16[512,128]{1,0:T(8,128)(2,1)S(1)} %broadcast_select_fusion.1), channel_id=1, source_target_pairs={{0,2},{1,3},{2,0},{3,1},{4,6},{5,7},{6,4},{7,5},{8,10},{9,11},{10,... | collective-permute-start | bytes 393224 | tf_op jit(solution)/shard_map/ppermute | solution.py:263
  42.3 5.5 %collective-permute-start.12 = (bf16[512,128]{1,0:T(8,128)(2,1)S(1)}, bf16[512,128]{1,0:T(8,128)(2,1)S(1)}, u32[]{:S(2)}, u32[]{:S(2)}) collective-permute-start(bf16[512,128]{1,0:T(8,128)(2,1)S(1)} %broadcast_select_fusion), channel_id=1, source_target_pairs={{0,2},{1,3},{2,0},{3,1},{4,6},{5,7},{6,4},{7,5},{8,10},{9,11},{10,... | collective-permute-start | bytes 393224 | tf_op jit(solution)/shard_map/ppermute | solution.py:263
  43.3 9.4 %collective-permute-start.16 = (bf16[512,128]{1,0:T(8,128)(2,1)S(1)}, bf16[512,128]{1,0:T(8,128)(2,1)S(1)}, u32[]{:S(2)}, u32[]{:S(2)}) collective-permute-start(bf16[512,128]{1,0:T(8,128)(2,1)S(1)} %add_convert_fusion.refs_0_), channel_id=1, source_target_pairs={{0,2},{1,5},{2,0},{3,7},{4,6},{5,1},{6,4},{7,3},{8,10},{9,13},{10,... | collective-permute-start | bytes 393224 | tf_op jit(solution)/shard_map/ppermute | solution.py:263
  44.9 7.8 %collective-permute-start.17 = (bf16[512,128]{1,0:T(8,128)(2,1)S(1)}, bf16[512,128]{1,0:T(8,128)(2,1)S(1)}, u32[]{:S(2)}, u32[]{:S(2)}) collective-permute-start(bf16[512,128]{1,0:T(8,128)(2,1)S(1)} %collective-permute-done.15.refs_1_), channel_id=1, source_target_pairs={{0,2},{1,5},{2,0},{3,7},{4,6},{5,1},{6,4},{7,3},{8,10},{9,13},{10,... | collective-permute-start | bytes 393224 | tf_op jit(solution)/shard_map/ppermute | solution.py:263
  52.5 3.4 %copy-start.2 = (bf16[128,1024]{1,0:T(8,128)(2,1)S(1)}, bf16[128,1024]{1,0:T(8,128)(2,1)}, u32[]{:S(2)}) copy-start(bf16[128,1024]{1,0:T(8,128)(2,1)} %queries.1) | copy-start | bytes 786436
  52.5 3.4 %collective-permute-start.13 = (bf16[2,512,512]{2,1,0:T(8,128)(2,1)S(1)}, bf16[2,512,512]{2,1,0:T(8,128)(2,1)S(1)}, u32[]{:S(2)}, u32[]{:S(2)}) collective-permute-start(bf16[2,512,512]{2,1,0:T(8,128)(2,1)S(1)} %shard_map.72.refs_4_.own), channel_id=1, source_target_pairs={{0,1},{1,0},{2,3},{3,2},{4,5},{5,4},{6,7},{7,6},{8,9},{9,8},{10,11... | collective-permute-start | bytes 3145736 | tf_op jit(solution)/shard_map/ppermute | solution.py:263
  55.4 2.2 %collective-permute-start.18 = (bf16[1,512,512]{2,1,0:T(8,128)(2,1)S(1)}, bf16[1,512,512]{2,1,0:T(8,128)(2,1)S(1)}, u32[]{:S(2)}, u32[]{:S(2)}) collective-permute-start(bf16[1,512,512]{2,1,0:T(8,128)(2,1)S(1)} %get-tuple-element.43.own_down), channel_id=1, source_target_pairs={{0,1},{1,0},{2,3},{3,2},{4,5},{5,4},{6,7},{7,6},{8,9},{9,8},{10,11... | collective-permute-start | bytes 1572872 | tf_op jit(solution)/shard_map/ppermute | solution.py:263

commit v7 on v6

--- a/solution.py
+++ b/solution.py
@@ -329,12 +329,17 @@
         over = move(part, second)
         return part, over, move(part, first), move(over, first)
 
+    def paired(part):
+        over = move(part, second)
+        both = move(jnp.stack([part, over]), first)
+        return part, over, both[0], both[1]
+
     pair = move(jnp.stack(send[1:]), second)
     parts = [reduced(0)] + [(keep[1 + at] + pair[at].astype(F32)).astype(BF16) for at in range(2)]
     sums = [crossed(parts[0]), crossed(parts[1])]
     sums[0], parts[2] = tie(sums[0], parts[2])
     sums.append(crossed(parts[2]))
-    four = [mixed(sums[0]), mixed(sums[1]), pieces(sums[2])]
+    four = [mixed(sums[0]), mixed(sums[1]), paired(sums[2])]
     (new_a,) = updated((0, 1), four[:2], mine)
     new_d, new_weights = updated((2,), four[2:], mine, (0, 1), new_a)
 

time: 58.7 us -> 58.7 us (level)
  waiting for transfers between devices: 16 us -> 17.1 us
  starting transfers between devices: 23.5 us -> 22.5 us
    ppermute x19 -> x18, starting transfers between devices: 23.5 us -> 22.5 us  [move(): return lax.ppermute(value, 'tok', pairs)]
    ppermute x19 -> x18, waiting for transfers between devices: 16 us -> 17.1 us  [move(): return lax.ppermute(value, 'tok', pairs)]
  transfers between devices with their start and end apart: 19 -> 18, of which waited for: 9 -> 9; matrix products, arithmetic and copies ran while one was open for 0% -> 1% of each run, Pallas kernels for 20% -> 20%
where the time goes in v7:
time: 58.7 us; the launch traced here: 58.5 us
  starting transfers between devices  22.5 us (38%)
  waiting for transfers between devices  17.1 us (29%)
  Pallas kernels  15.1 us (26%)
  local copies, waits for them, and re-layouts  2.87 us (5%)
  between operations  0.78 us (1%)
    ppermute x18, starting transfers between devices, move(): return lax.ppermute(value, 'tok', pairs)  22.5 us
    ppermute x18, waiting for transfers between devices, move(): return lax.ppermute(value, 'tok', pairs)  17.1 us
    pallas_call x2, Pallas kernels, updated(): pl.pallas_call(functools.partial(ns_kernel, which, earlier), out_shape=ou...  7.39 us
    unnamed x6, local copies, waits for them, and re-layouts  2.85 us
    pallas_call x1, Pallas kernels, body(): pl.pallas_call(pack_kernel, out_shape=(pair, pair), in_specs=[ANY_SPEC] *...  1.96 us
    pallas_call x1, Pallas kernels, body(): pl.pallas_call(gate_up_kernel, out_shape=(jax.ShapeDtypeStruct(half_reado...  1.63 us
    pallas_call x1, Pallas kernels, body(): pl.pallas_call(near_kernel, out_shape=(three32, three32, jax.ShapeDtypeSt...  1.55 us
  transfers between devices with their start and end apart: 18, of which 9 were waited for; matrix products, arithmetic and copies ran while one was open for 1% of the time, Pallas kernels for 20%

profile of v7, /device:TPU:0, one launch (start us, length us, event | category | flops | bytes accessed | tf_op | source)
XLA Modules:
  0.0 58.5 jit_solution(11296681595221557969)
XLA Ops:
  0.6 2.0 %shard_map.68 = (bf16[2,128,512]{2,1,0:T(8,128)(2,1)}, bf16[2,128,512]{2,1,0:T(8,128)(2,1)}) custom-call(bf16[128,1024]{1,0:T(8,128)(2,1)} %keys.1, bf16[128,1024]{1,0:T(8,128)(2,1)} %values.1, f32[2,128]{1,0:T(2,128)} %rates.1), custom_call_target="tpu_custom_call" | custom-call | tf_op jit(solution)/shard_map/pallas_call | solution.py:269
  2.6 0.5 collective-permute-start
  3.1 2.6 %collective-permute-start.1 = (bf16[2,128,512]{2,1,0:T(8,128)(2,1)}, bf16[2,128,512]{2,1,0:T(8,128)(2,1)S(1)}, u32[]{:S(2)}, u32[]{:S(2)}) collective-permute-start(bf16[2,128,512]{2,1,0:T(8,128)(2,1)} %get-tuple-element.26.t0), channel_id=1, source_target_pairs={{0,2},{1,5},{2,0},{3,7},{4,6},{5,1},{6,4},{7,3},{8,10},{9,13},{10,... | collective-permute-start | bytes 786440 | tf_op jit(solution)/shard_map/ppermute | solution.py:263
  5.7 0.1 collective-permute-start.2
  5.8 0.0 collective-permute-done.t1
  5.8 1.9 %copy-done = bf16[2,3,512,512]{3,2,1,0:T(8,128)(2,1)S(1)} copy-done((bf16[2,3,512,512]{3,2,1,0:T(8,128)(2,1)S(1)}, bf16[2,3,512,512]{3,2,1,0:T(8,128)(2,1)}, u32[]{:S(2)}) %copy-start) | copy-done | bytes 3145752
  7.7 0.9 %copy-done.1 = bf16[2,128,512]{2,1,0:T(8,128)(2,1)S(1)} copy-done((bf16[2,128,512]{2,1,0:T(8,128)(2,1)S(1)}, bf16[2,128,512]{2,1,0:T(8,128)(2,1)}, u32[]{:S(2)}) %copy-start.1) | copy-done | bytes 262168
  8.7 1.5 %shard_map.69 = (f32[3,512,128]{2,1,0:T(8,128)S(1)}, f32[3,512,128]{2,1,0:T(8,128)S(1)}, bf16[3,512,512]{2,1,0:T(8,128)(2,1)S(1)}) custom-call(bf16[2,128,512]{2,1,0:T(8,128)(2,1)S(1)} %copy-done.1, bf16[2,128,512]{2,1,0:T(8,128)(2,1)S(1)} %collective-permute-done.t1, bf16[2,3,512,512]{3,2,1,0:T(8,128)(2,1)S(1)} %copy-done), custom_call_target="tpu_custom_call" | custom-call | tf_op jit(solution)/shard_map/pallas_call | solution.py:285
  10.2 2.0 %collective-permute-done.1.t2 = bf16[2,128,512]{2,1,0:T(8,128)(2,1)S(1)} collective-permute-done((bf16[2,128,512]{2,1,0:T(8,128)(2,1)}, bf16[2,128,512]{2,1,0:T(8,128)(2,1)S(1)}, u32[]{:S(2)}, u32[]{:S(2)}) %collective-permute-start.1) | collective-permute-done | bytes 262176 | tf_op jit(solution)/shard_map/ppermute | solution.py:263
  12.2 0.8 %collective-permute-done.2.t3 = bf16[2,128,512]{2,1,0:T(8,128)(2,1)S(1)} collective-permute-done((bf16[2,128,512]{2,1,0:T(8,128)(2,1)}, bf16[2,128,512]{2,1,0:T(8,128)(2,1)S(1)}, u32[]{:S(2)}, u32[]{:S(2)}) %collective-permute-start.2) | collective-permute-done | bytes 262176 | tf_op jit(solution)/shard_map/ppermute | solution.py:263
  13.1 0.7 %shard_map.70 = (bf16[512,128]{1,0:T(8,128)(2,1)S(1)}, bf16[256,128]{1,0:T(8,128)(2,1)S(1)}, bf16[256,128]{1,0:T(8,128)(2,1)S(1)}, bf16[256,512]{1,0:T(8,128)(2,1)S(1)}, bf16[256,512]{1,0:T(8,128)(2,1)S(1)}) custom-call(bf16[2,128,512]{2,1,0:T(8,128)(2,1)S(1)} %collective-permute-done.1.t2, bf16[2,128,512]{2,1,0:T(8,128)(2,1)S(1)} %collective-permute-done.2.t3, ...), custom_call_target="tpu_custom_call" | custom-call | tf_op jit(solution)/shard_map/pallas_call | solution.py:295
  13.8 2.1 %collective-permute-start.3 = (bf16[512,128]{1,0:T(8,128)(2,1)S(1)}, bf16[512,128]{1,0:T(8,128)(2,1)S(1)}, u32[]{:S(2)}, u32[]{:S(2)}) collective-permute-start(bf16[512,128]{1,0:T(8,128)(2,1)S(1)} %get-tuple-element.36), channel_id=1, source_target_pairs={{0,4},{1,3},{2,6},{3,1},{4,0},{5,7},{6,2},{7,5},{8,12},{9,11},{10,... | collective-permute-start | bytes 393224 | tf_op jit(solution)/shard_map/ppermute | solution.py:263
  15.9 0.9 %shard_map.71 = (bf16[512,128]{1,0:T(8,128)(2,1)S(1)}, bf16[512,128]{1,0:T(8,128)(2,1)S(1)}, f32[512,128]{1,0:T(8,128)S(1)}, f32[512,128]{1,0:T(8,128)S(1)}, f32[512,128]{1,0:T(8,128)S(1)}) custom-call(bf16[256,512]{1,0:T(8,128)(2,1)S(1)} %get-tuple-element.30.keys, bf16[256,512]{1,0:T(8,128)(2,1)S(1)} %get-tuple-element.31.outer, ...), custom_call_target="tpu_custom_call" | custom-call | flops 13421772800 | bytes 16777216 | tf_op jit(solution)/shard_map/pallas_call | solution.py:302
  16.9 0.1 collective-permute-start.5
  17.0 1.9 %collective-permute-done.3 = bf16[512,128]{1,0:T(8,128)(2,1)S(1)} collective-permute-done((bf16[512,128]{1,0:T(8,128)(2,1)S(1)}, bf16[512,128]{1,0:T(8,128)(2,1)S(1)}, u32[]{:S(2)}, u32[]{:S(2)}) %collective-permute-start.3) | collective-permute-done | bytes 131104 | tf_op jit(solution)/shard_map/ppermute | solution.py:263
  18.9 3.1 %collective-permute-start.4 = (bf16[512,128]{1,0:T(8,128)(2,1)S(1)}, bf16[512,128]{1,0:T(8,128)(2,1)S(1)}, u32[]{:S(2)}, u32[]{:S(2)}) collective-permute-start(bf16[512,128]{1,0:T(8,128)(2,1)S(1)} %add_convert_fusion.3), channel_id=1, source_target_pairs={{0,8},{1,9},{2,10},{3,11},{4,12},{5,13},{6,14},{7,15},{8,0},{9,1},... | collective-permute-start | bytes 393224 | tf_op jit(solution)/shard_map/ppermute | solution.py:263
  22.0 4.9 %collective-permute-done.5 = bf16[2,512,128]{2,1,0:T(8,128)(2,1)S(1)} collective-permute-done((bf16[2,512,128]{2,1,0:T(8,128)(2,1)S(1)}, bf16[2,512,128]{2,1,0:T(8,128)(2,1)S(1)}, u32[]{:S(2)}, u32[]{:S(2)}) %collective-permute-start.5) | collective-permute-done | bytes 262176 | tf_op jit(solution)/shard_map/ppermute | solution.py:263
  26.9 0.1 fusion
  26.9 0.9 %collective-permute-start.9 = (bf16[512,128]{1,0:T(8,128)(2,1)S(1)}, bf16[512,128]{1,0:T(8,128)(2,1)S(1)}, u32[]{:S(2)}, u32[]{:S(2)}) collective-permute-start(bf16[512,128]{1,0:T(8,128)(2,1)S(1)} %get-tuple-element.52), channel_id=1, source_target_pairs={{0,8},{1,9},{2,10},{3,11},{4,12},{5,13},{6,14},{7,15},{8,0},{9,1},... | collective-permute-start | bytes 393224 | tf_op jit(solution)/shard_map/ppermute | solution.py:263
  27.8 0.0 collective-permute-done.4
  27.8 4.9 %collective-permute-start.7 = (bf16[512,128]{1,0:T(8,128)(2,1)S(1)}, bf16[512,128]{1,0:T(8,128)(2,1)S(1)}, u32[]{:S(2)}, u32[]{:S(2)}) collective-permute-start(bf16[512,128]{1,0:T(8,128)(2,1)S(1)} %add_convert_fusion.2.refs_0_), channel_id=1, source_target_pairs={{0,2},{1,5},{2,0},{3,7},{4,6},{5,1},{6,4},{7,3},{8,10},{9,13},{10,... | collective-permute-start | bytes 393224 | tf_op jit(solution)/shard_map/ppermute | solution.py:263
  32.8 0.0 collective-permute-start.6
  32.8 2.4 %collective-permute-start.14 = (bf16[512,128]{1,0:T(8,128)(2,1)S(1)}, bf16[512,128]{1,0:T(8,128)(2,1)S(1)}, u32[]{:S(2)}, u32[]{:S(2)}) collective-permute-start(bf16[512,128]{1,0:T(8,128)(2,1)S(1)} %get-tuple-element.42), channel_id=1, source_target_pairs={{0,8},{1,9},{2,10},{3,11},{4,12},{5,13},{6,14},{7,15},{8,0},{9,1},... | collective-permute-start | bytes 393224 | tf_op jit(solution)/shard_map/ppermute | solution.py:263
  35.2 0.0 collective-permute-done.9
  35.2 0.6 %collective-permute-start.11 = (bf16[512,128]{1,0:T(8,128)(2,1)S(1)}, bf16[512,128]{1,0:T(8,128)(2,1)S(1)}, u32[]{:S(2)}, u32[]{:S(2)}) collective-permute-start(bf16[512,128]{1,0:T(8,128)(2,1)S(1)} %add_convert_fusion.1.refs_4_), channel_id=1, source_target_pairs={{0,2},{1,5},{2,0},{3,7},{4,6},{5,1},{6,4},{7,3},{8,10},{9,13},{10,... | collective-permute-start | bytes 393224 | tf_op jit(solution)/shard_map/ppermute | solution.py:263
  35.9 0.0 collective-permute-start.10
  35.9 3.1 %collective-permute-done.14 = bf16[512,128]{1,0:T(8,128)(2,1)S(1)} collective-permute-done((bf16[512,128]{1,0:T(8,128)(2,1)S(1)}, bf16[512,128]{1,0:T(8,128)(2,1)S(1)}, u32[]{:S(2)}, u32[]{:S(2)}) %collective-permute-start.14) | collective-permute-done | bytes 131104 | tf_op jit(solution)/shard_map/ppermute | solution.py:263
  39.0 2.1 %collective-permute-start.15 = (bf16[512,128]{1,0:T(8,128)(2,1)S(1)}, bf16[512,128]{1,0:T(8,128)(2,1)S(1)}, u32[]{:S(2)}, u32[]{:S(2)}) collective-permute-start(bf16[512,128]{1,0:T(8,128)(2,1)S(1)} %add_convert_fusion.refs_0_), channel_id=1, source_target_pairs={{0,4},{1,3},{2,6},{3,1},{4,0},{5,7},{6,2},{7,5},{8,12},{9,11},{10,... | collective-permute-start | bytes 393224 | tf_op jit(solution)/shard_map/ppermute | solution.py:263
  41.0 0.0 collective-permute-done.7.refs_2_
  41.0 0.0 collective-permute-done.6.refs_1_
  41.1 0.8 %collective-permute-start.8 = (bf16[512,128]{1,0:T(8,128)(2,1)S(1)}, bf16[512,128]{1,0:T(8,128)(2,1)S(1)}, u32[]{:S(2)}, u32[]{:S(2)}) collective-permute-start(bf16[512,128]{1,0:T(8,128)(2,1)S(1)} %broadcast_select_fusion.1), channel_id=1, source_target_pairs={{0,2},{1,3},{2,0},{3,1},{4,6},{5,7},{6,4},{7,5},{8,10},{9,11},{10,... | collective-permute-start | bytes 393224 | tf_op jit(solution)/shard_map/ppermute | solution.py:263
  41.9 0.0 collective-permute-done.11.refs_6_
  41.9 0.4 collective-permute-done.10.refs_5_
  42.3 0.9 %collective-permute-start.12 = (bf16[512,128]{1,0:T(8,128)(2,1)S(1)}, bf16[512,128]{1,0:T(8,128)(2,1)S(1)}, u32[]{:S(2)}, u32[]{:S(2)}) collective-permute-start(bf16[512,128]{1,0:T(8,128)(2,1)S(1)} %broadcast_select_fusion), channel_id=1, source_target_pairs={{0,2},{1,3},{2,0},{3,1},{4,6},{5,7},{6,4},{7,5},{8,10},{9,11},{10,... | collective-permute-start | bytes 393224 | tf_op jit(solution)/shard_map/ppermute | solution.py:263
  43.3 1.5 %collective-permute-done.15.refs_1_ = bf16[512,128]{1,0:T(8,128)(2,1)S(1)} collective-permute-done((bf16[512,128]{1,0:T(8,128)(2,1)S(1)}, bf16[512,128]{1,0:T(8,128)(2,1)S(1)}, u32[]{:S(2)}, u32[]{:S(2)}) %collective-permute-start.15) | collective-permute-done | bytes 131104 | tf_op jit(solution)/shard_map/ppermute | solution.py:263
  44.8 0.6 %collective-permute-start.16 = (bf16[2,512,128]{2,1,0:T(8,128)(2,1)S(1)}, bf16[2,512,128]{2,1,0:T(8,128)(2,1)S(1)}, u32[]{:S(2)}, u32[]{:S(2)}) collective-permute-start(bf16[2,512,128]{2,1,0:T(8,128)(2,1)S(1)} %pad_maximum_fusion.1), channel_id=1, source_target_pairs={{0,2},{1,5},{2,0},{3,7},{4,6},{5,1},{6,4},{7,3},{8,10},{9,13},{10,... | collective-permute-start | bytes 786440 | tf_op jit(solution)/shard_map/ppermute | solution.py:263
  45.5 1.0 %collective-permute-done.8.refs_3_ = bf16[512,128]{1,0:T(8,128)(2,1)S(1)} collective-permute-done((bf16[512,128]{1,0:T(8,128)(2,1)S(1)}, bf16[512,128]{1,0:T(8,128)(2,1)S(1)}, u32[]{:S(2)}, u32[]{:S(2)}) %collective-permute-start.8) | collective-permute-done | bytes 131104 | tf_op jit(solution)/shard_map/ppermute | solution.py:263
  46.5 1.4 %collective-permute-done.12.refs_7_ = bf16[512,128]{1,0:T(8,128)(2,1)S(1)} collective-permute-done((bf16[512,128]{1,0:T(8,128)(2,1)S(1)}, bf16[512,128]{1,0:T(8,128)(2,1)S(1)}, u32[]{:S(2)}, u32[]{:S(2)}) %collective-permute-start.12) | collective-permute-done | bytes 131104 | tf_op jit(solution)/shard_map/ppermute | solution.py:263
  47.9 4.6 %shard_map.72.refs_4_.own = bf16[2,512,512]{2,1,0:T(8,128)(2,1)S(1)} custom-call(bf16[3,512,512]{2,1,0:T(8,128)(2,1)S(1)} %get-tuple-element.28.mine, bf16[512,128]{1,0:T(8,128)(2,1)S(1)} %add_convert_fusion.2.refs_0_, bf16[512,128]{1,0:T(8,128)(2,1)S(1)} %collective-permute-done.6.refs_1_, bf16[512,128]{1,0:T(8,128)(2,1)S(1)} %collective-permute-done.7.refs_2_, ...), custom_call_target="tpu_custom_call" | custom-call | flops 64424509440 | bytes 33554432 | tf_op jit(solution)/shard_map/pallas_call | solution.py:197
  52.5 0.1 collective-permute-start.13
  52.6 0.0 collective-permute-done.16
  52.6 0.0 copy-start.2
  52.7 2.7 %shard_map.73 = (bf16[1,512,512]{2,1,0:T(8,128)(2,1)S(1)}, bf16[2,3,512,512]{3,2,1,0:T(8,128)(2,1)}) custom-call(bf16[3,512,512]{2,1,0:T(8,128)(2,1)S(1)} %get-tuple-element.28.mine, bf16[512,128]{1,0:T(8,128)(2,1)S(1)} %add_convert_fusion.refs_0_, bf16[512,128]{1,0:T(8,128)(2,1)S(1)} %collective-permute-done.15.refs_1_, ...), custom_call_target="tpu_custom_call" | custom-call | flops 32212254720 | bytes 16777216 | tf_op jit(solution)/shard_map/pallas_call | solution.py:197
  55.4 0.6 collective-permute-start.17
  56.0 0.0 collective-permute-done.13.other
  56.0 1.6 %shard_map.74 = (bf16[128,512]{1,0:T(8,128)(2,1)S(1)}, bf16[2,3,512,512]{3,2,1,0:T(8,128)(2,1)}, bf16[128,1024]{1,0:T(8,128)(2,1)}) custom-call(bf16[128,1024]{1,0:T(8,128)(2,1)S(1)} %copy-done.2, bf16[2,512,512]{2,1,0:T(8,128)(2,1)S(1)} %shard_map.72.refs_4_.own, ...), custom_call_target="tpu_custom_call", output_to_operand_aliasing={{1}: (4, {})} | custom-call | tf_op jit(solution)/shard_map/pallas_call | solution.py:349
  57.6 0.0 collective-permute-done.17.other
  57.6 0.9 %shard_map.75 = (bf16[2,3,512,512]{3,2,1,0:T(8,128)(2,1)}, bf16[128,1024]{1,0:T(8,128)(2,1)}) custom-call(bf16[128,512]{1,0:T(8,128)(2,1)S(1)} %get-tuple-element.45.hidden, bf16[1,512,512]{2,1,0:T(8,128)(2,1)S(1)} %collective-permute-done.17.other, bf16[2,3,512,512]{3,2,1,0:T(8,128)(2,1)} %get-tuple-element.46.held, ...), custom_call_target="tpu_custom_call", output_to_operand_aliasing={{0}: (2, {}), {1}: (3, {})} | custom-call | tf_op jit(solution)/shard_map/pallas_call | solution.py:358
  (12 shorter events, 0.3 us)
Async XLA Ops:
  2.6 3.2 %collective-permute-start = (bf16[2,128,512]{2,1,0:T(8,128)(2,1)}, bf16[2,128,512]{2,1,0:T(8,128)(2,1)S(1)}, u32[]{:S(2)}, u32[]{:S(2)}) collective-permute-start(bf16[2,128,512]{2,1,0:T(8,128)(2,1)} %get-tuple-element.27), channel_id=1, source_target_pairs={{0,1},{1,0},{2,3},{3,2},{4,5},{5,4},{6,7},{7,6},{8,9},{9,8},{10,11... | collective-permute-start | bytes 786440 | tf_op jit(solution)/shard_map/ppermute | solution.py:263
  3.1 9.1 %collective-permute-start.1 = (bf16[2,128,512]{2,1,0:T(8,128)(2,1)}, bf16[2,128,512]{2,1,0:T(8,128)(2,1)S(1)}, u32[]{:S(2)}, u32[]{:S(2)}) collective-permute-start(bf16[2,128,512]{2,1,0:T(8,128)(2,1)} %get-tuple-element.26.t0), channel_id=1, source_target_pairs={{0,2},{1,5},{2,0},{3,7},{4,6},{5,1},{6,4},{7,3},{8,10},{9,13},{10,... | collective-permute-start | bytes 786440 | tf_op jit(solution)/shard_map/ppermute | solution.py:263
  5.7 7.4 %collective-permute-start.2 = (bf16[2,128,512]{2,1,0:T(8,128)(2,1)}, bf16[2,128,512]{2,1,0:T(8,128)(2,1)S(1)}, u32[]{:S(2)}, u32[]{:S(2)}) collective-permute-start(bf16[2,128,512]{2,1,0:T(8,128)(2,1)} %get-tuple-element.27), channel_id=1, source_target_pairs={{0,5},{1,2},{2,7},{3,0},{4,1},{5,6},{6,3},{7,4},{8,13},{9,10},{10,... | collective-permute-start | bytes 786440 | tf_op jit(solution)/shard_map/ppermute | solution.py:263
  5.8 1.9 %copy-start = (bf16[2,3,512,512]{3,2,1,0:T(8,128)(2,1)S(1)}, bf16[2,3,512,512]{3,2,1,0:T(8,128)(2,1)}, u32[]{:S(2)}) copy-start(bf16[2,3,512,512]{3,2,1,0:T(8,128)(2,1)} %weights.1) | copy-start | bytes 9437188
  7.7 0.9 %copy-start.1 = (bf16[2,128,512]{2,1,0:T(8,128)(2,1)S(1)}, bf16[2,128,512]{2,1,0:T(8,128)(2,1)}, u32[]{:S(2)}) copy-start(bf16[2,128,512]{2,1,0:T(8,128)(2,1)} %get-tuple-element.26.t0) | copy-start | bytes 786436
  13.8 5.1 %collective-permute-start.3 = (bf16[512,128]{1,0:T(8,128)(2,1)S(1)}, bf16[512,128]{1,0:T(8,128)(2,1)S(1)}, u32[]{:S(2)}, u32[]{:S(2)}) collective-permute-start(bf16[512,128]{1,0:T(8,128)(2,1)S(1)} %get-tuple-element.36), channel_id=1, source_target_pairs={{0,4},{1,3},{2,6},{3,1},{4,0},{5,7},{6,2},{7,5},{8,12},{9,11},{10,... | collective-permute-start | bytes 393224 | tf_op jit(solution)/shard_map/ppermute | solution.py:263
  16.9 10.0 %collective-permute-start.5 = (bf16[2,512,128]{2,1,0:T(8,128)(2,1)S(1)}, bf16[2,512,128]{2,1,0:T(8,128)(2,1)S(1)}, u32[]{:S(2)}, u32[]{:S(2)}) collective-permute-start(bf16[2,512,128]{2,1,0:T(8,128)(2,1)S(1)} %pad_maximum_fusion), channel_id=1, source_target_pairs={{0,4},{1,3},{2,6},{3,1},{4,0},{5,7},{6,2},{7,5},{8,12},{9,11},{10,... | collective-permute-start | bytes 786440 | tf_op jit(solution)/shard_map/ppermute | solution.py:263
  18.9 8.9 %collective-permute-start.4 = (bf16[512,128]{1,0:T(8,128)(2,1)S(1)}, bf16[512,128]{1,0:T(8,128)(2,1)S(1)}, u32[]{:S(2)}, u32[]{:S(2)}) collective-permute-start(bf16[512,128]{1,0:T(8,128)(2,1)S(1)} %add_convert_fusion.3), channel_id=1, source_target_pairs={{0,8},{1,9},{2,10},{3,11},{4,12},{5,13},{6,14},{7,15},{8,0},{9,1},... | collective-permute-start | bytes 393224 | tf_op jit(solution)/shard_map/ppermute | solution.py:263
  26.9 8.3 %collective-permute-start.9 = (bf16[512,128]{1,0:T(8,128)(2,1)S(1)}, bf16[512,128]{1,0:T(8,128)(2,1)S(1)}, u32[]{:S(2)}, u32[]{:S(2)}) collective-permute-start(bf16[512,128]{1,0:T(8,128)(2,1)S(1)} %get-tuple-element.52), channel_id=1, source_target_pairs={{0,8},{1,9},{2,10},{3,11},{4,12},{5,13},{6,14},{7,15},{8,0},{9,1},... | collective-permute-start | bytes 393224 | tf_op jit(solution)/shard_map/ppermute | solution.py:263
  27.8 13.2 %collective-permute-start.7 = (bf16[512,128]{1,0:T(8,128)(2,1)S(1)}, bf16[512,128]{1,0:T(8,128)(2,1)S(1)}, u32[]{:S(2)}, u32[]{:S(2)}) collective-permute-start(bf16[512,128]{1,0:T(8,128)(2,1)S(1)} %add_convert_fusion.2.refs_0_), channel_id=1, source_target_pairs={{0,2},{1,5},{2,0},{3,7},{4,6},{5,1},{6,4},{7,3},{8,10},{9,13},{10,... | collective-permute-start | bytes 393224 | tf_op jit(solution)/shard_map/ppermute | solution.py:263
  32.8 8.3 %collective-permute-start.6 = (bf16[512,128]{1,0:T(8,128)(2,1)S(1)}, bf16[512,128]{1,0:T(8,128)(2,1)S(1)}, u32[]{:S(2)}, u32[]{:S(2)}) collective-permute-start(bf16[512,128]{1,0:T(8,128)(2,1)S(1)} %add_convert_fusion.2.refs_0_), channel_id=1, source_target_pairs={{0,4},{1,3},{2,6},{3,1},{4,0},{5,7},{6,2},{7,5},{8,12},{9,11},{10,... | collective-permute-start | bytes 393224 | tf_op jit(solution)/shard_map/ppermute | solution.py:263
  32.8 6.2 %collective-permute-start.14 = (bf16[512,128]{1,0:T(8,128)(2,1)S(1)}, bf16[512,128]{1,0:T(8,128)(2,1)S(1)}, u32[]{:S(2)}, u32[]{:S(2)}) collective-permute-start(bf16[512,128]{1,0:T(8,128)(2,1)S(1)} %get-tuple-element.42), channel_id=1, source_target_pairs={{0,8},{1,9},{2,10},{3,11},{4,12},{5,13},{6,14},{7,15},{8,0},{9,1},... | collective-permute-start | bytes 393224 | tf_op jit(solution)/shard_map/ppermute | solution.py:263
  35.2 6.7 %collective-permute-start.11 = (bf16[512,128]{1,0:T(8,128)(2,1)S(1)}, bf16[512,128]{1,0:T(8,128)(2,1)S(1)}, u32[]{:S(2)}, u32[]{:S(2)}) collective-permute-start(bf16[512,128]{1,0:T(8,128)(2,1)S(1)} %add_convert_fusion.1.refs_4_), channel_id=1, source_target_pairs={{0,2},{1,5},{2,0},{3,7},{4,6},{5,1},{6,4},{7,3},{8,10},{9,13},{10,... | collective-permute-start | bytes 393224 | tf_op jit(solution)/shard_map/ppermute | solution.py:263
  35.9 6.5 %collective-permute-start.10 = (bf16[512,128]{1,0:T(8,128)(2,1)S(1)}, bf16[512,128]{1,0:T(8,128)(2,1)S(1)}, u32[]{:S(2)}, u32[]{:S(2)}) collective-permute-start(bf16[512,128]{1,0:T(8,128)(2,1)S(1)} %add_convert_fusion.1.refs_4_), channel_id=1, source_target_pairs={{0,4},{1,3},{2,6},{3,1},{4,0},{5,7},{6,2},{7,5},{8,12},{9,11},{10,... | collective-permute-start | bytes 393224 | tf_op jit(solution)/shard_map/ppermute | solution.py:263
  39.0 5.8 %collective-permute-start.15 = (bf16[512,128]{1,0:T(8,128)(2,1)S(1)}, bf16[512,128]{1,0:T(8,128)(2,1)S(1)}, u32[]{:S(2)}, u32[]{:S(2)}) collective-permute-start(bf16[512,128]{1,0:T(8,128)(2,1)S(1)} %add_convert_fusion.refs_0_), channel_id=1, source_target_pairs={{0,4},{1,3},{2,6},{3,1},{4,0},{5,7},{6,2},{7,5},{8,12},{9,11},{10,... | collective-permute-start | bytes 393224 | tf_op jit(solution)/shard_map/ppermute | solution.py:263
  41.1 5.4 %collective-permute-start.8 = (bf16[512,128]{1,0:T(8,128)(2,1)S(1)}, bf16[512,128]{1,0:T(8,128)(2,1)S(1)}, u32[]{:S(2)}, u32[]{:S(2)}) collective-permute-start(bf16[512,128]{1,0:T(8,128)(2,1)S(1)} %broadcast_select_fusion.1), channel_id=1, source_target_pairs={{0,2},{1,3},{2,0},{3,1},{4,6},{5,7},{6,4},{7,5},{8,10},{9,11},{10,... | collective-permute-start | bytes 393224 | tf_op jit(solution)/shard_map/ppermute | solution.py:263
  42.3 5.5 %collective-permute-start.12 = (bf16[512,128]{1,0:T(8,128)(2,1)S(1)}, bf16[512,128]{1,0:T(8,128)(2,1)S(1)}, u32[]{:S(2)}, u32[]{:S(2)}) collective-permute-start(bf16[512,128]{1,0:T(8,128)(2,1)S(1)} %broadcast_select_fusion), channel_id=1, source_target_pairs={{0,2},{1,3},{2,0},{3,1},{4,6},{5,7},{6,4},{7,5},{8,10},{9,11},{10,... | collective-permute-start | bytes 393224 | tf_op jit(solution)/shard_map/ppermute | solution.py:263
  44.8 7.8 %collective-permute-start.16 = (bf16[2,512,128]{2,1,0:T(8,128)(2,1)S(1)}, bf16[2,512,128]{2,1,0:T(8,128)(2,1)S(1)}, u32[]{:S(2)}, u32[]{:S(2)}) collective-permute-start(bf16[2,512,128]{2,1,0:T(8,128)(2,1)S(1)} %pad_maximum_fusion.1), channel_id=1, source_target_pairs={{0,2},{1,5},{2,0},{3,7},{4,6},{5,1},{6,4},{7,3},{8,10},{9,13},{10,... | collective-permute-start | bytes 786440 | tf_op jit(solution)/shard_map/ppermute | solution.py:263
  52.5 3.4 %collective-permute-start.13 = (bf16[2,512,512]{2,1,0:T(8,128)(2,1)S(1)}, bf16[2,512,512]{2,1,0:T(8,128)(2,1)S(1)}, u32[]{:S(2)}, u32[]{:S(2)}) collective-permute-start(bf16[2,512,512]{2,1,0:T(8,128)(2,1)S(1)} %shard_map.72.refs_4_.own), channel_id=1, source_target_pairs={{0,1},{1,0},{2,3},{3,2},{4,5},{5,4},{6,7},{7,6},{8,9},{9,8},{10,11... | collective-permute-start | bytes 3145736 | tf_op jit(solution)/shard_map/ppermute | solution.py:263
  52.6 3.3 %copy-start.2 = (bf16[128,1024]{1,0:T(8,128)(2,1)S(1)}, bf16[128,1024]{1,0:T(8,128)(2,1)}, u32[]{:S(2)}) copy-start(bf16[128,1024]{1,0:T(8,128)(2,1)} %queries.1) | copy-start | bytes 786436
  55.4 2.2 %collective-permute-start.17 = (bf16[1,512,512]{2,1,0:T(8,128)(2,1)S(1)}, bf16[1,512,512]{2,1,0:T(8,128)(2,1)S(1)}, u32[]{:S(2)}, u32[]{:S(2)}) collective-permute-start(bf16[1,512,512]{2,1,0:T(8,128)(2,1)S(1)} %get-tuple-element.43.own_down), channel_id=1, source_target_pairs={{0,1},{1,0},{2,3},{3,2},{4,5},{5,4},{6,7},{7,6},{8,9},{9,8},{10,11... | collective-permute-start | bytes 1572872 | tf_op jit(solution)/shard_map/ppermute | solution.py:263

commit v8 on v6

--- a/solution.py
+++ b/solution.py
@@ -216,11 +216,9 @@
     core, _, _ = place()
     copies = [
         pltpu.make_async_copy(other, new_weights.at[1 - core, pl.ds(0, 2)], sems.at[0]),
-        pltpu.make_async_copy(own_down, new_weights.at[core, pl.ds(2, 1)], sems.at[1]),
-        pltpu.make_async_copy(product, readout.at[:, span(core, width)], sems.at[2]),
+        pltpu.make_async_copy(product, readout.at[:, span(core, width)], sems.at[1]),
     ]
-    for copy in copies[:2]:
-        copy.start()
+    copies[0].start()
 
     def units(head, part):
         cols = span(head, width)
@@ -229,22 +227,24 @@
         return (gate * jax.nn.sigmoid(gate) * upper).astype(BF16)
 
     product[...] = dot(units(core, own), own_down[0]).astype(BF16)
-    copies[2].start()
+    copies[1].start()
     hidden[...] = units(1 - core, other)
     for copy in copies:
         copy.wait()
 
 
-def down_kernel(hidden, other, held, held_readout, new_weights, readout, product, sems):
+def down_kernel(hidden, own, other, held, held_readout, new_weights, readout, product, sems):
     width = other.shape[2]
     core, _, _ = place()
     copies = [
         pltpu.make_async_copy(other, new_weights.at[1 - core, pl.ds(2, 1)], sems.at[0]),
-        pltpu.make_async_copy(product, readout.at[:, span(1 - core, width)], sems.at[1]),
+        pltpu.make_async_copy(own, new_weights.at[core, pl.ds(2, 1)], sems.at[1]),
+        pltpu.make_async_copy(product, readout.at[:, span(1 - core, width)], sems.at[2]),
     ]
-    copies[0].start()
+    for copy in copies[:2]:
+        copy.start()
     product[...] = dot(hidden[...], other[0]).astype(BF16)
-    copies[1].start()
+    copies[2].start()
     for copy in copies:
         copy.wait()
 
@@ -346,19 +346,19 @@
         out_shape=(jax.ShapeDtypeStruct(half_readout, BF16), out_weights, out_readout),
         in_specs=[VMEM_SPEC] * 4 + [ANY_SPEC],
         out_specs=(VMEM_SPEC, ANY_SPEC, ANY_SPEC),
-        scratch_shapes=[pltpu.VMEM(half_readout, BF16), pltpu.SemaphoreType.DMA((3,))],
+        scratch_shapes=[pltpu.VMEM(half_readout, BF16), pltpu.SemaphoreType.DMA((2,))],
         input_output_aliases={4: 1},
         compiler_params=PARAMS,
     )(queries, new_a, move(new_a, sibling), new_d, new_weights)
     new_weights, readout = pl.pallas_call(
         down_kernel,
         out_shape=(out_weights, out_readout),
-        in_specs=[VMEM_SPEC] * 2 + [ANY_SPEC] * 2,
+        in_specs=[VMEM_SPEC] * 3 + [ANY_SPEC] * 2,
         out_specs=(ANY_SPEC, ANY_SPEC),
-        scratch_shapes=[pltpu.VMEM(half_readout, BF16), pltpu.SemaphoreType.DMA((2,))],
-        input_output_aliases={2: 0, 3: 1},
-        compiler_params=PARAMS,
-    )(hidden, move(new_d, sibling), new_weights, readout)
+        scratch_shapes=[pltpu.VMEM(half_readout, BF16), pltpu.SemaphoreType.DMA((3,))],
+        input_output_aliases={3: 0, 4: 1},
+        compiler_params=PARAMS,
+    )(hidden, new_d, move(new_d, sibling), new_weights, readout)
     return readout, new_weights
 
 

time: 58.7 us -> 58.8 us (level)
  transfers between devices with their start and end apart: 19 -> 19, of which waited for: 9 -> 10; matrix products, arithmetic and copies ran while one was open for 0% -> 0% of each run, Pallas kernels for 20% -> 19%
where the time goes in v8:
time: 58.8 us; the launch traced here: 58.6 us
  starting transfers between devices  23.5 us (40%)
  waiting for transfers between devices  16.4 us (28%)
  Pallas kernels  14.8 us (25%)
  local copies, waits for them, and re-layouts  2.85 us (5%)
  between operations  0.77 us (1%)
    ppermute x19, starting transfers between devices, move(): return lax.ppermute(value, 'tok', pairs)  23.5 us
    ppermute x19, waiting for transfers between devices, move(): return lax.ppermute(value, 'tok', pairs)  16.4 us
    pallas_call x2, Pallas kernels, updated(): pl.pallas_call(functools.partial(ns_kernel, which, earlier), out_shape=ou...  7.39 us
    unnamed x6, local copies, waits for them, and re-layouts  2.85 us
    pallas_call x1, Pallas kernels, body(): pl.pallas_call(pack_kernel, out_shape=(pair, pair), in_specs=[ANY_SPEC] *...  1.96 us
    pallas_call x1, Pallas kernels, body(): pl.pallas_call(near_kernel, out_shape=(three32, three32, jax.ShapeDtypeSt...  1.55 us
  transfers between devices with their start and end apart: 19, of which 10 were waited for; matrix products, arithmetic and copies ran while one was open for 0% of the time, Pallas kernels for 19%

profile of v8, /device:TPU:0, one launch (start us, length us, event | category | flops | bytes accessed | tf_op | source)
XLA Modules:
  0.0 58.6 jit_solution(6351901268572287964)
XLA Ops:
  0.6 2.0 %shard_map.68 = (bf16[2,128,512]{2,1,0:T(8,128)(2,1)}, bf16[2,128,512]{2,1,0:T(8,128)(2,1)}) custom-call(bf16[128,1024]{1,0:T(8,128)(2,1)} %keys.1, bf16[128,1024]{1,0:T(8,128)(2,1)} %values.1, f32[2,128]{1,0:T(2,128)} %rates.1), custom_call_target="tpu_custom_call" | custom-call | tf_op jit(solution)/shard_map/pallas_call | solution.py:269
  2.6 0.5 collective-permute-start
  3.1 2.6 %collective-permute-start.1 = (bf16[2,128,512]{2,1,0:T(8,128)(2,1)}, bf16[2,128,512]{2,1,0:T(8,128)(2,1)S(1)}, u32[]{:S(2)}, u32[]{:S(2)}) collective-permute-start(bf16[2,128,512]{2,1,0:T(8,128)(2,1)} %get-tuple-element.26.t0), channel_id=1, source_target_pairs={{0,2},{1,5},{2,0},{3,7},{4,6},{5,1},{6,4},{7,3},{8,10},{9,13},{10,... | collective-permute-start | bytes 786440 | tf_op jit(solution)/shard_map/ppermute | solution.py:263
  5.7 0.1 collective-permute-start.2
  5.8 0.0 collective-permute-done.t1
  5.8 1.9 %copy-done = bf16[2,3,512,512]{3,2,1,0:T(8,128)(2,1)S(1)} copy-done((bf16[2,3,512,512]{3,2,1,0:T(8,128)(2,1)S(1)}, bf16[2,3,512,512]{3,2,1,0:T(8,128)(2,1)}, u32[]{:S(2)}) %copy-start) | copy-done | bytes 3145752
  7.7 0.9 %copy-done.1 = bf16[2,128,512]{2,1,0:T(8,128)(2,1)S(1)} copy-done((bf16[2,128,512]{2,1,0:T(8,128)(2,1)S(1)}, bf16[2,128,512]{2,1,0:T(8,128)(2,1)}, u32[]{:S(2)}) %copy-start.1) | copy-done | bytes 262168
  8.7 1.5 %shard_map.69 = (f32[3,512,128]{2,1,0:T(8,128)S(1)}, f32[3,512,128]{2,1,0:T(8,128)S(1)}, bf16[3,512,512]{2,1,0:T(8,128)(2,1)S(1)}) custom-call(bf16[2,128,512]{2,1,0:T(8,128)(2,1)S(1)} %copy-done.1, bf16[2,128,512]{2,1,0:T(8,128)(2,1)S(1)} %collective-permute-done.t1, bf16[2,3,512,512]{3,2,1,0:T(8,128)(2,1)S(1)} %copy-done), custom_call_target="tpu_custom_call" | custom-call | tf_op jit(solution)/shard_map/pallas_call | solution.py:285
  10.2 2.0 %collective-permute-done.1.t2 = bf16[2,128,512]{2,1,0:T(8,128)(2,1)S(1)} collective-permute-done((bf16[2,128,512]{2,1,0:T(8,128)(2,1)}, bf16[2,128,512]{2,1,0:T(8,128)(2,1)S(1)}, u32[]{:S(2)}, u32[]{:S(2)}) %collective-permute-start.1) | collective-permute-done | bytes 262176 | tf_op jit(solution)/shard_map/ppermute | solution.py:263
  12.2 0.8 %collective-permute-done.2.t3 = bf16[2,128,512]{2,1,0:T(8,128)(2,1)S(1)} collective-permute-done((bf16[2,128,512]{2,1,0:T(8,128)(2,1)}, bf16[2,128,512]{2,1,0:T(8,128)(2,1)S(1)}, u32[]{:S(2)}, u32[]{:S(2)}) %collective-permute-start.2) | collective-permute-done | bytes 262176 | tf_op jit(solution)/shard_map/ppermute | solution.py:263
  13.1 0.7 %shard_map.70 = (bf16[512,128]{1,0:T(8,128)(2,1)S(1)}, bf16[256,128]{1,0:T(8,128)(2,1)S(1)}, bf16[256,128]{1,0:T(8,128)(2,1)S(1)}, bf16[256,512]{1,0:T(8,128)(2,1)S(1)}, bf16[256,512]{1,0:T(8,128)(2,1)S(1)}) custom-call(bf16[2,128,512]{2,1,0:T(8,128)(2,1)S(1)} %collective-permute-done.1.t2, bf16[2,128,512]{2,1,0:T(8,128)(2,1)S(1)} %collective-permute-done.2.t3, ...), custom_call_target="tpu_custom_call" | custom-call | tf_op jit(solution)/shard_map/pallas_call | solution.py:295
  13.8 2.1 %collective-permute-start.3 = (bf16[512,128]{1,0:T(8,128)(2,1)S(1)}, bf16[512,128]{1,0:T(8,128)(2,1)S(1)}, u32[]{:S(2)}, u32[]{:S(2)}) collective-permute-start(bf16[512,128]{1,0:T(8,128)(2,1)S(1)} %get-tuple-element.36), channel_id=1, source_target_pairs={{0,4},{1,3},{2,6},{3,1},{4,0},{5,7},{6,2},{7,5},{8,12},{9,11},{10,... | collective-permute-start | bytes 393224 | tf_op jit(solution)/shard_map/ppermute | solution.py:263
  15.9 0.9 %shard_map.71 = (bf16[512,128]{1,0:T(8,128)(2,1)S(1)}, bf16[512,128]{1,0:T(8,128)(2,1)S(1)}, f32[512,128]{1,0:T(8,128)S(1)}, f32[512,128]{1,0:T(8,128)S(1)}, f32[512,128]{1,0:T(8,128)S(1)}) custom-call(bf16[256,512]{1,0:T(8,128)(2,1)S(1)} %get-tuple-element.30.keys, bf16[256,512]{1,0:T(8,128)(2,1)S(1)} %get-tuple-element.31.outer, ...), custom_call_target="tpu_custom_call" | custom-call | flops 13421772800 | bytes 16777216 | tf_op jit(solution)/shard_map/pallas_call | solution.py:302
  16.9 0.1 collective-permute-start.5
  17.0 1.9 %collective-permute-done.3 = bf16[512,128]{1,0:T(8,128)(2,1)S(1)} collective-permute-done((bf16[512,128]{1,0:T(8,128)(2,1)S(1)}, bf16[512,128]{1,0:T(8,128)(2,1)S(1)}, u32[]{:S(2)}, u32[]{:S(2)}) %collective-permute-start.3) | collective-permute-done | bytes 131104 | tf_op jit(solution)/shard_map/ppermute | solution.py:263
  18.9 3.1 %collective-permute-start.4 = (bf16[512,128]{1,0:T(8,128)(2,1)S(1)}, bf16[512,128]{1,0:T(8,128)(2,1)S(1)}, u32[]{:S(2)}, u32[]{:S(2)}) collective-permute-start(bf16[512,128]{1,0:T(8,128)(2,1)S(1)} %add_convert_fusion.3), channel_id=1, source_target_pairs={{0,8},{1,9},{2,10},{3,11},{4,12},{5,13},{6,14},{7,15},{8,0},{9,1},... | collective-permute-start | bytes 393224 | tf_op jit(solution)/shard_map/ppermute | solution.py:263
  22.0 4.9 %collective-permute-done.5 = bf16[2,512,128]{2,1,0:T(8,128)(2,1)S(1)} collective-permute-done((bf16[2,512,128]{2,1,0:T(8,128)(2,1)S(1)}, bf16[2,512,128]{2,1,0:T(8,128)(2,1)S(1)}, u32[]{:S(2)}, u32[]{:S(2)}) %collective-permute-start.5) | collective-permute-done | bytes 262176 | tf_op jit(solution)/shard_map/ppermute | solution.py:263
  26.9 0.1 fusion
  26.9 0.9 %collective-permute-start.9 = (bf16[512,128]{1,0:T(8,128)(2,1)S(1)}, bf16[512,128]{1,0:T(8,128)(2,1)S(1)}, u32[]{:S(2)}, u32[]{:S(2)}) collective-permute-start(bf16[512,128]{1,0:T(8,128)(2,1)S(1)} %get-tuple-element.50), channel_id=1, source_target_pairs={{0,8},{1,9},{2,10},{3,11},{4,12},{5,13},{6,14},{7,15},{8,0},{9,1},... | collective-permute-start | bytes 393224 | tf_op jit(solution)/shard_map/ppermute | solution.py:263
  27.8 0.0 collective-permute-done.4
  27.8 4.9 %collective-permute-start.7 = (bf16[512,128]{1,0:T(8,128)(2,1)S(1)}, bf16[512,128]{1,0:T(8,128)(2,1)S(1)}, u32[]{:S(2)}, u32[]{:S(2)}) collective-permute-start(bf16[512,128]{1,0:T(8,128)(2,1)S(1)} %add_convert_fusion.2.refs_0_), channel_id=1, source_target_pairs={{0,2},{1,5},{2,0},{3,7},{4,6},{5,1},{6,4},{7,3},{8,10},{9,13},{10,... | collective-permute-start | bytes 393224 | tf_op jit(solution)/shard_map/ppermute | solution.py:263
  32.8 0.0 collective-permute-start.6
  32.8 2.4 %collective-permute-start.14 = (bf16[512,128]{1,0:T(8,128)(2,1)S(1)}, bf16[512,128]{1,0:T(8,128)(2,1)S(1)}, u32[]{:S(2)}, u32[]{:S(2)}) collective-permute-start(bf16[512,128]{1,0:T(8,128)(2,1)S(1)} %get-tuple-element.42), channel_id=1, source_target_pairs={{0,8},{1,9},{2,10},{3,11},{4,12},{5,13},{6,14},{7,15},{8,0},{9,1},... | collective-permute-start | bytes 393224 | tf_op jit(solution)/shard_map/ppermute | solution.py:263
  35.2 0.0 collective-permute-done.9
  35.2 0.6 %collective-permute-start.11 = (bf16[512,128]{1,0:T(8,128)(2,1)S(1)}, bf16[512,128]{1,0:T(8,128)(2,1)S(1)}, u32[]{:S(2)}, u32[]{:S(2)}) collective-permute-start(bf16[512,128]{1,0:T(8,128)(2,1)S(1)} %add_convert_fusion.1.refs_4_), channel_id=1, source_target_pairs={{0,2},{1,5},{2,0},{3,7},{4,6},{5,1},{6,4},{7,3},{8,10},{9,13},{10,... | collective-permute-start | bytes 393224 | tf_op jit(solution)/shard_map/ppermute | solution.py:263
  35.9 0.0 collective-permute-start.10
  35.9 3.1 %collective-permute-done.14 = bf16[512,128]{1,0:T(8,128)(2,1)S(1)} collective-permute-done((bf16[512,128]{1,0:T(8,128)(2,1)S(1)}, bf16[512,128]{1,0:T(8,128)(2,1)S(1)}, u32[]{:S(2)}, u32[]{:S(2)}) %collective-permute-start.14) | collective-permute-done | bytes 131104 | tf_op jit(solution)/shard_map/ppermute | solution.py:263
  39.0 2.1 %collective-permute-start.15 = (bf16[512,128]{1,0:T(8,128)(2,1)S(1)}, bf16[512,128]{1,0:T(8,128)(2,1)S(1)}, u32[]{:S(2)}, u32[]{:S(2)}) collective-permute-start(bf16[512,128]{1,0:T(8,128)(2,1)S(1)} %add_convert_fusion.refs_0_), channel_id=1, source_target_pairs={{0,4},{1,3},{2,6},{3,1},{4,0},{5,7},{6,2},{7,5},{8,12},{9,11},{10,... | collective-permute-start | bytes 393224 | tf_op jit(solution)/shard_map/ppermute | solution.py:263
  41.0 0.0 collective-permute-done.7.refs_2_
  41.0 0.0 collective-permute-done.6.refs_1_
  41.1 0.8 %collective-permute-start.8 = (bf16[512,128]{1,0:T(8,128)(2,1)S(1)}, bf16[512,128]{1,0:T(8,128)(2,1)S(1)}, u32[]{:S(2)}, u32[]{:S(2)}) collective-permute-start(bf16[512,128]{1,0:T(8,128)(2,1)S(1)} %broadcast_select_fusion.1), channel_id=1, source_target_pairs={{0,2},{1,3},{2,0},{3,1},{4,6},{5,7},{6,4},{7,5},{8,10},{9,11},{10,... | collective-permute-start | bytes 393224 | tf_op jit(solution)/shard_map/ppermute | solution.py:263
  41.9 0.4 collective-permute-done.10.refs_5_
  42.3 0.9 %collective-permute-start.12 = (bf16[512,128]{1,0:T(8,128)(2,1)S(1)}, bf16[512,128]{1,0:T(8,128)(2,1)S(1)}, u32[]{:S(2)}, u32[]{:S(2)}) collective-permute-start(bf16[512,128]{1,0:T(8,128)(2,1)S(1)} %broadcast_select_fusion), channel_id=1, source_target_pairs={{0,2},{1,3},{2,0},{3,1},{4,6},{5,7},{6,4},{7,5},{8,10},{9,11},{10,... | collective-permute-start | bytes 393224 | tf_op jit(solution)/shard_map/ppermute | solution.py:263
  43.3 1.2 %collective-permute-start.16 = (bf16[512,128]{1,0:T(8,128)(2,1)S(1)}, bf16[512,128]{1,0:T(8,128)(2,1)S(1)}, u32[]{:S(2)}, u32[]{:S(2)}) collective-permute-start(bf16[512,128]{1,0:T(8,128)(2,1)S(1)} %add_convert_fusion.refs_0_), channel_id=1, source_target_pairs={{0,2},{1,5},{2,0},{3,7},{4,6},{5,1},{6,4},{7,3},{8,10},{9,13},{10,... | collective-permute-start | bytes 393224 | tf_op jit(solution)/shard_map/ppermute | solution.py:263
  44.4 0.4 collective-permute-done.15.refs_1_
  44.9 0.5 collective-permute-start.17
  45.4 1.1 %collective-permute-done.8.refs_3_ = bf16[512,128]{1,0:T(8,128)(2,1)S(1)} collective-permute-done((bf16[512,128]{1,0:T(8,128)(2,1)S(1)}, bf16[512,128]{1,0:T(8,128)(2,1)S(1)}, u32[]{:S(2)}, u32[]{:S(2)}) %collective-permute-start.8) | collective-permute-done | bytes 131104 | tf_op jit(solution)/shard_map/ppermute | solution.py:263
  46.5 1.4 %collective-permute-done.12.refs_7_ = bf16[512,128]{1,0:T(8,128)(2,1)S(1)} collective-permute-done((bf16[512,128]{1,0:T(8,128)(2,1)S(1)}, bf16[512,128]{1,0:T(8,128)(2,1)S(1)}, u32[]{:S(2)}, u32[]{:S(2)}) %collective-permute-start.12) | collective-permute-done | bytes 131104 | tf_op jit(solution)/shard_map/ppermute | solution.py:263
  47.9 4.6 %shard_map.72.refs_4_.own = bf16[2,512,512]{2,1,0:T(8,128)(2,1)S(1)} custom-call(bf16[3,512,512]{2,1,0:T(8,128)(2,1)S(1)} %get-tuple-element.28.mine, bf16[512,128]{1,0:T(8,128)(2,1)S(1)} %add_convert_fusion.2.refs_0_, bf16[512,128]{1,0:T(8,128)(2,1)S(1)} %collective-permute-done.6.refs_1_, bf16[512,128]{1,0:T(8,128)(2,1)S(1)} %collective-permute-done.7.refs_2_, ...), custom_call_target="tpu_custom_call" | custom-call | flops 64424509440 | bytes 33554432 | tf_op jit(solution)/shard_map/pallas_call | solution.py:197
  52.5 0.0 copy-start.2
  52.5 0.1 collective-permute-start.13
  52.6 0.0 collective-permute-done.17.refs_3_
  52.6 2.7 %shard_map.73 = (bf16[1,512,512]{2,1,0:T(8,128)(2,1)S(1)}, bf16[2,3,512,512]{3,2,1,0:T(8,128)(2,1)}) custom-call(bf16[3,512,512]{2,1,0:T(8,128)(2,1)S(1)} %get-tuple-element.28.mine, bf16[512,128]{1,0:T(8,128)(2,1)S(1)} %add_convert_fusion.refs_0_, bf16[512,128]{1,0:T(8,128)(2,1)S(1)} %collective-permute-done.15.refs_1_, ...), custom_call_target="tpu_custom_call" | custom-call | flops 32212254720 | bytes 16777216 | tf_op jit(solution)/shard_map/pallas_call | solution.py:197
  55.4 0.5 collective-permute-start.18
  55.9 0.0 collective-permute-done.13.other
  55.9 1.2 %shard_map.74 = (bf16[128,512]{1,0:T(8,128)(2,1)S(1)}, bf16[2,3,512,512]{3,2,1,0:T(8,128)(2,1)}, bf16[128,1024]{1,0:T(8,128)(2,1)}) custom-call(bf16[128,1024]{1,0:T(8,128)(2,1)S(1)} %copy-done.2, bf16[2,512,512]{2,1,0:T(8,128)(2,1)S(1)} %shard_map.72.refs_4_.own, ...), custom_call_target="tpu_custom_call", output_to_operand_aliasing={{1}: (4, {})} | custom-call | tf_op jit(solution)/shard_map/pallas_call | solution.py:344
  57.1 0.4 collective-permute-done.18.other
  57.5 1.1 %shard_map.75 = (bf16[2,3,512,512]{3,2,1,0:T(8,128)(2,1)}, bf16[128,1024]{1,0:T(8,128)(2,1)}) custom-call(bf16[128,512]{1,0:T(8,128)(2,1)S(1)} %get-tuple-element.45.hidden, bf16[1,512,512]{2,1,0:T(8,128)(2,1)S(1)} %get-tuple-element.43.own_down.own, ...), custom_call_target="tpu_custom_call", output_to_operand_aliasing={{0}: (3, {}), {1}: (4, {})} | custom-call | tf_op jit(solution)/shard_map/pallas_call | solution.py:353
  (12 shorter events, 0.2 us)
Async XLA Ops:
  2.6 3.2 %collective-permute-start = (bf16[2,128,512]{2,1,0:T(8,128)(2,1)}, bf16[2,128,512]{2,1,0:T(8,128)(2,1)S(1)}, u32[]{:S(2)}, u32[]{:S(2)}) collective-permute-start(bf16[2,128,512]{2,1,0:T(8,128)(2,1)} %get-tuple-element.27), channel_id=1, source_target_pairs={{0,1},{1,0},{2,3},{3,2},{4,5},{5,4},{6,7},{7,6},{8,9},{9,8},{10,11... | collective-permute-start | bytes 786440 | tf_op jit(solution)/shard_map/ppermute | solution.py:263
  3.1 9.1 %collective-permute-start.1 = (bf16[2,128,512]{2,1,0:T(8,128)(2,1)}, bf16[2,128,512]{2,1,0:T(8,128)(2,1)S(1)}, u32[]{:S(2)}, u32[]{:S(2)}) collective-permute-start(bf16[2,128,512]{2,1,0:T(8,128)(2,1)} %get-tuple-element.26.t0), channel_id=1, source_target_pairs={{0,2},{1,5},{2,0},{3,7},{4,6},{5,1},{6,4},{7,3},{8,10},{9,13},{10,... | collective-permute-start | bytes 786440 | tf_op jit(solution)/shard_map/ppermute | solution.py:263
  5.7 7.4 %collective-permute-start.2 = (bf16[2,128,512]{2,1,0:T(8,128)(2,1)}, bf16[2,128,512]{2,1,0:T(8,128)(2,1)S(1)}, u32[]{:S(2)}, u32[]{:S(2)}) collective-permute-start(bf16[2,128,512]{2,1,0:T(8,128)(2,1)} %get-tuple-element.27), channel_id=1, source_target_pairs={{0,5},{1,2},{2,7},{3,0},{4,1},{5,6},{6,3},{7,4},{8,13},{9,10},{10,... | collective-permute-start | bytes 786440 | tf_op jit(solution)/shard_map/ppermute | solution.py:263
  5.8 1.9 %copy-start = (bf16[2,3,512,512]{3,2,1,0:T(8,128)(2,1)S(1)}, bf16[2,3,512,512]{3,2,1,0:T(8,128)(2,1)}, u32[]{:S(2)}) copy-start(bf16[2,3,512,512]{3,2,1,0:T(8,128)(2,1)} %weights.1) | copy-start | bytes 9437188
  7.7 0.9 %copy-start.1 = (bf16[2,128,512]{2,1,0:T(8,128)(2,1)S(1)}, bf16[2,128,512]{2,1,0:T(8,128)(2,1)}, u32[]{:S(2)}) copy-start(bf16[2,128,512]{2,1,0:T(8,128)(2,1)} %get-tuple-element.26.t0) | copy-start | bytes 786436
  13.8 5.1 %collective-permute-start.3 = (bf16[512,128]{1,0:T(8,128)(2,1)S(1)}, bf16[512,128]{1,0:T(8,128)(2,1)S(1)}, u32[]{:S(2)}, u32[]{:S(2)}) collective-permute-start(bf16[512,128]{1,0:T(8,128)(2,1)S(1)} %get-tuple-element.36), channel_id=1, source_target_pairs={{0,4},{1,3},{2,6},{3,1},{4,0},{5,7},{6,2},{7,5},{8,12},{9,11},{10,... | collective-permute-start | bytes 393224 | tf_op jit(solution)/shard_map/ppermute | solution.py:263
  16.9 10.0 %collective-permute-start.5 = (bf16[2,512,128]{2,1,0:T(8,128)(2,1)S(1)}, bf16[2,512,128]{2,1,0:T(8,128)(2,1)S(1)}, u32[]{:S(2)}, u32[]{:S(2)}) collective-permute-start(bf16[2,512,128]{2,1,0:T(8,128)(2,1)S(1)} %pad_maximum_fusion), channel_id=1, source_target_pairs={{0,4},{1,3},{2,6},{3,1},{4,0},{5,7},{6,2},{7,5},{8,12},{9,11},{10,... | collective-permute-start | bytes 786440 | tf_op jit(solution)/shard_map/ppermute | solution.py:263
  18.9 8.9 %collective-permute-start.4 = (bf16[512,128]{1,0:T(8,128)(2,1)S(1)}, bf16[512,128]{1,0:T(8,128)(2,1)S(1)}, u32[]{:S(2)}, u32[]{:S(2)}) collective-permute-start(bf16[512,128]{1,0:T(8,128)(2,1)S(1)} %add_convert_fusion.3), channel_id=1, source_target_pairs={{0,8},{1,9},{2,10},{3,11},{4,12},{5,13},{6,14},{7,15},{8,0},{9,1},... | collective-permute-start | bytes 393224 | tf_op jit(solution)/shard_map/ppermute | solution.py:263
  26.9 8.3 %collective-permute-start.9 = (bf16[512,128]{1,0:T(8,128)(2,1)S(1)}, bf16[512,128]{1,0:T(8,128)(2,1)S(1)}, u32[]{:S(2)}, u32[]{:S(2)}) collective-permute-start(bf16[512,128]{1,0:T(8,128)(2,1)S(1)} %get-tuple-element.50), channel_id=1, source_target_pairs={{0,8},{1,9},{2,10},{3,11},{4,12},{5,13},{6,14},{7,15},{8,0},{9,1},... | collective-permute-start | bytes 393224 | tf_op jit(solution)/shard_map/ppermute | solution.py:263
  27.8 13.2 %collective-permute-start.7 = (bf16[512,128]{1,0:T(8,128)(2,1)S(1)}, bf16[512,128]{1,0:T(8,128)(2,1)S(1)}, u32[]{:S(2)}, u32[]{:S(2)}) collective-permute-start(bf16[512,128]{1,0:T(8,128)(2,1)S(1)} %add_convert_fusion.2.refs_0_), channel_id=1, source_target_pairs={{0,2},{1,5},{2,0},{3,7},{4,6},{5,1},{6,4},{7,3},{8,10},{9,13},{10,... | collective-permute-start | bytes 393224 | tf_op jit(solution)/shard_map/ppermute | solution.py:263
  32.8 8.3 %collective-permute-start.6 = (bf16[512,128]{1,0:T(8,128)(2,1)S(1)}, bf16[512,128]{1,0:T(8,128)(2,1)S(1)}, u32[]{:S(2)}, u32[]{:S(2)}) collective-permute-start(bf16[512,128]{1,0:T(8,128)(2,1)S(1)} %add_convert_fusion.2.refs_0_), channel_id=1, source_target_pairs={{0,4},{1,3},{2,6},{3,1},{4,0},{5,7},{6,2},{7,5},{8,12},{9,11},{10,... | collective-permute-start | bytes 393224 | tf_op jit(solution)/shard_map/ppermute | solution.py:263
  32.8 6.2 %collective-permute-start.14 = (bf16[512,128]{1,0:T(8,128)(2,1)S(1)}, bf16[512,128]{1,0:T(8,128)(2,1)S(1)}, u32[]{:S(2)}, u32[]{:S(2)}) collective-permute-start(bf16[512,128]{1,0:T(8,128)(2,1)S(1)} %get-tuple-element.42), channel_id=1, source_target_pairs={{0,8},{1,9},{2,10},{3,11},{4,12},{5,13},{6,14},{7,15},{8,0},{9,1},... | collective-permute-start | bytes 393224 | tf_op jit(solution)/shard_map/ppermute | solution.py:263
  35.2 6.7 %collective-permute-start.11 = (bf16[512,128]{1,0:T(8,128)(2,1)S(1)}, bf16[512,128]{1,0:T(8,128)(2,1)S(1)}, u32[]{:S(2)}, u32[]{:S(2)}) collective-permute-start(bf16[512,128]{1,0:T(8,128)(2,1)S(1)} %add_convert_fusion.1.refs_4_), channel_id=1, source_target_pairs={{0,2},{1,5},{2,0},{3,7},{4,6},{5,1},{6,4},{7,3},{8,10},{9,13},{10,... | collective-permute-start | bytes 393224 | tf_op jit(solution)/shard_map/ppermute | solution.py:263
  35.9 6.5 %collective-permute-start.10 = (bf16[512,128]{1,0:T(8,128)(2,1)S(1)}, bf16[512,128]{1,0:T(8,128)(2,1)S(1)}, u32[]{:S(2)}, u32[]{:S(2)}) collective-permute-start(bf16[512,128]{1,0:T(8,128)(2,1)S(1)} %add_convert_fusion.1.refs_4_), channel_id=1, source_target_pairs={{0,4},{1,3},{2,6},{3,1},{4,0},{5,7},{6,2},{7,5},{8,12},{9,11},{10,... | collective-permute-start | bytes 393224 | tf_op jit(solution)/shard_map/ppermute | solution.py:263
  39.0 5.9 %collective-permute-start.15 = (bf16[512,128]{1,0:T(8,128)(2,1)S(1)}, bf16[512,128]{1,0:T(8,128)(2,1)S(1)}, u32[]{:S(2)}, u32[]{:S(2)}) collective-permute-start(bf16[512,128]{1,0:T(8,128)(2,1)S(1)} %add_convert_fusion.refs_0_), channel_id=1, source_target_pairs={{0,4},{1,3},{2,6},{3,1},{4,0},{5,7},{6,2},{7,5},{8,12},{9,11},{10,... | collective-permute-start | bytes 393224 | tf_op jit(solution)/shard_map/ppermute | solution.py:263
  41.1 5.4 %collective-permute-start.8 = (bf16[512,128]{1,0:T(8,128)(2,1)S(1)}, bf16[512,128]{1,0:T(8,128)(2,1)S(1)}, u32[]{:S(2)}, u32[]{:S(2)}) collective-permute-start(bf16[512,128]{1,0:T(8,128)(2,1)S(1)} %broadcast_select_fusion.1), channel_id=1, source_target_pairs={{0,2},{1,3},{2,0},{3,1},{4,6},{5,7},{6,4},{7,5},{8,10},{9,11},{10,... | collective-permute-start | bytes 393224 | tf_op jit(solution)/shard_map/ppermute | solution.py:263
  42.3 5.5 %collective-permute-start.12 = (bf16[512,128]{1,0:T(8,128)(2,1)S(1)}, bf16[512,128]{1,0:T(8,128)(2,1)S(1)}, u32[]{:S(2)}, u32[]{:S(2)}) collective-permute-start(bf16[512,128]{1,0:T(8,128)(2,1)S(1)} %broadcast_select_fusion), channel_id=1, source_target_pairs={{0,2},{1,3},{2,0},{3,1},{4,6},{5,7},{6,4},{7,5},{8,10},{9,11},{10,... | collective-permute-start | bytes 393224 | tf_op jit(solution)/shard_map/ppermute | solution.py:263
  43.3 9.4 %collective-permute-start.16 = (bf16[512,128]{1,0:T(8,128)(2,1)S(1)}, bf16[512,128]{1,0:T(8,128)(2,1)S(1)}, u32[]{:S(2)}, u32[]{:S(2)}) collective-permute-start(bf16[512,128]{1,0:T(8,128)(2,1)S(1)} %add_convert_fusion.refs_0_), channel_id=1, source_target_pairs={{0,2},{1,5},{2,0},{3,7},{4,6},{5,1},{6,4},{7,3},{8,10},{9,13},{10,... | collective-permute-start | bytes 393224 | tf_op jit(solution)/shard_map/ppermute | solution.py:263
  44.9 7.8 %collective-permute-start.17 = (bf16[512,128]{1,0:T(8,128)(2,1)S(1)}, bf16[512,128]{1,0:T(8,128)(2,1)S(1)}, u32[]{:S(2)}, u32[]{:S(2)}) collective-permute-start(bf16[512,128]{1,0:T(8,128)(2,1)S(1)} %collective-permute-done.15.refs_1_), channel_id=1, source_target_pairs={{0,2},{1,5},{2,0},{3,7},{4,6},{5,1},{6,4},{7,3},{8,10},{9,13},{10,... | collective-permute-start | bytes 393224 | tf_op jit(solution)/shard_map/ppermute | solution.py:263
  52.5 3.4 %copy-start.2 = (bf16[128,1024]{1,0:T(8,128)(2,1)S(1)}, bf16[128,1024]{1,0:T(8,128)(2,1)}, u32[]{:S(2)}) copy-start(bf16[128,1024]{1,0:T(8,128)(2,1)} %queries.1) | copy-start | bytes 786436
  52.5 3.4 %collective-permute-start.13 = (bf16[2,512,512]{2,1,0:T(8,128)(2,1)S(1)}, bf16[2,512,512]{2,1,0:T(8,128)(2,1)S(1)}, u32[]{:S(2)}, u32[]{:S(2)}) collective-permute-start(bf16[2,512,512]{2,1,0:T(8,128)(2,1)S(1)} %shard_map.72.refs_4_.own), channel_id=1, source_target_pairs={{0,1},{1,0},{2,3},{3,2},{4,5},{5,4},{6,7},{7,6},{8,9},{9,8},{10,11... | collective-permute-start | bytes 3145736 | tf_op jit(solution)/shard_map/ppermute | solution.py:263
  55.4 2.1 %collective-permute-start.18 = (bf16[1,512,512]{2,1,0:T(8,128)(2,1)S(1)}, bf16[1,512,512]{2,1,0:T(8,128)(2,1)S(1)}, u32[]{:S(2)}, u32[]{:S(2)}) collective-permute-start(bf16[1,512,512]{2,1,0:T(8,128)(2,1)S(1)} %get-tuple-element.43.own_down.own), channel_id=1, source_target_pairs={{0,1},{1,0},{2,3},{3,2},{4,5},{5,4},{6,7},{7,6},{8,9},{9,8},{10,11... | collective-permute-start | bytes 1572872 | tf_op jit(solution)/shard_map/ppermute | solution.py:263
